TPU v7x, 32 devices: a whole 2x2x4 slice. The times are simulated.
32 devices in a mesh: dp: 8 (over z, x), sp: 4 (over y, core).
Axes of the slice: x: 2, y: 2, z: 4, core: 2. Of those that a mesh axis runs over, the one named last changes fastest.
Arguments:
- tokens: bfloat16 [8, 4096, 256], P('dp', 'sp'), may hold values from -12 to 12, as said below
- ln1_gain: bfloat16 [256], replicated, may hold values from 0.25 to 1.75
- ffn1_in: bfloat16 [256, 1024], replicated, may hold values from -0.375 to 0.375
- ffn1_out: bfloat16 [1024, 256], replicated, may hold values from -0.1875 to 0.1875
- ln2_gain: bfloat16 [256], replicated, may hold values from 0.25 to 1.75
- w_qkv: bfloat16 [256, 768], replicated, may hold values from -0.375 to 0.375
- w_out: bfloat16 [256, 256], replicated, may hold values from -1.5 to 1.5
- ln3_gain: bfloat16 [256], replicated, may hold values from 0.25 to 1.75
- w_point1: bfloat16 [256, 512], replicated, may hold values from -0.375 to 0.375
- depthwise: bfloat16 [32, 256], replicated, may hold values from -1 to 1
- bn_gain: bfloat16 [256], replicated, may hold values from 0.25 to 1.75
- bn_bias: bfloat16 [256], replicated, may hold values from -3 to 3
- w_point2: bfloat16 [256, 256], replicated, may hold values from -0.375 to 0.375
- ln4_gain: bfloat16 [256], replicated, may hold values from 0.25 to 1.75
- ffn2_in: bfloat16 [256, 1024], replicated, may hold values from -0.375 to 0.375
- ffn2_out: bfloat16 [1024, 256], replicated, may hold values from -0.1875 to 0.1875
- ln5_gain: bfloat16 [256], replicated, may hold values from 0.25 to 1.75
- lengths: int32 [8, 4], P('dp'), may hold values from 128 to 3328, as said below
- cotangent: bfloat16 [8, 4096, 256], P('dp', 'sp'), may hold values from -6 to 6
Outputs:
- output: bfloat16 [8, 4096, 256], P('dp', 'sp')
- input_grad: bfloat16 [8, 4096, 256], P('dp', 'sp')
- grad_ln1_gain: float32 [256], replicated
- grad_ffn1_in: float32 [256, 1024], replicated
- grad_ffn1_out: float32 [1024, 256], replicated
- grad_ln2_gain: float32 [256], replicated
- grad_w_qkv: float32 [256, 768], replicated
- grad_w_out: float32 [256, 256], replicated
- grad_ln3_gain: float32 [256], replicated
- grad_w_point1: float32 [256, 512], replicated
- grad_depthwise: float32 [32, 256], replicated
- grad_bn_gain: float32 [256], replicated
- grad_bn_bias: float32 [256], replicated
- grad_w_point2: float32 [256, 256], replicated
- grad_ln4_gain: float32 [256], replicated
- grad_ffn2_in: float32 [256, 1024], replicated
- grad_ffn2_out: float32 [1024, 256], replicated
- grad_ln5_gain: float32 [256], replicated
Inputs may be any that keep to these rules, and one draw needn't show every extreme that they name: `lengths`: one item of each sequence, at a place drawn from the seed, has exactly (3) * 1024 + 1024 // 4 frames; the others have 1024 // 8 to 256. Frames after the last item are padding. `tokens`: frames have features of order one, with a part in common along one direction.
All inputs are finite; a program needn't handle non-finite values.
Results may differ from a plain program's by a relative error of at most 0.025.
Values may be sent and summed in bfloat16 or wider, within the bound.
A program may use at most 192 MiB of HBM per device.

v0:
```python
import jax
import jax.numpy as jnp
from jax import lax
from jax.sharding import PartitionSpec as P

HEADS = 4


EPS = 1e-05
BIG = -1e30


def with_halo(block, sides, width):
    for axis, dim in sides:
        count = lax.axis_size(axis)
        forward = [(i, i + 1) for i in range(count - 1)]
        backward = [(target, source) for source, target in forward]
        low = lax.ppermute(
            lax.slice_in_dim(block, block.shape[dim] - width, None, axis=dim), axis, forward
        )
        high = lax.ppermute(lax.slice_in_dim(block, 0, width, axis=dim), axis, backward)
        block = jnp.concatenate([low, block, high], axis=dim)
    return block


def dot_plain(left, right):
    return jnp.dot(left, right, preferred_element_type=jnp.float32)


def dot_first(left, right):
    return lax.dot_general(
        left, right, (((0,), (0,)), ((), ())), preferred_element_type=jnp.float32
    )


def dot_last(left, right):
    return lax.dot_general(
        left, right, (((1,), (1,)), ((), ())), preferred_element_type=jnp.float32
    )


def layer_norm(rows, gain):
    centre = rows - jnp.mean(rows, axis=-1, keepdims=True)
    spread = jnp.mean(centre * centre, axis=-1, keepdims=True)
    return centre * lax.rsqrt(spread + EPS) * gain


def segment_of(index, item_ends):
    return jnp.sum((index[:, None] >= item_ends[None, :]).astype(jnp.int32), axis=1)


def position_of(index, segment, starts, whole_total):
    begins = jnp.concatenate([starts, whole_total[None]])
    labels = jnp.arange(begins.shape[0], dtype=jnp.int32)
    picked = jnp.sum(jnp.where(segment[:, None] == labels[None, :], begins[None, :], 0), axis=1)
    return (index - picked).astype(jnp.float32)


def rotate(rows, position, head_dim, sign):
    count = rows.shape[0]
    split = rows.reshape(count, rows.shape[1] // head_dim, head_dim)
    half = head_dim // 2
    freq = 10000.0 ** (-(jnp.arange(half, dtype=jnp.float32) / half))
    angle = position[:, None, None] * freq[None, None, :]
    cosine = jnp.cos(angle)
    sine = jnp.sin(angle)
    first_half = split[..., :half]
    second_half = split[..., half:]
    turned = jnp.concatenate(
        [
            first_half * cosine - sign * second_half * sine,
            sign * first_half * sine + second_half * cosine,
        ],
        axis=-1,
    )
    return turned.reshape(count, rows.shape[1])


def gated_unit(joined):
    half = joined.shape[1] // 2
    return joined[:, :half] * jax.nn.sigmoid(joined[:, half:])


def feed_forward(rows, gain, w_in, w_out):
    normed, norm_back = jax.vjp(layer_norm, rows, gain)
    normed_low = normed.astype(jnp.bfloat16)
    hidden = dot_plain(normed_low, w_in)
    activated, act_back = jax.vjp(jax.nn.silu, hidden)
    act_low = activated.astype(jnp.bfloat16)
    return (rows + 0.5 * dot_plain(act_low, w_out), (norm_back, normed_low, act_low, act_back))


def feed_back(grad_rows, kept, w_in, w_out):
    norm_back, normed_low, act_low, act_back = kept
    grad_branch = (0.5 * grad_rows).astype(jnp.bfloat16)
    grad_w_out = dot_first(act_low, grad_branch)
    grad_act = dot_last(grad_branch, w_out)
    grad_hidden = act_back(grad_act)[0].astype(jnp.bfloat16)
    grad_w_in = dot_first(normed_low, grad_hidden)
    grad_normed = dot_last(grad_hidden, w_in)
    grad_input, grad_gain = norm_back(grad_normed)
    return (grad_rows + grad_input, grad_gain, grad_w_in, grad_w_out)


def masked_scores(query_block, segment_block, key_rows, segment, score_scale):
    scores = dot_last(query_block, key_rows) * score_scale
    return jnp.where(segment_block[:, None] == segment[None, :], scores, BIG)


def attend(queries, key_rows, value_rows, segment, block_rows):
    length, head_dim = queries.shape
    score_scale = head_dim ** (-0.5)
    blocks = length // block_rows

    def score_block(inputs):
        query_block, segment_block = inputs
        scores = masked_scores(query_block, segment_block, key_rows, segment, score_scale)
        row_max = jnp.max(scores, axis=1, keepdims=True)
        powers = jnp.exp(scores - row_max)
        row_sum = jnp.sum(powers, axis=1, keepdims=True)
        probs = (powers / row_sum).astype(jnp.bfloat16)
        return (dot_plain(probs, value_rows), (row_max + jnp.log(row_sum))[:, 0])

    context, log_sums = lax.map(
        score_block,
        (queries.reshape(blocks, block_rows, head_dim), segment.reshape(blocks, block_rows)),
    )
    return (context.reshape(length, head_dim), log_sums.reshape(length))


def attend_back(queries, key_rows, value_rows, segment, log_sums, grad_context, block_rows):
    length, head_dim = queries.shape
    score_scale = head_dim ** (-0.5)
    blocks = length // block_rows

    def block_step(carry, inputs):
        grad_keys, grad_values = carry
        query_block, segment_block, sum_block, grad_block = inputs
        scores = masked_scores(query_block, segment_block, key_rows, segment, score_scale)
        probs = jnp.exp(scores - sum_block[:, None])
        grad_probs = dot_last(grad_block, value_rows)
        row_dot = jnp.sum(probs * grad_probs, axis=1, keepdims=True)
        grad_scores = (probs * (grad_probs - row_dot)).astype(jnp.bfloat16)
        grad_query = dot_plain(grad_scores, key_rows) * score_scale
        grad_keys = grad_keys + dot_first(grad_scores, query_block) * score_scale
        grad_values = grad_values + dot_first(probs.astype(jnp.bfloat16), grad_block)
        return ((grad_keys, grad_values), grad_query)

    empty = jnp.zeros((length, head_dim), jnp.float32)
    (grad_keys, grad_values), grad_queries = lax.scan(
        block_step,
        (empty, empty),
        (
            queries.reshape(blocks, block_rows, head_dim),
            segment.reshape(blocks, block_rows),
            log_sums.reshape(blocks, block_rows),
            grad_context.reshape(blocks, block_rows, head_dim),
        ),
    )
    return (grad_queries.reshape(length, head_dim), grad_keys, grad_values)


def on_device(
    tokens,
    ln1_gain,
    ffn1_in,
    ffn1_out,
    ln2_gain,
    w_qkv,
    w_out,
    ln3_gain,
    w_point1,
    depthwise,
    bn_gain,
    bn_bias,
    w_point2,
    ln4_gain,
    ffn2_in,
    ffn2_out,
    ln5_gain,
    lengths,
    cotangent,
):
    frames = tokens.shape[1]
    model_width = tokens.shape[2]
    sp_count = lax.axis_size("sp")
    length = frames * sp_count
    head_dim = model_width // HEADS
    block_rows = min(512, length)
    tap_count = depthwise.shape[0]
    half_taps = tap_count // 2
    offset = lax.axis_index("sp") * frames
    item_lengths = lengths[0]
    item_count = item_lengths.shape[0]
    item_ends = jnp.cumsum(item_lengths)
    starts = item_ends - item_lengths
    whole_index = jnp.arange(length, dtype=jnp.int32)
    whole_segment = segment_of(whole_index, item_ends)
    whole_position = position_of(whole_index, whole_segment, starts, item_ends[-1])
    local_index = offset + jnp.arange(frames, dtype=jnp.int32)
    local_segment = segment_of(local_index, item_ends)
    local_position = position_of(local_index, local_segment, starts, item_ends[-1])
    rim_segment = segment_of(
        offset - half_taps + jnp.arange(frames + 2 * half_taps, dtype=jnp.int32), item_ends
    )
    valid_rows = (local_segment < item_count).astype(jnp.float32)[:, None]
    tap_masks = [
        (rim_segment[j : j + frames] == local_segment).astype(jnp.float32)[:, None]
        for j in range(2 * half_taps + 1)
    ]
    gain_one = ln1_gain.astype(jnp.float32)
    gain_two = ln2_gain.astype(jnp.float32)
    gain_three = ln3_gain.astype(jnp.float32)
    gain_four = ln4_gain.astype(jnp.float32)
    gain_five = ln5_gain.astype(jnp.float32)
    norm_gain = bn_gain.astype(jnp.float32)
    norm_bias = bn_bias.astype(jnp.float32)
    kernel = depthwise.astype(jnp.float32)
    start_rows = tokens[0].astype(jnp.float32)
    after_first, first_kept = feed_forward(start_rows, gain_one, ffn1_in, ffn1_out)
    attn_normed, attn_norm_back = jax.vjp(layer_norm, after_first, gain_two)
    attn_low = attn_normed.astype(jnp.bfloat16)
    joined = dot_plain(attn_low, w_qkv)
    queries = rotate(joined[:, :model_width], local_position, head_dim, 1.0).astype(jnp.bfloat16)
    key_rows = rotate(
        joined[:, model_width : 2 * model_width], local_position, head_dim, 1.0
    ).astype(jnp.bfloat16)
    value_rows = joined[:, 2 * model_width :].astype(jnp.bfloat16)
    head_queries, head_keys, head_values = (
        lax.all_to_all(queries, "sp", split_axis=1, concat_axis=0, tiled=True),
        lax.all_to_all(key_rows, "sp", split_axis=1, concat_axis=0, tiled=True),
        lax.all_to_all(value_rows, "sp", split_axis=1, concat_axis=0, tiled=True),
    )
    context, log_sums = attend(head_queries, head_keys, head_values, whole_segment, block_rows)
    head_context = context.astype(jnp.bfloat16)
    frame_context = lax.all_to_all(head_context, "sp", split_axis=0, concat_axis=1, tiled=True)
    after_attn = after_first + dot_plain(frame_context, w_out)
    conv_normed, conv_norm_back = jax.vjp(layer_norm, after_attn, gain_three)
    conv_low = conv_normed.astype(jnp.bfloat16)
    point_out = dot_plain(conv_low, w_point1)
    gated_rows, gated_back = jax.vjp(gated_unit, point_out)
    gated_low = gated_rows.astype(jnp.bfloat16)
    rim_gated = with_halo(gated_low, (("sp", 0),), half_taps).astype(jnp.float32)
    conv_out = jnp.zeros((frames, model_width), jnp.float32)
    for tap_index in range(tap_count):
        conv_out = (
            conv_out
            + kernel[tap_index][None, :]
            * rim_gated[tap_index : tap_index + frames]
            * tap_masks[tap_index]
        )
    first_sums, frame_count = lax.psum(
        (jnp.sum(valid_rows * conv_out, axis=0), jnp.sum(valid_rows)), ("dp", "sp")
    )
    bn_mean = first_sums / frame_count
    centered = conv_out - bn_mean
    variance = (
        lax.psum(jnp.sum(valid_rows * centered * centered, axis=0), ("dp", "sp")) / frame_count
    )
    inv_std = lax.rsqrt(variance + EPS)
    normed = centered * inv_std
    swished, swish_back = jax.vjp(jax.nn.silu, normed * norm_gain + norm_bias)
    swish_low = swished.astype(jnp.bfloat16)
    after_conv = after_attn + dot_plain(swish_low, w_point2)
    after_second, second_kept = feed_forward(after_conv, gain_four, ffn2_in, ffn2_out)
    output, final_back = jax.vjp(layer_norm, after_second, gain_five)
    grad_second, grad_gain_five = final_back(cotangent[0].astype(jnp.float32))
    grad_conv_rows, grad_gain_four, grad_in_two, grad_out_two = feed_back(
        grad_second, second_kept, ffn2_in, ffn2_out
    )
    grad_branch = grad_conv_rows.astype(jnp.bfloat16)
    grad_point_two = dot_first(swish_low, grad_branch)
    grad_swish = dot_last(grad_branch, w_point2)
    grad_norm_out = swish_back(grad_swish)[0]
    grad_norm_bias, grad_norm_gain = lax.psum(
        (jnp.sum(grad_norm_out, axis=0), jnp.sum(grad_norm_out * normed, axis=0)), ("dp", "sp")
    )
    grad_variance = -0.5 * inv_std * inv_std * norm_gain * grad_norm_gain
    grad_mean = -inv_std * norm_gain * grad_norm_bias
    grad_conv = (
        grad_norm_out * norm_gain * inv_std
        + valid_rows * (2.0 * centered * grad_variance + grad_mean) / frame_count
    )
    rim_grad = with_halo(grad_conv.astype(jnp.bfloat16), (("sp", 0),), half_taps).astype(
        grad_conv.dtype
    )
    grad_gated = jnp.zeros((frames, model_width), jnp.float32)
    for tap_index in range(tap_count):
        mirror = 2 * half_taps - tap_index
        grad_gated = (
            grad_gated
            + kernel[tap_index][None, :] * rim_grad[mirror : mirror + frames] * tap_masks[mirror]
        )
    grad_kernel = jnp.stack(
        [
            jnp.sum(grad_conv * rim_gated[j : j + frames] * tap_masks[j], axis=0)
            for j in range(tap_count)
        ]
    )
    grad_point_out = gated_back(grad_gated)[0].astype(jnp.bfloat16)
    grad_point_one = dot_first(conv_low, grad_point_out)
    grad_conv_normed = dot_last(grad_point_out, w_point1)
    grad_conv_input, grad_gain_three = conv_norm_back(grad_conv_normed)
    grad_attn_rows = grad_conv_rows + grad_conv_input
    grad_attn_out = grad_attn_rows.astype(jnp.bfloat16)
    grad_out_weight = dot_first(frame_context, grad_attn_out)
    grad_frame_context = dot_last(grad_attn_out, w_out).astype(jnp.bfloat16)
    grad_head_context = lax.all_to_all(
        grad_frame_context, "sp", split_axis=1, concat_axis=0, tiled=True
    )
    grad_query, grad_key, grad_value = attend_back(
        head_queries, head_keys, head_values, whole_segment, log_sums, grad_head_context, block_rows
    )
    query_grads = rotate(grad_query, whole_position, head_dim, -1.0)
    key_grads = rotate(grad_key, whole_position, head_dim, -1.0)
    head_grad_query = query_grads.astype(jnp.bfloat16)
    head_grad_key = key_grads.astype(jnp.bfloat16)
    head_grad_value = grad_value.astype(jnp.bfloat16)
    frame_grad_query, frame_grad_key, frame_grad_value = (
        lax.all_to_all(head_grad_query, "sp", split_axis=0, concat_axis=1, tiled=True),
        lax.all_to_all(head_grad_key, "sp", split_axis=0, concat_axis=1, tiled=True),
        lax.all_to_all(head_grad_value, "sp", split_axis=0, concat_axis=1, tiled=True),
    )
    grad_joined = jnp.concatenate([frame_grad_query, frame_grad_key, frame_grad_value], axis=1)
    grad_qkv_weight = dot_first(attn_low, grad_joined)
    grad_attn_normed = dot_last(grad_joined, w_qkv)
    grad_attn_input, grad_gain_two = attn_norm_back(grad_attn_normed)
    grad_first_rows = grad_attn_rows + grad_attn_input
    grad_start, grad_gain_one, grad_in_one, grad_out_one = feed_back(
        grad_first_rows, first_kept, ffn1_in, ffn1_out
    )
    summed = lax.psum(
        (
            grad_gain_one,
            grad_in_one,
            grad_out_one,
            grad_gain_two,
            grad_qkv_weight,
            grad_out_weight,
            grad_gain_three,
            grad_point_one,
            grad_kernel,
            grad_point_two,
            grad_gain_four,
            grad_in_two,
            grad_out_two,
            grad_gain_five,
        ),
        ("dp", "sp"),
    )
    return (
        output[None].astype(jnp.bfloat16),
        grad_start[None].astype(jnp.bfloat16),
        summed[0],
        summed[1],
        summed[2],
        summed[3],
        summed[4],
        summed[5],
        summed[6],
        summed[7],
        summed[8],
        grad_norm_gain,
        grad_norm_bias,
        summed[9],
        summed[10],
        summed[11],
        summed[12],
        summed[13],
    )


def solution(mesh):
    return jax.shard_map(
        on_device,
        mesh=mesh,
        in_specs=(
            P("dp", "sp", None),
            P(),
            P(),
            P(),
            P(),
            P(),
            P(),
            P(),
            P(),
            P(),
            P(),
            P(),
            P(),
            P(),
            P(),
            P(),
            P(),
            P("dp", None),
            P("dp", "sp", None),
        ),
        out_specs=(
            P("dp", "sp", None),
            P("dp", "sp", None),
            P(),
            P(),
            P(),
            P(),
            P(),
            P(),
            P(),
            P(),
            P(),
            P(),
            P(),
            P(),
            P(),
            P(),
            P(),
            P(),
        ),
        check_vma=False,
    )
```

profile of v0, /device:TPU:0, one launch (start us, length us, event | category | flops | bytes accessed | tf_op | source)
XLA Modules:
  0.0 845.8 jit_solution(5427411305399500891)
XLA Ops:
  38.6 6.3 all-to-all-done.1
  60.2 70.4 %while.27 = (s32[]{:T(128)}, bf16[8,512,64]{1,2,0:T(8,128)(2,1)}, f32[8,512]{1,0:T(8,128)}, s32[8,512]{1,0:T(8,128)S(1)}, s32[4096]{0:T(1024)S(1)}, /*index=5*/b...) while((s32[]{:T(128)}, bf16[8,512,64]{1,2,0:T(8,128)(2,1)}, ...), condition=%wide.region_11.12_spmd, body=%wide.region_8.11_spmd.sunk | while | flops 555744768 | bytes 27043964 | solution.py:124
  140.2 7.5 all-to-all-done.3
  159.5 9.5 %multiply_reduce_fusion.42 = (f32[256]{0:T(256)S(1)}, f32[1024,256]{1,0:T(8,128)}) fusion(f32[1024]{0:T(1024)S(1)} %get-tuple-element.452, f32[1024]{0:T(1024)S(1)} %get-tuple-element.418, f32[1056,256]{1,0:T(8,128)S(1)} %maximum_convert_fusion, f32[256]{0:T(256)} %bitcast.338, f32[1024]{0:T(1024)S(1)} %get-tuple-element.419, f32[256]{0:T(256)} %bitcast.336, ...), kind=kLoop, calls=%fused_computation.241 | loop fusion | flops 25427712 | bytes 34771968 | tf_op jit(solution)/shard_map/reduce_sum | solution.py:253
  169.1 43.1 %all-reduce.4 = (f32[256]{0:T(256)}, f32[]{:T(128)}) all-reduce(f32[256]{0:T(256)S(1)} %get-tuple-element.358, f32[]{:T(128)} %fusion.201), channel_id=1, replica_groups=mesh['dp'=8,'sp'=4] {'dp','sp'}, use_global_device_ids=true, to_apply=%region_16.17 | all-reduce | flops 257 | bytes 2056 | tf_op jit(solution)/shard_map/psum | solution.py:252
  216.0 40.6 %psum.135 = f32[256]{0:T(256)S(1)} all-reduce(f32[256]{0:T(256)} %fusion.46), channel_id=1, replica_groups=mesh['dp'=8,'sp'=4] {'dp','sp'}, use_global_device_ids=true, to_apply=%region_20.21 | all-reduce | flops 256 | bytes 2048 | tf_op jit(solution)/shard_map/psum | solution.py:258
  272.4 39.9 %all-reduce.3 = (f32[256]{0:T(256)S(1)}, f32[256]{0:T(256)S(1)}) all-reduce(f32[256]{0:T(256)S(1)} %get-tuple-element.296, f32[256]{0:T(256)S(1)} %get-tuple-element.295), channel_id=1, replica_groups=mesh['dp'=8,'sp'=4] {'dp','sp'}, use_global_device_ids=true, to_apply=%region_32.33 | all-reduce | flops 512 | bytes 4096 | tf_op jit(solution)/shard_map/psum | solution.py:275
  322.4 11.2 %collective-permute-start.3 = (bf16[16,256]{1,0:T(8,128)(2,1)S(1)}, bf16[16,256]{1,0:T(8,128)(2,1)S(1)}, u32[]{:S(2)}, u32[]{:S(2)}) collective-permute-start(bf16[16,256]{1,0:T(8,128)(2,1)S(1)} %get-tuple-element.378), channel_id=1, source_target_pairs={{1,0},{2,1},{3,2},{5,4},{6,5},{7,6},{9,8},{10,9},{11,10},{13,12},{... | collective-permute-start | bytes 24584 | tf_op jit(solution)/shard_map/ppermute | solution.py:21
  334.1 8.6 %fusion.49 = (f32[1024,256]{1,0:T(8,128)S(1)}, f32[1024,256]{1,0:T(8,128)S(1)}) fusion(f32[1024,512]{1,0:T(8,128)S(1)} %copy-done.15, f32[1024]{0:T(1024)S(1)} %copy-done.105, f32[1056,256]{1,0:T(8,128)S(1)} %maximum_convert_fusion.1, f32[256]{0:T(256)} %bitcast.339, f32[1024]{0:T(1024)S(1)} %copy-done.103, f32[256]{0:T(256)} %bitcast.337, ...), kind=kLoop, calls=%fused_computation.87 | loop fusion | flops 26738688 | bytes 37912576 | tf_op jit(solution)/shard_map/transpose(jvp())/mul | solution.py:81
  346.7 6.5 all-to-all-start.4
  353.3 8.7 %all-to-all-done.4 = bf16[1024,4,64]{0,2,1:T(8,128)(2,1)S(1)} async-done(((bf16[1024,4,64]{0,2,1:T(8,128)(2,1)}), bf16[1024,4,64]{0,2,1:T(8,128)(2,1)S(1)}, u32[]{:S(2)}, u32[]{:S(2)}) %all-to-all-start.4) | async-done | bytes 524320 | tf_op jit(solution)/shard_map/all_to_all | solution.py:308
  363.4 248.8 %while.28 = (s32[]{:T(128)}, f32[4096,64]{0,1:T(8,128)}, f32[4096,64]{0,1:T(8,128)}, f32[8,512,64]{1,0,2:T(8,128)}, s32[8,512]{1,0:T(8,128)S(1)}, /*index=5*/s32...) while((s32[]{:T(128)}, f32[4096,64]{0,1:T(8,128)}, ...), condition=%wide.region_37.38_spmd.clone, body=%wide.region_35.37_spmd.clone.sunk | while | flops 1364491776 | bytes 112361728 | solution.py:150
  372.8 7.9 multiply_convert_fusion.24
  403.6 7.9 multiply_convert_fusion.24
  434.8 7.9 multiply_convert_fusion.24
  465.9 7.9 multiply_convert_fusion.24
  490.9 6.1 multiply_reduce_fusion.46
  497.0 7.9 multiply_convert_fusion.24
  522.1 6.1 multiply_reduce_fusion.46
  528.2 7.9 multiply_convert_fusion.24
  559.3 7.9 multiply_convert_fusion.24
  590.5 7.9 multiply_convert_fusion.24
  682.6 41.0 %all-reduce.2 = (f32[256]{0:T(256)}, f32[256]{0:T(256)}, f32[256]{0:T(256)}, f32[32,256]{1,0:T(8,128)}, f32[256]{0:T(256)}, /*index=5*/f32[256]{0:T(256)}) all-reduce(f32[256]{0:T(256)S(1)} %get-tuple-element.291, f32[256]{0:T(256)S(1)} %get-tuple-element.285, f32[256]{0:T(256)S(1)} %copy-done.178, ...), channel_id=1, replica_groups=mesh['dp'=8,'sp'=4] {'dp','sp'}, use_global_device_ids=true, to_apply=%region_44.45 | all-reduce | flops 9472 | bytes 75776 | tf_op jit(solution)/shard_map/psum | solution.py:332
  723.6 105.1 %all-reduce.8.cloned.1.call-done = (f32[256,1024]{1,0:T(8,128)}, f32[1024,256]{1,0:T(8,128)}, f32[256,768]{1,0:T(8,128)}, f32[256,256]{1,0:T(8,128)}, f32[256,51...) async-done(((f32[256,1024]{1,0:T(8,128)}, f32[1024,256]{1,0:T(8,128)}, f32[256,768]{1,0:T(8,128)}, f32[256,256]{1,0:T(8,128)}, ...) | async-done | bytes 6029328 | tf_op jit(solution)/shard_map/psum | solution.py:332
  (722 shorter events, 424.5 us)
Async XLA Ops:
  7.2 252.5 %copy-start = (bf16[256,1024]{1,0:T(8,128)(2,1)S(1)}, bf16[256,1024]{1,0:T(8,128)(2,1)}, u32[]{:S(2)}) copy-start(bf16[256,1024]{1,0:T(8,128)(2,1)} %param.37) | copy-start | bytes 1572868
  16.5 131.2 %copy-start.10 = (f32[1024,256]{0,1:T(8,128)}, f32[1024,256]{0,1:T(8,128)S(1)}, u32[]{:S(2)}) copy-start(f32[1024,256]{0,1:T(8,128)S(1)} %get-tuple-element.460) | copy-start | bytes 3145732
  19.5 13.1 %all-to-all-start.2 = ((bf16[1024,4,64]{0,2,1:T(8,128)(2,1)}), bf16[1024,4,64]{0,2,1:T(8,128)(2,1)S(1)}, u32[]{:S(2)}, u32[]{:S(2)}) async-start(bf16[1024,4,64]{0,2,1:T(8,128)(2,1)} %bitcast.15), calls=%async_computation.2 | async-start | bytes 1048576 | tf_op jit(solution)/shard_map/all_to_all | solution.py:232
  32.6 12.3 %all-to-all-start.1 = ((bf16[1024,4,64]{0,2,1:T(8,128)(2,1)}), bf16[1024,4,64]{0,2,1:T(8,128)(2,1)S(1)}, u32[]{:S(2)}, u32[]{:S(2)}) async-start(bf16[1024,4,64]{0,2,1:T(8,128)(2,1)} %pad_maximum_fusion.4), calls=%async_computation.1 | async-start | bytes 1048576 | tf_op jit(solution)/shard_map/all_to_all | solution.py:231
  44.8 13.0 %all-to-all-start = ((bf16[1024,4,64]{0,2,1:T(8,128)(2,1)}), bf16[1024,4,64]{0,2,1:T(8,128)(2,1)}, u32[]{:S(2)}, u32[]{:S(2)}) async-start(bf16[1024,4,64]{0,2,1:T(8,128)(2,1)} %pad_maximum_fusion.3), calls=%async_computation | async-start | bytes 1048576 | tf_op jit(solution)/shard_map/all_to_all | solution.py:230
  49.9 283.8 %copy-start.72 = (f32[1024]{0:T(1024)}, f32[1024]{0:T(1024)S(1)}, u32[]{:S(2)}) copy-start(f32[1024]{0:T(1024)S(1)} %get-tuple-element.437) | copy-start | bytes 12292
  49.9 283.8 %copy-start.74 = (f32[1024]{0:T(1024)}, f32[1024]{0:T(1024)S(1)}, u32[]{:S(2)}) copy-start(f32[1024]{0:T(1024)S(1)} %get-tuple-element.438) | copy-start | bytes 12292
  49.9 283.8 %copy-start.76 = (f32[1024]{0:T(1024)}, f32[1024]{0:T(1024)S(1)}, u32[]{:S(2)}) copy-start(f32[1024]{0:T(1024)S(1)} %get-tuple-element.439) | copy-start | bytes 12292
  49.9 283.8 %copy-start.78 = (f32[1024]{0:T(1024)}, f32[1024]{0:T(1024)S(1)}, u32[]{:S(2)}) copy-start(f32[1024]{0:T(1024)S(1)} %get-tuple-element.440) | copy-start | bytes 12292
  49.9 283.8 %copy-start.80 = (f32[1024]{0:T(1024)}, f32[1024]{0:T(1024)S(1)}, u32[]{:S(2)}) copy-start(f32[1024]{0:T(1024)S(1)} %get-tuple-element.441) | copy-start | bytes 12292
  49.9 283.8 %copy-start.82 = (f32[1024]{0:T(1024)}, f32[1024]{0:T(1024)S(1)}, u32[]{:S(2)}) copy-start(f32[1024]{0:T(1024)S(1)} %get-tuple-element.442) | copy-start | bytes 12292
  135.2 12.5 %all-to-all-start.3 = ((bf16[4,1024,64]{1,2,0:T(8,128)(2,1)}), bf16[4,1024,64]{1,2,0:T(8,128)(2,1)S(1)}, u32[]{:S(2)}, u32[]{:S(2)}) async-start(bf16[4,1024,64]{1,2,0:T(8,128)(2,1)} %copy.91), calls=%async_computation.3 | async-start | bytes 1048576 | tf_op jit(solution)/shard_map/all_to_all | solution.py:236
  152.3 5.4 collective-permute-start
  153.8 4.5 collective-permute-start.1
  155.7 112.1 %copy-start.70 = (f32[256]{0:T(256)}, f32[256]{0:T(256)S(1)}, u32[]{:S(2)}) copy-start(f32[256]{0:T(256)S(1)} %convert_element_type.323) | copy-start | bytes 3076
  159.5 158.7 %copy-start.2 = (f32[1056,256]{1,0:T(8,128)}, f32[1056,256]{1,0:T(8,128)S(1)}, u32[]{:S(2)}) copy-start(f32[1056,256]{1,0:T(8,128)S(1)} %maximum_convert_fusion) | copy-start | bytes 3244036
  321.1 12.5 %collective-permute-start.2 = (bf16[16,256]{1,0:T(8,128)(2,1)S(1)}, bf16[16,256]{1,0:T(8,128)(2,1)S(1)}, u32[]{:S(2)}, u32[]{:S(2)}) collective-permute-start(bf16[16,256]{1,0:T(8,128)(2,1)S(1)} %get-tuple-element.377), channel_id=1, source_target_pairs={{0,1},{1,2},{2,3},{4,5},{5,6},{6,7},{8,9},{9,10},{10,11},{12,13},{... | collective-permute-start | bytes 24584 | tf_op jit(solution)/shard_map/ppermute | solution.py:18
  322.4 11.2 %collective-permute-start.3 = (bf16[16,256]{1,0:T(8,128)(2,1)S(1)}, bf16[16,256]{1,0:T(8,128)(2,1)S(1)}, u32[]{:S(2)}, u32[]{:S(2)}) collective-permute-start(bf16[16,256]{1,0:T(8,128)(2,1)S(1)} %get-tuple-element.378), channel_id=1, source_target_pairs={{1,0},{2,1},{3,2},{5,4},{6,5},{7,6},{9,8},{10,9},{11,10},{13,12},{... | collective-permute-start | bytes 24584 | tf_op jit(solution)/shard_map/ppermute | solution.py:21
  346.7 15.4 %all-to-all-start.4 = ((bf16[1024,4,64]{0,2,1:T(8,128)(2,1)}), bf16[1024,4,64]{0,2,1:T(8,128)(2,1)S(1)}, u32[]{:S(2)}, u32[]{:S(2)}) async-start(bf16[1024,4,64]{0,2,1:T(8,128)(2,1)} %bitcast.54), calls=%async_computation.4 | async-start | bytes 1048576 | tf_op jit(solution)/shard_map/all_to_all | solution.py:308
  363.4 250.2 %copy-start.184 = (f32[32]{0:T(128)S(1)}, f32[32]{0:T(128)}, u32[]{:S(2)}) copy-start(f32[32]{0:T(128)} %copy-done.183) | copy-start | bytes 388
  619.0 13.1 %all-to-all-start.5 = ((bf16[4,1024,64]{1,2,0:T(8,128)(2,1)}), bf16[4,1024,64]{1,2,0:T(8,128)(2,1)}, u32[]{:S(2)}, u32[]{:S(2)}) async-start(bf16[4,1024,64]{1,2,0:T(8,128)(2,1)} %copy.95), calls=%async_computation.5 | async-start | bytes 1048576 | tf_op jit(solution)/shard_map/all_to_all | solution.py:320
  632.1 13.3 %all-to-all-start.6 = ((bf16[4,1024,64]{1,2,0:T(8,128)(2,1)}), bf16[4,1024,64]{1,2,0:T(8,128)(2,1)}, u32[]{:S(2)}, u32[]{:S(2)}) async-start(bf16[4,1024,64]{1,2,0:T(8,128)(2,1)} %copy.96), calls=%async_computation.6 | async-start | bytes 1048576 | tf_op jit(solution)/shard_map/all_to_all | solution.py:321
  645.4 12.3 %all-to-all-start.7 = ((bf16[4,1024,64]{1,2,0:T(8,128)(2,1)}), bf16[4,1024,64]{1,2,0:T(8,128)(2,1)S(1)}, u32[]{:S(2)}, u32[]{:S(2)}) async-start(bf16[4,1024,64]{1,2,0:T(8,128)(2,1)} %bitcast.223), calls=%async_computation.7 | async-start | bytes 1048576 | tf_op jit(solution)/shard_map/all_to_all | solution.py:322
  648.8 179.8 %all-reduce.8.cloned.1.call-start = ((), (), s32[]{:S(2)}) async-start(), calls=%async_computation.8 | async-start | bytes 12058624 | tf_op jit(solution)/shard_map/psum | solution.py:332
  (211 other events, 1650.3 us)
Sparse Core Ops, SparseCore 0:
  672.5 156.1 all-reduce.7
where the time goes:
time: 858 us; the launch traced here: 846 us
  matrix products  235 us (27%)
  blocking collectives  165 us (19%)
  waiting for transfers between devices  144 us (17%)
  other arithmetic  132 us (15%)
  local copies, waits for them, and re-layouts  103 us (12%)
  starting transfers between devices  49.4 us (6%)
  between operations  17.2 us (2%)
    psum x1, waiting for transfers between devices, on_device(): lax.psum((grad_gain_one, grad_in_one, grad_out_one, grad_gain_two, grad_q...  105 us
    dot_general x32, matrix products, dot_last(): lax.dot_general(left, right, (((1,), (1,)), ((), ())), preferred_element_...  102 us
    dot_general x24, matrix products, dot_first(): lax.dot_general(left, right, (((0,), (0,)), ((), ())), preferred_element_...  79.4 us
    convert_element_type x8, other arithmetic, block_step(): grad_scores = (probs * (grad_probs - row_dot)).astype(jnp.bfloat16)  63.4 us
    dot_general x24, matrix products, dot_plain(): return jnp.dot(left, right, preferred_element_type=jnp.float32)  53.6 us
    psum x1, blocking collectives, on_device(): lax.psum((jnp.sum(valid_rows * conv_out, axis=0), jnp.sum(valid_rows)), (...  43.1 us
    dynamic_update_slice x24, local copies, waits for them, and re-layouts, attend(): lax.map(score_block, (queries.reshape(blocks, block_rows, head_dim), segm...  41.8 us
    psum x1, blocking collectives, on_device(): lax.psum((grad_gain_one, grad_in_one, grad_out_one, grad_gain_two, grad_q...  41 us
  transfers between devices with their start and end apart: 13, of which 9 were waited for; matrix products, arithmetic and copies ran while one was open for 5% of the time, Pallas kernels for 0%

commit v1 on v0

v1 whole, which is shorter than its diff:
```python
import functools

import jax
import jax.numpy as jnp
import numpy as np
from jax import lax
from jax.experimental import pallas as pl
from jax.experimental.pallas import tpu as pltpu
from jax.sharding import PartitionSpec as P

HEADS = 4
EPS = 1e-05
NEG = -1e30
LN2 = float(np.log(2.0))
F32 = jnp.float32
BF16 = jnp.bfloat16
I32 = jnp.int32
MESH = pl.DeviceIdType.MESH
VMEM = pl.BlockSpec(memory_space=pltpu.VMEM)
SMEM = pl.BlockSpec(memory_space=pltpu.SMEM)
DMA = pltpu.SemaphoreType.DMA
VMEM_LIMIT = 56 * 2**20


def dg(left, right, left_dim, right_dim):
    return lax.dot_general(
        left, right, (((left_dim,), (right_dim,)), ((), ())), preferred_element_type=F32
    )


def rows_at(index, count):
    return pl.ds(pl.multiple_of(index * count, count), count)


def greet(devices):
    barrier = pltpu.get_barrier_semaphore()
    for device in devices:
        pl.semaphore_signal(barrier, inc=1, device_id=device, device_id_type=MESH)
    pl.semaphore_wait(barrier, len(devices))


def sp_peers(count):
    dp, sp = lax.axis_index("dp"), lax.axis_index("sp")
    return [(dp, lax.rem(sp + step, count)) for step in range(1, count)]


def ends_of(len_ref, items):
    ends, total = [], 0
    for item in range(items):
        total = total + len_ref[0, item]
        ends.append(total)
    return ends


def segment_row(first, count, ends):
    frame = first + lax.broadcasted_iota(I32, (1, count), 1)
    segment = jnp.zeros((1, count), I32)
    for end in ends:
        segment = segment + (frame >= end).astype(I32)
    return segment


def position_row(first, count, ends):
    frame = first + lax.broadcasted_iota(I32, (1, count), 1)
    start = jnp.zeros((1, count), I32)
    for end in ends:
        start = jnp.where(frame >= end, end, start)
    return (frame - start).astype(F32)


def block_bounds(first, count, ends, length):
    low, high = 0, length
    for end in ends:
        low = jnp.where(first >= end, end, low)
    for end in reversed(ends):
        high = jnp.where(first + count - 1 < end, end, high)
    return low, high


def onehot_rows(segment, items, other, same):
    row = lax.broadcasted_iota(I32, (16, segment.shape[1]), 0)
    return jnp.where(row <= items, jnp.where(row == segment, same, other), 0.0)


def norm_parts(rows):
    centre = rows - jnp.mean(rows, axis=-1, keepdims=True)
    inv = lax.rsqrt(jnp.mean(centre * centre, axis=-1, keepdims=True) + EPS)
    return centre * inv, inv


def norm_back(grad, hat, inv, gain):
    scaled = grad * gain
    first = jnp.mean(scaled, axis=-1, keepdims=True)
    second = jnp.mean(scaled * hat, axis=-1, keepdims=True)
    return inv * (scaled - first - hat * second)


def sigmoid(x):
    return 1.0 / (1.0 + jnp.exp(-x))


def sine_cosine(position, freq_hi, freq_lo):
    turns = position * freq_hi
    turns = turns - jnp.round(turns) + position * freq_lo
    turns = turns - jnp.round(turns)
    x = turns * float(np.pi)
    x2 = x * x
    s = x * (1 + x2 * (-1 / 6 + x2 * (1 / 120 + x2 * (-1 / 5040 + x2 * (1 / 362880 - x2 / 39916800)))))
    c = 1 + x2 * (-1 / 2 + x2 * (1 / 24 + x2 * (-1 / 720 + x2 * (1 / 40320 + x2 * (-1 / 3628800 + x2 / 479001600)))))
    return 2 * s * c, 1 - 2 * s * s


def front_kernel(
    sp, items, chunk, len_ref, tok, gain1, w_in, w_out, gain2, w_qkv, freq,
    x1_ref, n2_ref, trig, heads, parts, send, recv, local,
):
    me = lax.axis_index("sp")
    frames = tok.shape[0]
    width = heads.shape[1]
    half = trig.shape[0] // 2
    peers = sp_peers(sp)
    greet(peers)
    ends = ends_of(len_ref, items)
    scale = float(np.log2(np.e)) * (2 * half) ** -0.5

    def copies(c):
        cols = rows_at(c, chunk)
        out = [
            pltpu.make_async_remote_copy(
                src_ref=parts.at[peer[1], :, cols],
                dst_ref=heads.at[me, :, cols],
                send_sem=send.at[i, c],
                recv_sem=recv.at[i, c],
                device_id=peer,
                device_id_type=MESH,
            )
            for i, peer in enumerate(peers)
        ]
        own = pltpu.make_async_copy(parts.at[me, :, cols], heads.at[me, :, cols], local.at[c])
        return out, own

    def step(c, carry):
        rows = rows_at(c, chunk)
        x = tok[rows, :].astype(F32)
        hat, _ = norm_parts(x)
        n1 = (hat * gain1[...].astype(F32)).astype(BF16)
        a = dg(n1, w_in[...], 1, 0)
        s = (a * sigmoid(a)).astype(BF16)
        x1 = x + 0.5 * dg(s, w_out[...], 1, 0)
        x1_ref[rows, :] = x1
        hat, _ = norm_parts(x1)
        n2 = (hat * gain2[...].astype(F32)).astype(BF16)
        n2_ref[rows, :] = n2
        joined = dg(w_qkv[...], n2, 1, 1)
        sine, cosine = sine_cosine(
            position_row(me * frames + c * chunk, chunk, ends), freq[:, 0:1], freq[:, 1:2]
        )
        trig[0:half, rows] = sine
        trig[half:, rows] = cosine
        for head in range(sp):
            base = head * width
            for part, factor in ((0, scale), (1, 1.0)):
                low = base + part * 2 * half
                first, second = joined[low : low + half], joined[low + half : low + 2 * half]
                parts[head, part * 2 * half : part * 2 * half + half, rows] = (
                    (first * cosine - second * sine) * factor
                ).astype(BF16)
                parts[head, part * 2 * half + half : (part + 1) * 2 * half, rows] = (
                    (first * sine + second * cosine) * factor
                ).astype(BF16)
            parts[head, 4 * half : 6 * half, rows] = joined[base + 4 * half : base + 6 * half].astype(BF16)
        out, own = copies(c)
        for copy in out:
            copy.start()
        own.start()
        return carry

    lax.fori_loop(0, frames // chunk, step, 0)

    def finish(c, carry):
        out, own = copies(c)
        for copy in out:
            copy.wait()
        own.wait()
        return carry

    lax.fori_loop(0, frames // chunk, finish, 0)


def front(lengths, tok, gain1, w_in, w_out, gain2, w_qkv, freq, sp):
    frames, width = tok.shape
    chunk = min(256, frames)
    count = frames // chunk
    head_width = w_qkv.shape[0] // sp
    half = freq.shape[0]
    return pl.pallas_call(
        functools.partial(front_kernel, sp, lengths.shape[1], chunk),
        out_shape=[
            jax.ShapeDtypeStruct((frames, width), F32),
            jax.ShapeDtypeStruct((frames, width), BF16),
            jax.ShapeDtypeStruct((2 * half, frames), F32),
            jax.ShapeDtypeStruct((sp, head_width, frames), BF16),
        ],
        in_specs=[SMEM] + [VMEM] * 7,
        out_specs=[VMEM] * 4,
        scratch_shapes=[
            pltpu.VMEM((sp, head_width, frames), BF16),
            DMA((sp - 1, count)),
            DMA((sp - 1, count)),
            DMA((count,)),
        ],
        compiler_params=pltpu.CompilerParams(
            collective_id=0, has_side_effects=True, vmem_limit_bytes=VMEM_LIMIT
        ),
        name="front",
    )(lengths, tok, gain1, w_in, w_out, gain2, w_qkv, freq)


def fwd_kernel(items,bq,bk,nsub,len_ref,x_ref,ctx_ref,o_ref,lse_ref,qa,ka,va):
    srcs,rows,fr=x_ref.shape; hd=rows//3; L=srcs*fr
    ends=ends_of(len_ref,items)
    for s in range(srcs):
        cols=pl.ds(s*fr,fr)
        seg=segment_row(s*fr,fr,ends)
        qa[0:hd,cols]=x_ref[s,0:hd,:]
        qa[hd:hd+16,cols]=onehot_rows(seg,items,0.0,1.0).astype(BF16)
        qa[hd+16:2*hd,cols]=jnp.zeros((hd-16,fr),BF16)
        kT=jnp.concatenate([x_ref[s,hd:2*hd,:],onehot_rows(seg,items,NEG,0.0).astype(BF16),jnp.zeros((hd-16,fr),BF16)],axis=0)
        ka[cols,:]=kT.T
        va[0:hd,cols]=x_ref[s,2*hd:3*hd,:]
        one=lax.broadcasted_iota(I32,(16,fr),0)==0
        va[hd:hd+16,cols]=jnp.where(one,1.0,0.0).astype(BF16)
    per=fr//bq
    def qbody(i,c):
        q0=i*bq
        q=qa[:,pl.ds(pl.multiple_of(q0,bq),bq)]
        lo,hi=block_bounds(q0,bq,ends,L)
        def kbody(j,car):
            m,acc=car
            w=bk//nsub
            ks=[pl.ds(pl.multiple_of(j*bk+u*w,w),w) for u in range(nsub)]
            ss=[dg(ka[k,:],q,1,0) for k in ks]
            mn=m
            for s in ss: mn=jnp.maximum(mn,jnp.max(s,axis=0,keepdims=True))
            acc=acc*jnp.exp2(m-mn)
            for s,k in zip(ss,ks):
                p=jnp.exp2(s-mn).astype(BF16)
                acc=acc+dg(va[:,k],p,1,0)
            return mn,acc
        m,acc=lax.fori_loop(lo//bk,(hi+bk-1)//bk,kbody,(jnp.full((1,bq),NEG,F32),jnp.zeros((hd+16,bq),F32)))
        l=acc[hd:hd+1,:]
        o=acc[0:hd,:]/l
        d=i//per; qc=pl.ds(pl.multiple_of((i%per)*bq,bq),bq)
        ctx_ref[d,:,qc]=o.astype(BF16)
        o_ref[d,:,qc]=o
        lse_ref[:,pl.ds(pl.multiple_of(q0,bq),bq)]=m+jnp.log2(l)
        return c
    lax.fori_loop(0,L//bq,qbody,0)
def attend(x,lengths,bq=1024,bk=1024,nsub=4):
    srcs,rows,fr=x.shape; hd=rows//3; L=srcs*fr
    return pl.pallas_call(functools.partial(fwd_kernel,lengths.shape[1],min(bq,fr),min(bk,fr),nsub),
      out_shape=[jax.ShapeDtypeStruct((srcs,hd,fr),BF16),jax.ShapeDtypeStruct((srcs,hd,fr),F32),jax.ShapeDtypeStruct((1,L),F32)],
      in_specs=[SMEM,VMEM],out_specs=[VMEM]*3,
      scratch_shapes=[pltpu.VMEM((2*hd,L),BF16),pltpu.VMEM((L,2*hd),BF16),pltpu.VMEM((hd+16,L),BF16)],
      compiler_params=pltpu.CompilerParams(vmem_limit_bytes=VMEM_LIMIT),name="attend")(lengths,x)

def split3(v):
    a=v.astype(BF16); r=v-a.astype(F32); b=r.astype(BF16); c=(r-b.astype(F32)).astype(BF16)
    return a,b,c
def bwd_kernel(items,bq,bk,len_ref,x_ref,o_ref,lse_ref,do_ref,g_ref,qa,ka,da,va,dq,dk,dv):
    srcs,rows,fr=x_ref.shape; hd=rows//3; L=srcs*fr
    ends=ends_of(len_ref,items)
    row16=lax.broadcasted_iota(I32,(16,fr),0)
    pad=jnp.zeros((hd-32,fr),BF16)
    def stack3(v):
        a,b,c=[u.astype(F32) for u in split3(v)]
        return jnp.where(row16==0,a,jnp.where(row16==1,b,jnp.where(row16==2,c,0.0))).astype(BF16)
    ones3=jnp.where(row16<3,1.0,0.0).astype(BF16)
    for s in range(srcs):
        cols=pl.ds(s*fr,fr)
        seg=segment_row(s*fr,fr,ends)
        qT=jnp.concatenate([x_ref[s,0:hd,:],onehot_rows(seg,items,0.0,1.0).astype(BF16),stack3(-lse_ref[:,cols]),pad],axis=0)
        qa[cols,:]=qT.T
        ka[0:hd,cols]=x_ref[s,hd:2*hd,:]
        ka[hd:hd+16,cols]=onehot_rows(seg,items,NEG,0.0).astype(BF16)
        ka[hd+16:hd+32,cols]=ones3
        ka[hd+32:2*hd,cols]=pad
        do=do_ref[s]
        D=jnp.sum(do.astype(F32)*o_ref[s],axis=0,keepdims=True)
        dT=jnp.concatenate([do,stack3(-D),pad,jnp.zeros((16,fr),BF16)],axis=0)
        da[cols,:]=dT.T
        va[0:hd,cols]=x_ref[s,2*hd:3*hd,:]
        va[hd:hd+16,cols]=ones3
        va[hd+16:2*hd,cols]=jnp.zeros((hd-16,fr),BF16)
    dq[...]=jnp.zeros_like(dq)
    per=fr//bk; perq=fr//bq
    def kbody(j,c):
        k0=j*bk
        ks=pl.ds(pl.multiple_of(k0,bk),bk)
        lo,hi=block_bounds(k0,bk,ends,L)
        d=j//per; kc=pl.ds(pl.multiple_of((j%per)*bk,bk),bk)
        dk[...]=jnp.zeros_like(dk); dv[...]=jnp.zeros_like(dv)
        def qbody(i,car):
            qs=pl.ds(pl.multiple_of(i*bq,bq),bq)
            e=i//perq; qc=pl.ds(pl.multiple_of((i%perq)*bq,bq),bq)
            p=jnp.exp2(dg(qa[qs,:],ka[:,ks],1,0))
            dp=dg(da[qs,:],va[:,ks],1,0)
            ds=(p*dp).astype(BF16)
            pb=p.astype(BF16)
            dv[...]+=dg(do_ref[e,:,qc],pb,1,0)
            dk[...]+=dg(x_ref[e,0:hd,qc],ds,1,0)
            dq[:,qs]+=dg(ka[0:hd,ks],ds,1,1)
            return car
        lax.fori_loop(lo//bq,(hi+bq-1)//bq,qbody,0)
        g_ref[d,hd:2*hd,kc]=(dk[...]*float(np.log(2.0))).astype(BF16)
        g_ref[d,2*hd:3*hd,kc]=dv[...].astype(BF16)
        return c
    lax.fori_loop(0,L//bk,kbody,0)
    for s in range(srcs):
        g_ref[s,0:hd,:]=(dq[:,pl.ds(s*fr,fr)]*(hd**-0.5)).astype(BF16)
def attend_back(x,lengths,o,lse,do,bq=1024,bk=1024):
    srcs,rows,fr=x.shape; hd=rows//3; L=srcs*fr
    bq=min(bq,fr); bk=min(bk,fr)
    return pl.pallas_call(functools.partial(bwd_kernel,lengths.shape[1],bq,bk),
      out_shape=jax.ShapeDtypeStruct(x.shape,BF16),
      in_specs=[SMEM]+[VMEM]*4,out_specs=VMEM,
      scratch_shapes=[pltpu.VMEM((L,2*hd),BF16),pltpu.VMEM((2*hd,L),BF16),pltpu.VMEM((L,2*hd),BF16),pltpu.VMEM((2*hd,L),BF16),
        pltpu.VMEM((hd,L),F32),pltpu.VMEM((hd,bk),F32),pltpu.VMEM((hd,bk),F32)],
      compiler_params=pltpu.CompilerParams(vmem_limit_bytes=VMEM_LIMIT),name="attend_back")(lengths,x,o,lse,do)


def exchange_kernel(sp, parts, heads, send, recv, local):
    me = lax.axis_index("sp")
    peers = sp_peers(sp)
    greet(peers)
    copies = [
        pltpu.make_async_remote_copy(
            src_ref=parts.at[peer[1]],
            dst_ref=heads.at[me],
            send_sem=send.at[i],
            recv_sem=recv.at[i],
            device_id=peer,
            device_id_type=MESH,
        )
        for i, peer in enumerate(peers)
    ]
    for copy in copies:
        copy.start()
    own = pltpu.make_async_copy(parts.at[me], heads.at[me], local)
    own.start()
    own.wait()
    for copy in copies:
        copy.wait()


def exchange(parts, call):
    sp = parts.shape[0]
    anywhere = pl.BlockSpec(memory_space=pl.ANY)
    return pl.pallas_call(
        functools.partial(exchange_kernel, sp),
        out_shape=jax.ShapeDtypeStruct(parts.shape, parts.dtype),
        in_specs=[anywhere],
        out_specs=anywhere,
        scratch_shapes=[DMA((sp - 1,)), DMA((sp - 1,)), DMA],
        compiler_params=pltpu.CompilerParams(collective_id=call, has_side_effects=True),
        name="exchange",
    )(parts)


def gather_kernel(sp, dp, x_ref, all_ref, send, recv):
    me_d, me_s = lax.axis_index("dp"), lax.axis_index("sp")
    total = sp * dp
    me = me_d * sp + me_s
    peers = []
    for step in range(1, total):
        peer = lax.rem(me + step, total)
        peers.append((peer // sp, lax.rem(peer, sp)))
    greet(peers)
    copies = [
        pltpu.make_async_remote_copy(
            src_ref=x_ref,
            dst_ref=all_ref.at[i + 1],
            send_sem=send.at[i],
            recv_sem=recv.at[i],
            device_id=peer,
            device_id_type=MESH,
        )
        for i, peer in enumerate(peers)
    ]
    for copy in copies:
        copy.start()
    all_ref[0] = x_ref[...]
    for copy in copies:
        copy.wait()


def gather_all(x, sp, dp, call):
    total = sp * dp
    return pl.pallas_call(
        functools.partial(gather_kernel, sp, dp),
        out_shape=jax.ShapeDtypeStruct((total,) + x.shape, x.dtype),
        in_specs=[VMEM],
        out_specs=VMEM,
        scratch_shapes=[DMA((total - 1,)), DMA((total - 1,))],
        compiler_params=pltpu.CompilerParams(collective_id=call, has_side_effects=True),
        name="gather_all",
    )(x)


def with_halo(block, width):
    count = lax.axis_size("sp")
    forward = [(i, i + 1) for i in range(count - 1)]
    backward = [(target, source) for source, target in forward]
    low = lax.ppermute(block[-width:], "sp", forward)
    high = lax.ppermute(block[:width], "sp", backward)
    return jnp.concatenate([low, block, high], axis=0)


def layer_norm(rows, gain):
    centre = rows - jnp.mean(rows, axis=-1, keepdims=True)
    spread = jnp.mean(centre * centre, axis=-1, keepdims=True)
    return centre * lax.rsqrt(spread + EPS) * gain


def segment_of(index, item_ends):
    return jnp.sum((index[:, None] >= item_ends[None, :]).astype(jnp.int32), axis=1)


def gated_unit(joined):
    half = joined.shape[1] // 2
    return joined[:, :half] * jax.nn.sigmoid(joined[:, half:])


def feed_forward(rows, gain, w_in, w_out):
    normed, back = jax.vjp(layer_norm, rows, gain)
    normed_low = normed.astype(BF16)
    hidden = dg(normed_low, w_in, 1, 0)
    activated, act_back = jax.vjp(jax.nn.silu, hidden)
    act_low = activated.astype(BF16)
    return rows + 0.5 * dg(act_low, w_out, 1, 0), (back, normed_low, act_low, act_back)


def feed_back(grad_rows, kept, w_in, w_out):
    back, normed_low, act_low, act_back = kept
    grad_branch = (0.5 * grad_rows).astype(BF16)
    grad_w_out = dg(act_low, grad_branch, 0, 0)
    grad_act = dg(grad_branch, w_out, 1, 1)
    grad_hidden = act_back(grad_act)[0].astype(BF16)
    grad_w_in = dg(normed_low, grad_hidden, 0, 0)
    grad_normed = dg(grad_hidden, w_in, 1, 1)
    grad_input, grad_gain = back(grad_normed)
    return grad_rows + grad_input, grad_gain, grad_w_in, grad_w_out


def on_device(
    tokens, ln1_gain, ffn1_in, ffn1_out, ln2_gain, w_qkv, w_out, ln3_gain, w_point1, depthwise,
    bn_gain, bn_bias, w_point2, ln4_gain, ffn2_in, ffn2_out, ln5_gain, lengths, cotangent,
):
    frames, width = tokens.shape[1:]
    sp, dp = lax.axis_size("sp"), lax.axis_size("dp")
    assert HEADS == sp
    head_dim = width // HEADS
    half = head_dim // 2
    items = lengths.shape[1]
    taps = depthwise.shape[0]
    reach = taps // 2
    offset = lax.axis_index("sp") * frames
    item_ends = jnp.cumsum(lengths[0])
    local_segment = segment_of(offset + jnp.arange(frames, dtype=I32), item_ends)
    rim_segment = segment_of(offset - reach + jnp.arange(frames + 2 * reach, dtype=I32), item_ends)
    valid_rows = (local_segment < items).astype(F32)[:, None]
    tap_masks = [
        (rim_segment[j : j + frames] == local_segment).astype(F32)[:, None] for j in range(taps + 1)
    ]
    gain_one, gain_two, gain_three, gain_four, gain_five = (
        g.astype(F32) for g in (ln1_gain, ln2_gain, ln3_gain, ln4_gain, ln5_gain)
    )
    norm_gain, norm_bias, kernel = (g.astype(F32) for g in (bn_gain, bn_bias, depthwise))
    turns = 10000.0 ** (-np.arange(half, dtype=np.float64) / half) / (2 * np.pi)
    high = np.round(turns * 4096.0) / 4096.0
    freq = jnp.asarray(np.stack([high, turns - high], axis=1), F32)
    qkv_rows = w_qkv.T.reshape(3, HEADS, head_dim, width).transpose(1, 0, 2, 3).reshape(3 * width, width)

    after_first, attn_low, trig, heads = front(
        lengths, tokens[0], ln1_gain[None], ffn1_in, ffn1_out, ln2_gain[None], qkv_rows, freq, sp
    )
    context, raw_context, log_sums = attend(heads, lengths)
    context = exchange(context, 1).reshape(width, frames)
    after_attn = after_first + dg(context, w_out, 0, 0)
    conv_normed, conv_norm_back = jax.vjp(layer_norm, after_attn, gain_three)
    conv_low = conv_normed.astype(BF16)
    point_out = dg(conv_low, w_point1, 1, 0)
    gated_rows, gated_back = jax.vjp(gated_unit, point_out)
    rim_gated = with_halo(gated_rows.astype(BF16), reach).astype(F32)
    conv_out = jnp.zeros((frames, width), F32)
    for tap in range(taps):
        conv_out = conv_out + kernel[tap][None, :] * rim_gated[tap : tap + frames] * tap_masks[tap]
    own_count = jnp.sum(valid_rows)
    own_mean = jnp.sum(valid_rows * conv_out, axis=0) / jnp.maximum(own_count, 1.0)
    own_spread = jnp.sum(valid_rows * (conv_out - own_mean) ** 2, axis=0)
    rows = jnp.stack([own_mean, own_spread, jnp.broadcast_to(own_count, (width,))])
    every = gather_all(jnp.concatenate([rows, jnp.zeros((5, width), F32)]), sp, dp, 2)
    counts = every[:, 2]
    frame_count = jnp.sum(counts, axis=0)
    bn_mean = jnp.sum(counts * every[:, 0], axis=0) / frame_count
    variance = (
        jnp.sum(every[:, 1], axis=0) + jnp.sum(counts * (every[:, 0] - bn_mean) ** 2, axis=0)
    ) / frame_count
    centered = conv_out - bn_mean
    inv_std = lax.rsqrt(variance + EPS)
    normed = centered * inv_std
    swished, swish_back = jax.vjp(jax.nn.silu, normed * norm_gain + norm_bias)
    swish_low = swished.astype(BF16)
    after_conv = after_attn + dg(swish_low, w_point2, 1, 0)
    after_second, second_kept = feed_forward(after_conv, gain_four, ffn2_in, ffn2_out)
    output, final_back = jax.vjp(layer_norm, after_second, gain_five)
    grad_second, grad_gain_five = final_back(cotangent[0].astype(F32))
    grad_conv_rows, grad_gain_four, grad_in_two, grad_out_two = feed_back(
        grad_second, second_kept, ffn2_in, ffn2_out
    )
    grad_branch = grad_conv_rows.astype(BF16)
    grad_point_two = dg(swish_low, grad_branch, 0, 0)
    grad_norm_out = swish_back(dg(grad_branch, w_point2, 1, 1))[0]
    sums = jnp.stack([jnp.sum(grad_norm_out, axis=0), jnp.sum(grad_norm_out * normed, axis=0)])
    every = gather_all(jnp.concatenate([sums, jnp.zeros((6, width), F32)]), sp, dp, 3)
    grad_norm_bias, grad_norm_gain = jnp.sum(every[:, 0], axis=0), jnp.sum(every[:, 1], axis=0)
    grad_variance = -0.5 * inv_std * inv_std * norm_gain * grad_norm_gain
    grad_mean = -inv_std * norm_gain * grad_norm_bias
    grad_conv = (
        grad_norm_out * norm_gain * inv_std
        + valid_rows * (2.0 * centered * grad_variance + grad_mean) / frame_count
    )
    rim_grad = with_halo(grad_conv.astype(BF16), reach).astype(F32)
    grad_gated = jnp.zeros((frames, width), F32)
    for tap in range(taps):
        mirror = 2 * reach - tap
        grad_gated = (
            grad_gated + kernel[tap][None, :] * rim_grad[mirror : mirror + frames] * tap_masks[mirror]
        )
    grad_kernel = jnp.stack(
        [jnp.sum(grad_conv * rim_gated[j : j + frames] * tap_masks[j], axis=0) for j in range(taps)]
    )
    grad_point_out = gated_back(grad_gated)[0].astype(BF16)
    grad_point_one = dg(conv_low, grad_point_out, 0, 0)
    grad_conv_input, grad_gain_three = conv_norm_back(dg(grad_point_out, w_point1, 1, 1))
    grad_attn_rows = grad_conv_rows + grad_conv_input
    grad_attn_out = grad_attn_rows.astype(BF16)
    grad_out_weight = dg(context, grad_attn_out, 1, 0)
    grad_context = dg(w_out, grad_attn_out, 1, 1).astype(BF16).reshape(sp, head_dim, frames)
    grad_heads = attend_back(heads, lengths, raw_context, log_sums, exchange(grad_context, 4))
    grad_parts = exchange(grad_heads, 5).reshape(HEADS, 3, 2, half, frames).astype(F32)
    sine, cosine = trig[:half], trig[half:]
    first, second = grad_parts[:, :2, 0], grad_parts[:, :2, 1]
    turned = jnp.stack([first * cosine + second * sine, second * cosine - first * sine], axis=2)
    grad_joined = jnp.concatenate([turned, grad_parts[:, 2:]], axis=1).astype(BF16)
    grad_joined = grad_joined.reshape(3 * width, frames)
    grad_qkv = dg(grad_joined, attn_low, 1, 0).reshape(HEADS, 3, head_dim, width)
    grad_qkv = grad_qkv.transpose(1, 0, 2, 3).reshape(3 * width, width).T
    _, attn_norm_back = jax.vjp(layer_norm, after_first, gain_two)
    grad_attn_input, grad_gain_two = attn_norm_back(dg(grad_joined, qkv_rows, 0, 0))
    _, first_kept = feed_forward(tokens[0].astype(F32), gain_one, ffn1_in, ffn1_out)
    grad_start, grad_gain_one, grad_in_one, grad_out_one = feed_back(
        grad_attn_rows + grad_attn_input, first_kept, ffn1_in, ffn1_out
    )
    summed = lax.psum(
        (
            grad_gain_one, grad_in_one, grad_out_one, grad_gain_two, grad_qkv, grad_out_weight,
            grad_gain_three, grad_point_one, grad_kernel, grad_norm_gain, grad_norm_bias,
            grad_point_two, grad_gain_four, grad_in_two, grad_out_two, grad_gain_five,
        )[:9] + (
            grad_point_two, grad_gain_four, grad_in_two, grad_out_two, grad_gain_five,
        ),
        ("dp", "sp"),
    )
    return (
        (output[None].astype(BF16), grad_start[None].astype(BF16))
        + summed[:9] + (grad_norm_gain, grad_norm_bias) + summed[9:]
    )


def solution(mesh):
    split = P("dp", "sp", None)
    return jax.shard_map(
        on_device,
        mesh=mesh,
        in_specs=(split,) + (P(),) * 16 + (P("dp", None), split),
        out_specs=(split, split) + (P(),) * 16,
        check_vma=False,
    )
```

time: 858 us -> 465 us (0.54)
  matrix products: 235 us -> 36.2 us
  Pallas kernels: 0 us -> 165 us
  blocking collectives: 165 us -> 43.1 us
  other arithmetic: 132 us -> 50.7 us
  local copies, waits for them, and re-layouts: 103 us -> 31.5 us
  starting transfers between devices: 49.4 us -> 7.78 us
  waiting for transfers between devices: 144 us -> 109 us
    dot_general x80 -> x22, matrix products: 235 us -> 36.2 us  [dg(): lax.dot_general(left, right, (((left_dim,), (right_dim,)), ((), ())), pre...]
    pallas_call x0 -> x8, Pallas kernels: none -> 165 us  [the longest x1 45.9 us: attend_back(): pl.pallas_call(functools.partial(bwd_kernel, lengths.shape[1], bq, bk), o...]
    psum x3 -> x0, blocking collectives: 124 us -> none  [the longest x1 43.1 us: on_device(): lax.psum((jnp.sum(valid_rows * conv_out, axis=0), jnp.sum(valid_rows)), (...]
    convert_element_type x25 -> x15, other arithmetic: 70.1 us -> 9.95 us  [the longest x7 3.44 us: on_device(): g.astype(F32)]
    dynamic_update_slice x24 -> x0, local copies, waits for them, and re-layouts: 41.8 us -> none  [attend(): lax.map(score_block, (queries.reshape(blocks, block_rows, head_dim), segm...]
    all_to_all x8 -> x0, waiting for transfers between devices: 38.8 us -> none  [the longest x1 8.71 us: on_device(): lax.all_to_all(grad_frame_context, 'sp', split_axis=1, concat_axis=0, til...]
    all_to_all x8 -> x0, starting transfers between devices: 34.1 us -> none  [the longest x1 6.53 us: on_device(): lax.all_to_all(grad_frame_context, 'sp', split_axis=1, concat_axis=0, til...]
    reduce_sum x13 -> x7, other arithmetic: 22.6 us -> 11.7 us  [the longest x1 8.46 us: on_device(): jnp.sum(valid_rows * conv_out, axis=0) / jnp.maximum(own_count, 1.0)]
  transfers between devices with their start and end apart: 13 -> 5, of which waited for: 9 -> 2; matrix products, arithmetic and copies ran while one was open for 5% -> 6% of each run, Pallas kernels for 0% -> 0%
where the time goes in v1:
time: 465 us; the launch traced here: 460 us
  Pallas kernels  165 us (35%)
  waiting for transfers between devices  109 us (23%)
  other arithmetic  50.7 us (11%)
  blocking collectives  43.1 us (9%)
  matrix products  36.2 us (8%)
  local copies, waits for them, and re-layouts  31.5 us (7%)
  between operations  17.2 us (4%)
  starting transfers between devices  7.78 us (2%)
    psum x1, waiting for transfers between devices, on_device(): lax.psum((grad_gain_one, grad_in_one, grad_out_one, grad_gain_two, grad_q...  108 us
    pallas_call x1, Pallas kernels, attend_back(): pl.pallas_call(functools.partial(bwd_kernel, lengths.shape[1], bq, bk), o...  45.9 us
    psum x1, blocking collectives, on_device(): lax.psum((grad_gain_one, grad_in_one, grad_out_one, grad_gain_two, grad_q...  43.1 us
    pallas_call x3, Pallas kernels, exchange(): pl.pallas_call(functools.partial(exchange_kernel, sp), out_shape=jax.Shap...  37.8 us
    dot_general x22, matrix products, dg(): lax.dot_general(left, right, (((left_dim,), (right_dim,)), ((), ())), pre...  36.2 us
    pallas_call x1, Pallas kernels, attend(): pl.pallas_call(functools.partial(fwd_kernel, lengths.shape[1], min(bq, fr...  29.5 us
    pallas_call x2, Pallas kernels, gather_all(): pl.pallas_call(functools.partial(gather_kernel, sp, dp), out_shape=jax.Sh...  26.4 us
    pallas_call x1, Pallas kernels, front(): pl.pallas_call(functools.partial(front_kernel, sp, lengths.shape[1], chun...  25.2 us
  transfers between devices with their start and end apart: 5, of which 2 were waited for; matrix products, arithmetic and copies ran while one was open for 6% of the time, Pallas kernels for 0%

profile of v1, /device:TPU:0, one launch (start us, length us, event | category | flops | bytes accessed | tf_op | source)
XLA Modules:
  0.0 460.2 jit_solution(5223585058662087979)
XLA Ops:
  11.7 25.2 %front.1 = (f32[1024,256]{1,0:T(8,128)}, bf16[1024,256]{1,0:T(8,128)(2,1)}, f32[64,1024]{1,0:T(8,128)}, bf16[4,192,1024]{2,1,0:T(8,128)(2,1)}) custom-call(s32[1,4]{1,0:T(1,128)} %len_ref.5, bf16[1024,256]{1,0:T(8,128)(2,1)} %bitcast.159, bf16[1,256]{1,0:T(2,128)(2,1)} %broadcast_in_dim.28.gain1, bf16[256,1024]{1,0:T(8,128)(2,1)} %w_in.1, ...), custom_call_target="tpu_custom_call" | custom-call | tf_op jit(solution)/shard_map/front/pallas_call | solution.py:196
  36.9 29.5 %attend.1 = (bf16[4,64,1024]{2,1,0:T(8,128)(2,1)}, f32[4,64,1024]{2,1,0:T(8,128)}, f32[1,4096]{1,0:T(1,128)}) custom-call(s32[1,4]{1,0:T(1,128)} %len_ref.5, bf16[4,192,1024]{2,1,0:T(8,128)(2,1)} %get-tuple-element.26.x_ref), custom_call_target="tpu_custom_call" | custom-call | tf_op jit(solution)/shard_map/attend/pallas_call | solution.py:261
  66.4 8.4 %exchange.3 = bf16[4,64,1024]{2,1,0:T(8,128)(2,1)} custom-call(bf16[4,64,1024]{2,1,0:T(8,128)(2,1)} %get-tuple-element.27.parts), custom_call_target="tpu_custom_call" | custom-call | tf_op jit(solution)/shard_map/exchange/pallas_call | solution.py:359
  80.4 3.1 collective-permute-start
  92.3 3.8 fusion.159
  102.8 8.5 %multiply_reduce_fusion.43 = (f32[256]{0:T(256)S(1)}, f32[1024,256]{1,0:T(8,128)S(1)}) fusion(f32[1024]{0:T(1024)S(1)} %get-tuple-element.220, f32[1024]{0:T(1024)S(1)} %get-tuple-element.188, f32[1056,256]{1,0:T(8,128)S(1)} %maximum_convert_fusion.1, f32[256]{0:T(256)} %bitcast.233, f32[1024]{0:T(1024)S(1)} %get-tuple-element.189, f32[256]{0:T(256)} %bitcast.231, ...), kind=kLoop, calls=%fused_computation.205 | loop fusion | flops 25427712 | bytes 34771968 | tf_op jit(solution)/shard_map/reduce_sum | solution.py:499
  113.1 13.1 %gather_all.2 = f32[32,8,256]{2,1,0:T(8,128)} custom-call(f32[8,256]{1,0:T(8,128)} %maximum_maximum_fusion.x_ref), custom_call_target="tpu_custom_call" | custom-call | tf_op jit(solution)/shard_map/gather_all/pallas_call | solution.py:399
  137.2 2.4 fusion.2
  139.5 2.0 fusion.162
  147.4 13.3 %gather_all.3 = f32[32,8,256]{2,1,0:T(8,128)} custom-call(f32[8,256]{1,0:T(8,128)} %maximum_maximum_fusion.1.x_ref), custom_call_target="tpu_custom_call" | custom-call | tf_op jit(solution)/shard_map/gather_all/pallas_call | solution.py:399
  162.5 4.4 multiply_reduce_fusion.1
  167.0 2.5 multiply_reduce_fusion.10
  173.1 2.1 fusion.97
  176.8 7.7 %fusion.24 = (f32[1024,256]{1,0:T(8,128)S(1)}, f32[1024,256]{1,0:T(8,128)S(1)}) fusion(f32[1024,512]{1,0:T(8,128)S(1)} %copy-done.4, f32[1024]{0:T(1024)S(1)} %copy-done.49, f32[1056,256]{1,0:T(8,128)S(1)} %maximum_convert_fusion.2, f32[256]{0:T(256)S(1)} %bitcast.234, f32[1024]{0:T(1024)S(1)} %copy-done.47, f32[256]{0:T(256)S(1)} %bitcast.232, ...), kind=kLoop, calls=%fused_computation.48 | loop fusion | flops 26738688 | bytes 37912576 | tf_op jit(solution)/shard_map/transpose(jvp())/mul | solution.py:431
  190.3 9.6 %exchange.4.do_ref = bf16[4,64,1024]{2,1,0:T(8,128)(2,1)} custom-call(bf16[4,64,1024]{2,1,0:T(8,128)(2,1)} %bitcast.167), custom_call_target="tpu_custom_call" | custom-call | tf_op jit(solution)/shard_map/exchange/pallas_call | solution.py:359
  200.0 45.9 %attend_back.1.parts = bf16[4,192,1024]{2,1,0:T(8,128)(2,1)} custom-call(s32[1,4]{1,0:T(1,128)} %len_ref.5, bf16[4,192,1024]{2,1,0:T(8,128)(2,1)} %get-tuple-element.26.x_ref, f32[4,64,1024]{2,1,0:T(8,128)} %get-tuple-element.28.o_ref, f32[1,4096]{1,0:T(1,128)} %get-tuple-element.29.lse_ref, bf16[4,64,1024]{2,1,0:T(8,128)(2,1)} %exchange.4.do_ref), custom_call_target="tpu_custom_call" | custom-call | tf_op jit(solution)/shard_map/attend_back/pallas_call | solution.py:324
  245.9 19.7 %exchange.5 = bf16[4,192,1024]{2,1,0:T(8,128)(2,1)} custom-call(bf16[4,192,1024]{2,1,0:T(8,128)(2,1)} %attend_back.1.parts), custom_call_target="tpu_custom_call" | custom-call | tf_op jit(solution)/shard_map/exchange/pallas_call | solution.py:359
  275.9 2.3 fusion.6
  279.2 2.0 fusion.157
  287.3 2.5 fusion.20
  290.5 43.1 %all-reduce.2 = (f32[256]{0:T(256)}, f32[256]{0:T(256)}, f32[256]{0:T(256)}, f32[32,256]{1,0:T(8,128)}, f32[256]{0:T(256)}, /*index=5*/f32[256]{0:T(256)}) all-reduce(f32[256]{0:T(256)S(1)} %get-tuple-element.106, f32[256]{0:T(256)S(1)} %get-tuple-element.104, ...), channel_id=1, replica_groups=mesh['dp'=8,'sp'=4] {'dp','sp'}, use_global_device_ids=true, to_apply=%region_35.36 | all-reduce | flops 9472 | bytes 75776 | tf_op jit(solution)/shard_map/psum | solution.py:565
  335.2 107.8 %all-reduce.6.cloned.1.call-done = (f32[256,1024]{1,0:T(8,128)}, f32[1024,256]{1,0:T(8,128)}, f32[256,768]{0,1:T(8,128)}, f32[256,256]{1,0:T(8,128)}, f32[256,51...) async-done(((f32[256,1024]{1,0:T(8,128)}, f32[1024,256]{1,0:T(8,128)}, f32[256,768]{0,1:T(8,128)}, f32[256,256]{1,0:T(8,128)}, ...) | async-done | bytes 6029328 | tf_op jit(solution)/shard_map/psum | solution.py:565
  443.0 2.4 copy.82
  445.4 2.4 copy.109
  (397 shorter events, 79.3 us)
Async XLA Ops:
  7.2 123.1 %copy-start = (bf16[256,1024]{1,0:T(8,128)(2,1)S(1)}, bf16[256,1024]{1,0:T(8,128)(2,1)}, u32[]{:S(2)}) copy-start(bf16[256,1024]{1,0:T(8,128)(2,1)} %param.34) | copy-start | bytes 1572868
  7.2 435.8 %all-reduce.6.cloned.1.call-start = ((), (), s32[]{:S(2)}) async-start(), calls=%async_computation | async-start | bytes 12058624 | tf_op jit(solution)/shard_map/psum | solution.py:565
  11.7 63.1 %copy-start.35 = (bf16[256,256]{1,0:T(8,128)(2,1)S(1)}, bf16[256,256]{1,0:T(8,128)(2,1)}, u32[]{:S(2)}) copy-start(bf16[256,256]{1,0:T(8,128)(2,1)} %param.26) | copy-start | bytes 393220
  36.9 38.0 %copy-start.7 = (f32[1024,256]{1,0:T(8,128)S(1)}, f32[1024,256]{1,0:T(8,128)}, u32[]{:S(2)}) copy-start(f32[1024,256]{1,0:T(8,128)} %get-tuple-element.25) | copy-start | bytes 3145732
  78.7 6.3 %copy-start.103 = (s32[1,4]{1,0:T(1,128)S(1)}, s32[1,4]{1,0:T(1,128)}, u32[]{:S(2)}) copy-start(s32[1,4]{1,0:T(1,128)} %len_ref.5) | copy-start | bytes 52
  78.7 8.1 %copy-start.39 = (bf16[32,256]{1,0:T(8,128)(2,1)S(1)}, bf16[32,256]{1,0:T(8,128)(2,1)}, u32[]{:S(2)}) copy-start(bf16[32,256]{1,0:T(8,128)(2,1)} %param.29) | copy-start | bytes 49156
  78.7 9.4 %copy-start.2 = (bf16[1,1024,256]{2,1,0:T(8,128)(2,1)S(1)}, bf16[1,1024,256]{2,1,0:T(8,128)(2,1)}, u32[]{:S(2)}) copy-start(bf16[1,1024,256]{2,1,0:T(8,128)(2,1)} %param.20) | copy-start | bytes 1572868
  80.4 21.2 %collective-permute-start = (bf16[16,256]{1,0:T(8,128)(2,1)}, bf16[16,256]{1,0:T(8,128)(2,1)}, u32[]{:S(2)}, u32[]{:S(2)}) collective-permute-start(bf16[16,256]{1,0:T(8,128)(2,1)} %get-tuple-element.149), channel_id=1, source_target_pairs={{0,1},{1,2},{2,3},{4,5},{5,6},{6,7},{8,9},{9,10},{10,11},{12,13},{... | collective-permute-start | bytes 24584 | tf_op jit(solution)/shard_map/ppermute | solution.py:414
  83.5 18.1 %collective-permute-start.1 = (bf16[16,256]{1,0:T(8,128)(2,1)}, bf16[16,256]{1,0:T(8,128)(2,1)}, u32[]{:S(2)}, u32[]{:S(2)}) collective-permute-start(bf16[16,256]{1,0:T(8,128)(2,1)} %get-tuple-element.150), channel_id=1, source_target_pairs={{1,0},{2,1},{3,2},{5,4},{6,5},{7,6},{9,8},{10,9},{11,10},{13,12},{... | collective-permute-start | bytes 24584 | tf_op jit(solution)/shard_map/ppermute | solution.py:415
  88.9 7.2 %copy-start.60 = (f32[256]{0:T(256)}, f32[256]{0:T(256)S(1)}, u32[]{:S(2)}) copy-start(f32[256]{0:T(256)S(1)} %convert_element_type.306) | copy-start | bytes 3076
  92.2 6.5 %copy-start.129 = (bf16[256]{0:T(256)(128)(2,1)S(1)}, bf16[256]{0:T(256)(128)(2,1)}, u32[]{:S(2)}) copy-start(bf16[256]{0:T(256)(128)(2,1)} %param.30) | copy-start | bytes 1540
  92.2 7.0 %copy-start.135 = (bf16[256]{0:T(256)(128)(2,1)S(1)}, bf16[256]{0:T(256)(128)(2,1)}, u32[]{:S(2)}) copy-start(bf16[256]{0:T(256)(128)(2,1)} %param.31) | copy-start | bytes 1540
  92.3 7.6 %copy-start.136 = (bf16[256]{0:T(256)(128)(2,1)S(1)}, bf16[256]{0:T(256)(128)(2,1)}, u32[]{:S(2)}) copy-start(bf16[256]{0:T(256)(128)(2,1)} %param.33) | copy-start | bytes 1540
  92.3 8.1 %copy-start.137 = (bf16[256]{0:T(256)(128)(2,1)S(1)}, bf16[256]{0:T(256)(128)(2,1)}, u32[]{:S(2)}) copy-start(bf16[256]{0:T(256)(128)(2,1)} %param.36) | copy-start | bytes 1540
  127.6 16.5 %copy-start.101 = (f32[256]{0:T(256)}, f32[256]{0:T(256)S(1)}, u32[]{:S(2)}) copy-start(f32[256]{0:T(256)S(1)} %div.149) | copy-start | bytes 3076
  128.1 16.0 %copy-start.102 = (f32[256]{0:T(256)}, f32[256]{0:T(256)S(1)}, u32[]{:S(2)}) copy-start(f32[256]{0:T(256)S(1)} %add_rsqrt_fusion) | copy-start | bytes 3076
  145.0 16.8 %copy-start.130 = (bf16[256]{0:T(256)(128)(2,1)S(1)}, bf16[256]{0:T(256)(128)(2,1)}, u32[]{:S(2)}) copy-start(bf16[256]{0:T(256)(128)(2,1)} %param.30) | copy-start | bytes 1540
  145.0 17.5 %copy-start.64 = (f32[256]{0:T(256)S(1)}, f32[256]{0:T(256)}, u32[]{:S(2)}) copy-start(f32[256]{0:T(256)} %copy-done.63) | copy-start | bytes 3076
  166.9 6.1 %copy-start.13 = (f32[1024,256]{1,0:T(8,128)S(1)}, f32[1024,256]{1,0:T(8,128)}, u32[]{:S(2)}) copy-start(f32[1024,256]{1,0:T(8,128)} %copy-done.11) | copy-start | bytes 3145732
  166.9 6.1 %copy-start.16 = (f32[1024,256]{1,0:T(8,128)S(1)}, f32[1024,256]{1,0:T(8,128)}, u32[]{:S(2)}) copy-start(f32[1024,256]{1,0:T(8,128)} %copy-done.15) | copy-start | bytes 3145732
  169.5 5.7 %collective-permute-start.2 = (bf16[16,256]{1,0:T(8,128)(2,1)S(1)}, bf16[16,256]{1,0:T(8,128)(2,1)S(1)}, u32[]{:S(2)}, u32[]{:S(2)}) collective-permute-start(bf16[16,256]{1,0:T(8,128)(2,1)S(1)} %get-tuple-element.147), channel_id=1, source_target_pairs={{0,1},{1,2},{2,3},{4,5},{5,6},{6,7},{8,9},{9,10},{10,11},{12,13},{... | collective-permute-start | bytes 24584 | tf_op jit(solution)/shard_map/ppermute | solution.py:414
  171.7 4.6 collective-permute-start.3
  189.2 56.7 %copy-start.9 = (f32[1024,256]{1,0:T(8,128)}, f32[1024,256]{1,0:T(8,128)S(1)}, u32[]{:S(2)}) copy-start(f32[1024,256]{1,0:T(8,128)S(1)} %add_add_fusion.6) | copy-start | bytes 3145732
  287.3 46.3 %copy-start.19 = (f32[1024,256]{1,0:T(8,128)S(1)}, f32[1024,256]{1,0:T(8,128)}, u32[]{:S(2)}) copy-start(f32[1024,256]{1,0:T(8,128)} %copy-done.18) | copy-start | bytes 3145732
  (120 other events, 373.3 us)
Sparse Core Ops, SparseCore 0:
  282.9 160.0 all-reduce.5

commit v2 on v1

--- a/solution.py
+++ b/solution.py
@@ -329,6 +329,343 @@
       compiler_params=pltpu.CompilerParams(vmem_limit_bytes=VMEM_LIMIT),name="attend_back")(lengths,x,o,lse,do)
 
 
+def axis_bits():
+    bits = []
+    for axis in ("sp", "dp"):
+        step = 1
+        while step < lax.axis_size(axis):
+            bits.append((axis, step))
+            step *= 2
+        assert step == lax.axis_size(axis)
+    return bits
+
+
+def swap_partner(axis, step):
+    place = {name: lax.axis_index(name) for name in ("dp", "sp")}
+    bit = lax.rem(place[axis] // step, 2)
+    place[axis] = place[axis] + step - 2 * step * bit
+    return (place["dp"], place["sp"]), bit
+
+
+def orders(bits):
+    sp_bits = [b for b in bits if b[0] == "sp"]
+    dp_bits = [b for b in bits if b[0] == "dp"]
+    first, far = sp_bits[:1], sp_bits[1:]
+    return {
+        "x_first": first + dp_bits[:1] + far + dp_bits[1:],
+        "y_first": first + far + dp_bits,
+        "y_last": first + dp_bits + far,
+        "z_first": first + dp_bits[1:] + dp_bits[:1] + far,
+        "z_mid": first + far + dp_bits[1:] + dp_bits[:1],
+    }
+
+
+def exchange_plan(rows, steps, offset):
+    sizes, size = [], rows
+    for _ in range(steps):
+        halves = size % 32 == 0
+        size = size // 2 if halves else size
+        sizes.append((halves, size, offset))
+        offset += size
+    return sizes, offset, size
+
+
+class Reduction:
+    def __init__(self, base, rows, staged, order, acc, stage, land, full, send, recv, source=None):
+        self.base, self.rows, self.order = base, rows, order
+        self.acc, self.stage, self.land, self.full = acc, stage, land, full
+        self.send, self.recv = send, recv
+        self.source = acc if source is None else source
+        self.low = base
+        self.sizes, _, self.own = exchange_plan(rows, len(order), staged)
+
+    def at(self, low, size):
+        return pl.ds(pl.multiple_of(low, 16), size)
+
+    def copy(self, step, src, dst):
+        partner, _ = swap_partner(*self.order[step[1]])
+        index = step[0] * len(self.order) + step[1]
+        return pltpu.make_async_remote_copy(
+            src_ref=src,
+            dst_ref=dst,
+            send_sem=self.send.at[index],
+            recv_sem=self.recv.at[index],
+            device_id=partner,
+            device_id_type=MESH,
+        )
+
+    def sum_copy(self, k):
+        _, moved, offset = self.sizes[k]
+        where = pl.ds(offset, moved)
+        return self.copy((0, k), self.stage.at[where, :], self.land.at[where, :])
+
+    def sum_send(self, k):
+        halves, moved, offset = self.sizes[k]
+        _, bit = swap_partner(*self.order[k])
+        away = self.low + (1 - bit) * moved if halves else self.low
+        source = self.source if k == 0 else self.acc
+        self.stage[offset : offset + moved, :] = source[self.at(away, moved), :].astype(BF16)
+        self.sum_copy(k).start()
+
+    def sum_recv(self, k):
+        halves, moved, offset = self.sizes[k]
+        _, bit = swap_partner(*self.order[k])
+        self.sum_copy(k).wait()
+        other = self.land[offset : offset + moved, :].astype(F32)
+        if halves:
+            self.low = self.low + bit * moved
+            source = self.source if k == 0 else self.acc
+            mine = source[self.at(self.low, moved), :]
+        else:
+            mine = self.stage[offset : offset + moved, :].astype(F32)
+        self.acc[self.at(self.low, moved), :] = mine + other
+
+    def close(self):
+        where = self.at(self.low, self.own)
+        self.full[where, :] = self.acc[where, :].astype(BF16)
+
+    def share_copy(self, k):
+        where = self.at(self.low, self.sizes[k][1])
+        return self.copy((1, k), self.full.at[where, :], self.full.at[where, :])
+
+    def share_send(self, k):
+        if self.sizes[k][0]:
+            self.share_copy(k).start()
+
+    def share_recv(self, k):
+        halves, moved, _ = self.sizes[k]
+        if halves:
+            self.share_copy(k).wait()
+            _, bit = swap_partner(*self.order[k])
+            self.low = self.low - bit * moved
+
+
+def run_sum(streams, steps):
+    for k in steps:
+        for stream in streams:
+            if k > 0:
+                stream.sum_recv(k - 1)
+            stream.sum_send(k)
+
+
+def run_share(streams, count):
+    for stream in streams:
+        stream.sum_recv(count - 1)
+        stream.close()
+        stream.share_send(count - 1)
+    for k in reversed(range(count)):
+        for stream in streams:
+            stream.share_recv(k)
+            if k > 0:
+                stream.share_send(k - 1)
+
+
+def back_kernel(
+    sp, chunk, parts, trig, tok, x1_ref, n2_ref, grad_x2, gain1, gain2, w_in, w_out, w_qkv, mid, small,
+    grad_ref, full, heads, joined, n1_keep, branch, act, hidden, gains, acc, stage, land,
+    send, recv, local, sum_send, sum_recv,
+):
+    me = lax.axis_index("sp")
+    frames, width = tok.shape
+    wide = w_in.shape[1]
+    head_width = parts.shape[1]
+    half = trig.shape[0] // 2
+    count = frames // chunk
+    peers = sp_peers(sp)
+    bits = axis_bits()
+    partners = [swap_partner(*bit)[0] for bit in bits if bit[0] == "dp"]
+    greet(peers + partners)
+
+    def copies(c):
+        cols = rows_at(c, chunk)
+        out = [
+            pltpu.make_async_remote_copy(
+                src_ref=parts.at[peer[1], :, cols],
+                dst_ref=heads.at[me, :, cols],
+                send_sem=send.at[i, c],
+                recv_sem=recv.at[i, c],
+                device_id=peer,
+                device_id_type=MESH,
+            )
+            for i, peer in enumerate(peers)
+        ]
+        return out, pltpu.make_async_copy(parts.at[me, :, cols], heads.at[me, :, cols], local.at[c])
+
+    def begin(c, carry):
+        out, own = copies(c)
+        for copy in out:
+            copy.start()
+        own.start()
+        return carry
+
+    lax.fori_loop(0, count, begin, 0)
+
+    order = orders(bits)
+    unit = 4 * width
+    plan = [
+        (0, 2 * unit, "y_last", mid),
+        (2 * unit, unit, "z_first", mid),
+        (3 * unit, unit, "z_first", None),
+        (4 * unit, unit, "x_first", None),
+        (5 * unit, unit, "y_first", None),
+    ]
+    steps = len(bits)
+    streams, staged = [], 0
+    for i, (base, rows, name, source) in enumerate(plan):
+        streams.append(
+            Reduction(
+                base, rows, staged, order[name], acc, stage, land, full, sum_send.at[i], sum_recv.at[i], source
+            )
+        )
+        staged = exchange_plan(rows, steps, staged)[1]
+    run_sum(streams[:2], range(steps))
+    gains[...] = jnp.zeros_like(gains)
+
+    def step(c, carry):
+        rows = rows_at(c, chunk)
+        out, own = copies(c)
+        for copy in out:
+            copy.wait()
+        own.wait()
+        sine, cosine = trig[0:half, rows], trig[half:, rows]
+        for head in range(sp):
+            base = head * head_width
+            for part in range(2):
+                low = part * 2 * half
+                first = heads[head, low : low + half, rows].astype(F32)
+                second = heads[head, low + half : low + 2 * half, rows].astype(F32)
+                low = base + low
+                joined[low : low + half, rows] = (first * cosine + second * sine).astype(BF16)
+                joined[low + half : low + 2 * half, rows] = (second * cosine - first * sine).astype(BF16)
+            joined[base + 4 * half : base + 6 * half, rows] = heads[head, 4 * half : 6 * half, rows]
+        grad = dg(joined[:, rows], w_qkv[...], 0, 0)
+        hat, inv = norm_parts(x1_ref[rows, :])
+        gains[1:2, :] += jnp.sum(grad * hat, axis=0, keepdims=True)
+        grad_x1 = grad_x2[rows, :] + norm_back(grad, hat, inv, gain2[...].astype(F32))
+        low_grad = (0.5 * grad_x1).astype(BF16)
+        branch[rows, :] = low_grad
+        hat, inv = norm_parts(tok[rows, :].astype(F32))
+        gain = gain1[...].astype(F32)
+        n1 = (hat * gain).astype(BF16)
+        n1_keep[rows, :] = n1
+        a = dg(n1, w_in[...], 1, 0)
+        sig = sigmoid(a)
+        act[rows, :] = (a * sig).astype(BF16)
+        grad = dg(low_grad, w_out[...], 1, 1)
+        low_hidden = (grad * (sig * (1.0 + a * (1.0 - sig)))).astype(BF16)
+        hidden[rows, :] = low_hidden
+        grad = dg(low_hidden, w_in[...], 1, 1)
+        gains[0:1, :] += jnp.sum(grad * hat, axis=0, keepdims=True)
+        grad_ref[rows, :] = (grad_x1 + norm_back(grad, hat, inv, gain)).astype(BF16)
+        return carry
+
+    lax.fori_loop(0, count, step, 0)
+    run_share(streams[:2], steps)
+    base = 3 * unit
+    acc[base : base + 3 * width, :] = dg(joined[...], n2_ref[...], 1, 0)
+    base = base + 3 * width
+    acc[base : base + 8, :] = small[0:8, :] + gains[...]
+    acc[base + 8 : base + 64, :] = small[8:64, :]
+    acc[base + 64 : 4 * unit, :] = jnp.zeros((width - 64, width), F32)
+    streams[2].sum_send(0)
+    for j in range(wide // width):
+        base = 4 * unit + j * width
+        acc[base : base + width, :] = dg(act[:, j * width : (j + 1) * width], branch[...], 0, 0)
+    streams[3].sum_send(0)
+    for j in range(wide // width):
+        base = 5 * unit + j * width
+        acc[base : base + width, :] = dg(n1_keep[...], hidden[:, j * width : (j + 1) * width], 0, 0)
+    streams[4].sum_send(0)
+    run_sum(streams[2:], range(1, steps))
+    run_share(streams[2:], steps)
+
+
+def back(parts, trig, tok, x1, n2, grad_x2, gain1, gain2, w_in, w_out, w_qkv, mid, small):
+    frames, width = tok.shape
+    sp = parts.shape[0]
+    chunk = min(256, frames)
+    count = frames // chunk
+    wide = w_in.shape[1]
+    rows = 6 * 4 * width
+    steps = len(axis_bits())
+    staged = exchange_plan(8 * width, steps, 0)[1] + 4 * exchange_plan(4 * width, steps, 0)[1]
+    return pl.pallas_call(
+        functools.partial(back_kernel, sp, chunk),
+        out_shape=[
+            jax.ShapeDtypeStruct((frames, width), BF16),
+            jax.ShapeDtypeStruct((rows, width), BF16),
+        ],
+        in_specs=[pl.BlockSpec(memory_space=pl.ANY)] + [VMEM] * 12,
+        out_specs=[VMEM] * 2,
+        scratch_shapes=[
+            pltpu.VMEM(parts.shape, BF16),
+            pltpu.VMEM((3 * width, frames), BF16),
+            pltpu.VMEM((frames, width), BF16),
+            pltpu.VMEM((frames, width), BF16),
+            pltpu.VMEM((frames, wide), BF16),
+            pltpu.VMEM((frames, wide), BF16),
+            pltpu.VMEM((8, width), F32),
+            pltpu.VMEM((rows, width), F32),
+            pltpu.VMEM((staged, width), BF16),
+            pltpu.VMEM((staged, width), BF16),
+            DMA((sp - 1, count)),
+            DMA((sp - 1, count)),
+            DMA((count,)),
+            DMA((5, 2 * steps)),
+            DMA((5, 2 * steps)),
+        ],
+        compiler_params=pltpu.CompilerParams(
+            collective_id=6, has_side_effects=True, vmem_limit_bytes=VMEM_LIMIT
+        ),
+        name="back",
+    )(parts, trig, tok, x1, n2, grad_x2, gain1, gain2, w_in, w_out, w_qkv, mid, small)
+
+
+def unpack_kernel(full, in_two, out_two, point_one, point_two, out_weight, qkv, in_one, out_one, small):
+    width = full.shape[1]
+
+    def block(base):
+        return full[base : base + width, :].astype(F32)
+
+    unit = 4 * width
+    for j in range(4):
+        cols = slice(j * width, (j + 1) * width)
+        in_two[:, cols] = block(j * width)
+        out_two[cols, :] = block(unit + j * width)
+        out_one[cols, :] = block(4 * unit + j * width)
+        in_one[:, cols] = block(5 * unit + j * width)
+    base = 2 * unit
+    for j in range(2):
+        point_one[:, j * width : (j + 1) * width] = block(base + j * width)
+    point_two[...] = block(base + 2 * width)
+    out_weight[...] = block(base + 3 * width)
+    base = 3 * unit
+    head_dim = width // HEADS
+    for part in range(3):
+        rows = [
+            full[base + (3 * head + part) * head_dim : base + (3 * head + part + 1) * head_dim, :]
+            for head in range(HEADS)
+        ]
+        qkv[:, part * width : (part + 1) * width] = jnp.concatenate(rows, axis=0).astype(F32).T
+    small[...] = full[base + 3 * width : base + 3 * width + 64, :].astype(F32)
+
+
+def unpack(full):
+    width = full.shape[1]
+    shapes = [
+        (width, 4 * width), (4 * width, width), (width, 2 * width), (width, width), (width, width),
+        (width, 3 * width), (width, 4 * width), (4 * width, width), (64, width),
+    ]
+    return pl.pallas_call(
+        unpack_kernel,
+        out_shape=[jax.ShapeDtypeStruct(shape, F32) for shape in shapes],
+        in_specs=[VMEM],
+        out_specs=[VMEM] * len(shapes),
+        compiler_params=pltpu.CompilerParams(vmem_limit_bytes=VMEM_LIMIT),
+        name="unpack",
+    )(full)
+
+
 def exchange_kernel(sp, parts, heads, send, recv, local):
     me = lax.axis_index("sp")
     peers = sp_peers(sp)
@@ -548,33 +885,26 @@
     grad_out_weight = dg(context, grad_attn_out, 1, 0)
     grad_context = dg(w_out, grad_attn_out, 1, 1).astype(BF16).reshape(sp, head_dim, frames)
     grad_heads = attend_back(heads, lengths, raw_context, log_sums, exchange(grad_context, 4))
-    grad_parts = exchange(grad_heads, 5).reshape(HEADS, 3, 2, half, frames).astype(F32)
-    sine, cosine = trig[:half], trig[half:]
-    first, second = grad_parts[:, :2, 0], grad_parts[:, :2, 1]
-    turned = jnp.stack([first * cosine + second * sine, second * cosine - first * sine], axis=2)
-    grad_joined = jnp.concatenate([turned, grad_parts[:, 2:]], axis=1).astype(BF16)
-    grad_joined = grad_joined.reshape(3 * width, frames)
-    grad_qkv = dg(grad_joined, attn_low, 1, 0).reshape(HEADS, 3, head_dim, width)
-    grad_qkv = grad_qkv.transpose(1, 0, 2, 3).reshape(3 * width, width).T
-    _, attn_norm_back = jax.vjp(layer_norm, after_first, gain_two)
-    grad_attn_input, grad_gain_two = attn_norm_back(dg(grad_joined, qkv_rows, 0, 0))
-    _, first_kept = feed_forward(tokens[0].astype(F32), gain_one, ffn1_in, ffn1_out)
-    grad_start, grad_gain_one, grad_in_one, grad_out_one = feed_back(
-        grad_attn_rows + grad_attn_input, first_kept, ffn1_in, ffn1_out
-    )
-    summed = lax.psum(
-        (
-            grad_gain_one, grad_in_one, grad_out_one, grad_gain_two, grad_qkv, grad_out_weight,
-            grad_gain_three, grad_point_one, grad_kernel, grad_norm_gain, grad_norm_bias,
-            grad_point_two, grad_gain_four, grad_in_two, grad_out_two, grad_gain_five,
-        )[:9] + (
-            grad_point_two, grad_gain_four, grad_in_two, grad_out_two, grad_gain_five,
-        ),
-        ("dp", "sp"),
-    )
+    def blocks(matrix):
+        return [matrix[:, k : k + width] for k in range(0, matrix.shape[1], width)]
+
+    mid = jnp.concatenate(
+        blocks(grad_in_two) + [grad_out_two] + blocks(grad_point_one) + [grad_point_two, grad_out_weight]
+    )
+    zero = jnp.zeros((1, width), F32)
+    small = jnp.concatenate(
+        [zero, zero, grad_gain_three[None], grad_gain_four[None], grad_gain_five[None], zero, zero, zero]
+        + [grad_kernel, jnp.zeros((56 - taps, width), F32)]
+    )
+    grad_start, full = back(
+        grad_heads, trig, tokens[0], after_first, attn_low, grad_attn_rows, ln1_gain[None], ln2_gain[None],
+        ffn1_in, ffn1_out, qkv_rows, mid, small,
+    )
+    in_two, out_two, point_one, point_two, out_weight, qkv, in_one, out_one, small = unpack(full)
     return (
-        (output[None].astype(BF16), grad_start[None].astype(BF16))
-        + summed[:9] + (grad_norm_gain, grad_norm_bias) + summed[9:]
+        output[None].astype(BF16), grad_start[None], small[0], in_one, out_one, small[1], qkv, out_weight,
+        small[2], point_one, small[8 : 8 + taps], grad_norm_gain, grad_norm_bias, point_two, small[3],
+        in_two, out_two, small[4],
     )
 
 

time: 465 us -> 332 us (0.71)
  waiting for transfers between devices: 109 us -> 1.83 us
  Pallas kernels: 165 us -> 241 us
  blocking collectives: 43.1 us -> 0 us
  matrix products: 36.2 us -> 16.5 us
  between operations: 17.2 us -> 2.89 us
  other arithmetic: 50.7 us -> 39.9 us
  local copies, waits for them, and re-layouts: 31.5 us -> 21.8 us
    psum x1 -> x0, waiting for transfers between devices: 108 us -> none  [on_device(): lax.psum((grad_gain_one, grad_in_one, grad_out_one, grad_gain_two, grad_q...]
    pallas_call x0 -> x2, Pallas kernels: none -> 96.3 us  [the longest x1 91.5 us: back(): pl.pallas_call(functools.partial(back_kernel, sp, chunk), out_shape=[jax....]
    psum x1 -> x0, blocking collectives: 43.1 us -> none  [on_device(): lax.psum((grad_gain_one, grad_in_one, grad_out_one, grad_gain_two, grad_q...]
    pallas_call x3 -> x2, Pallas kernels: 37.8 us -> 17.5 us  [exchange(): pl.pallas_call(functools.partial(exchange_kernel, sp), out_shape=jax.Shap...]
    dot_general x22 -> x15, matrix products: 36.2 us -> 16.5 us  [dg(): lax.dot_general(left, right, (((left_dim,), (right_dim,)), ((), ())), pre...]
    unnamed x287 -> x182, local copies, waits for them, and re-layouts: 21.1 us -> 9.24 us
  transfers between devices with their start and end apart: 5 -> 4, of which waited for: 2 -> 1; matrix products, arithmetic and copies ran while one was open for 6% -> 3% of each run, Pallas kernels for 0% -> 0%
where the time goes in v2:
time: 332 us; the launch traced here: 331 us
  Pallas kernels  241 us (73%)
  other arithmetic  39.9 us (12%)
  local copies, waits for them, and re-layouts  21.8 us (7%)
  matrix products  16.5 us (5%)
  starting transfers between devices  7.02 us (2%)
    pallas_call x1, Pallas kernels, back(): pl.pallas_call(functools.partial(back_kernel, sp, chunk), out_shape=[jax....  91.5 us
    pallas_call x1, Pallas kernels, attend_back(): pl.pallas_call(functools.partial(bwd_kernel, lengths.shape[1], bq, bk), o...  45.7 us
    pallas_call x1, Pallas kernels, attend(): pl.pallas_call(functools.partial(fwd_kernel, lengths.shape[1], min(bq, fr...  29.5 us
    pallas_call x2, Pallas kernels, gather_all(): pl.pallas_call(functools.partial(gather_kernel, sp, dp), out_shape=jax.Sh...  26.9 us
    pallas_call x1, Pallas kernels, front(): pl.pallas_call(functools.partial(front_kernel, sp, lengths.shape[1], chun...  25.2 us
    pallas_call x2, Pallas kernels, exchange(): pl.pallas_call(functools.partial(exchange_kernel, sp), out_shape=jax.Shap...  17.5 us
    dot_general x15, matrix products, dg(): lax.dot_general(left, right, (((left_dim,), (right_dim,)), ((), ())), pre...  16.5 us
    unnamed x182, local copies, waits for them, and re-layouts  9.24 us
  transfers between devices with their start and end apart: 4, of which 1 were waited for; matrix products, arithmetic and copies ran while one was open for 3% of the time, Pallas kernels for 0%

profile of v2, /device:TPU:0, one launch (start us, length us, event | category | flops | bytes accessed | tf_op | source)
XLA Modules:
  0.0 331.0 jit_solution(10219938959130354991)
XLA Ops:
  5.1 25.2 %front.1 = (f32[1024,256]{1,0:T(8,128)}, bf16[1024,256]{1,0:T(8,128)(2,1)}, f32[64,1024]{1,0:T(8,128)}, bf16[4,192,1024]{2,1,0:T(8,128)(2,1)}) custom-call(s32[1,4]{1,0:T(1,128)} %len_ref.5, bf16[1024,256]{1,0:T(8,128)(2,1)} %bitcast.137, bf16[1,256]{1,0:T(2,128)(2,1)} %broadcast_in_dim.24.gain1, bf16[256,1024]{1,0:T(8,128)(2,1)} %w_in.3, ...), custom_call_target="tpu_custom_call" | custom-call | tf_op jit(solution)/shard_map/front/pallas_call | solution.py:196
  30.3 29.5 %attend.1 = (bf16[4,64,1024]{2,1,0:T(8,128)(2,1)}, f32[4,64,1024]{2,1,0:T(8,128)}, f32[1,4096]{1,0:T(1,128)}) custom-call(s32[1,4]{1,0:T(1,128)} %len_ref.5, bf16[4,192,1024]{2,1,0:T(8,128)(2,1)} %get-tuple-element.37.x_ref), custom_call_target="tpu_custom_call" | custom-call | tf_op jit(solution)/shard_map/attend/pallas_call | solution.py:261
  59.8 8.4 %exchange.2 = bf16[4,64,1024]{2,1,0:T(8,128)(2,1)} custom-call(bf16[4,64,1024]{2,1,0:T(8,128)(2,1)} %get-tuple-element.38.parts), custom_call_target="tpu_custom_call" | custom-call | tf_op jit(solution)/shard_map/exchange/pallas_call | solution.py:696
  68.3 1.5 fusion.147
  73.0 2.5 collective-permute-start
  86.3 8.5 %multiply_reduce_fusion.40 = (f32[256]{0:T(256)S(1)}, f32[1024,256]{1,0:T(8,128)S(1)}) fusion(f32[1024]{0:T(1024)S(1)} %get-tuple-element.187, f32[1024]{0:T(1024)S(1)} %get-tuple-element.155, f32[1056,256]{1,0:T(8,128)S(1)} %maximum_convert_fusion, f32[256]{0:T(256)} %bitcast.203, f32[1024]{0:T(1024)S(1)} %get-tuple-element.156, f32[256]{0:T(256)} %bitcast.201, ...), kind=kLoop, calls=%fused_computation.177 | loop fusion | flops 25427712 | bytes 34771968 | tf_op jit(solution)/shard_map/reduce_sum | solution.py:836
  96.7 13.7 %gather_all.2 = f32[32,8,256]{2,1,0:T(8,128)} custom-call(f32[8,256]{1,0:T(8,128)} %maximum_maximum_fusion.x_ref), custom_call_target="tpu_custom_call" | custom-call | tf_op jit(solution)/shard_map/gather_all/pallas_call | solution.py:736
  111.8 1.8 fusion.148
  118.9 2.2 fusion.2
  123.4 1.7 fusion.137
  125.8 13.3 %gather_all.3 = f32[32,8,256]{2,1,0:T(8,128)} custom-call(f32[8,256]{1,0:T(8,128)} %maximum_maximum_fusion.1.x_ref), custom_call_target="tpu_custom_call" | custom-call | tf_op jit(solution)/shard_map/gather_all/pallas_call | solution.py:736
  140.2 3.8 %multiply_reduce_fusion = (f32[256]{0:T(256)S(1)}, f32[256]{0:T(256)S(1)}, f32[256]{0:T(256)S(1)}, f32[256]{0:T(256)S(1)}, f32[256]{0:T(256)S(1)}, /*index=5*/f3...) fusion(f32[1056,256]{1,0:T(8,128)S(1)} %maximum_convert_fusion, ...), kind=kLoop, calls=%fused_computation.128 | loop fusion | flops 9172736 | bytes 12639232 | tf_op jit(solution)/shard_map/reduce_sum | solution.py:878
  144.1 2.1 multiply_reduce_fusion.18
  147.2 1.9 multiply_reduce_fusion.9
  150.2 1.9 collective-permute-start.2
  154.9 1.8 collective-permute-done.3
  157.1 7.8 %fusion.10 = (f32[1024,256]{1,0:T(8,128)S(1)}, f32[1024,256]{1,0:T(8,128)S(1)}) fusion(f32[1024,512]{1,0:T(8,128)S(1)} %copy-done.2, f32[1024]{0:T(1024)S(1)} %copy-done.32, f32[1056,256]{1,0:T(8,128)S(1)} %maximum_convert_fusion.1, f32[256]{0:T(256)S(1)} %bitcast.204, f32[1024]{0:T(1024)S(1)} %copy-done.31, f32[256]{0:T(256)S(1)} %bitcast.202, ...), kind=kLoop, calls=%fused_computation.28 | loop fusion | flops 26738688 | bytes 37912576 | tf_op jit(solution)/shard_map/transpose(jvp())/mul | solution.py:768
  170.9 1.7 copy-done.17
  172.6 9.1 %exchange.3.do_ref = bf16[4,64,1024]{2,1,0:T(8,128)(2,1)} custom-call(bf16[4,64,1024]{2,1,0:T(8,128)(2,1)} %bitcast.136), custom_call_target="tpu_custom_call" | custom-call | tf_op jit(solution)/shard_map/exchange/pallas_call | solution.py:696
  181.7 45.7 %attend_back.1.parts = bf16[4,192,1024]{2,1,0:T(8,128)(2,1)} custom-call(s32[1,4]{1,0:T(1,128)} %len_ref.5, bf16[4,192,1024]{2,1,0:T(8,128)(2,1)} %get-tuple-element.37.x_ref, f32[4,64,1024]{2,1,0:T(8,128)} %get-tuple-element.39.o_ref, f32[1,4096]{1,0:T(1,128)} %get-tuple-element.40.lse_ref, bf16[4,64,1024]{2,1,0:T(8,128)(2,1)} %exchange.3.do_ref), custom_call_target="tpu_custom_call" | custom-call | tf_op jit(solution)/shard_map/attend_back/pallas_call | solution.py:324
  227.4 3.7 %concatenate.31.small = f32[64,256]{1,0:T(8,128)} concatenate(f32[2,256]{1,0:T(2,128)S(1)} %concatenate.29, f32[1,256]{1,0:T(1,128)S(1)} %bitcast.235, f32[1,256]{1,0:T(1,128)S(1)} %bitcast.244, f32[1,256]{1,0:T(1,128)S(1)} %bitcast.207, f32[3,256]{1,0:T(4,128)S(1)} %concatenate.30, f32[1,256]{1,0:T(1,128)S(1)} %bitcast.241, f32[1,256]{1,0:T(1,128)S(1)} %bitcast.240, ...), dimensions={0} | concatenate | bytes 131072 | tf_op jit(solution)/shard_map/concatenate | solution.py:895
  231.1 91.5 %back.1 = (bf16[1024,256]{1,0:T(8,128)(2,1)}, bf16[6144,256]{1,0:T(8,128)(2,1)}) custom-call(bf16[4,192,1024]{2,1,0:T(8,128)(2,1)} %attend_back.1.parts, f32[64,1024]{1,0:T(8,128)} %get-tuple-element.41.trig, bf16[1024,256]{1,0:T(8,128)(2,1)} %bitcast.138, f32[1024,256]{1,0:T(8,128)} %get-tuple-element.36.x1_ref, ...), custom_call_target="tpu_custom_call" | custom-call | tf_op jit(solution)/shard_map/back/pallas_call | solution.py:592
  322.7 4.7 %unpack.1 = (f32[256,1024]{1,0:T(8,128)}, f32[1024,256]{1,0:T(8,128)}, f32[256,512]{1,0:T(8,128)}, f32[256,256]{1,0:T(8,128)}, f32[256,256]{1,0:T(8,128)}, /*ind...) custom-call(bf16[6144,256]{1,0:T(8,128)(2,1)} %get-tuple-element.44.full), custom_call_target="tpu_custom_call" | custom-call | tf_op jit(solution)/shard_map/unpack/pallas_call | solution.py:659
  328.8 1.5 fusion.144
  (263 shorter events, 42.7 us)
Async XLA Ops:
  0.7 113.4 %copy-start = (bf16[256,1024]{1,0:T(8,128)(2,1)S(1)}, bf16[256,1024]{1,0:T(8,128)(2,1)}, u32[]{:S(2)}) copy-start(bf16[256,1024]{1,0:T(8,128)(2,1)} %param.34) | copy-start | bytes 1572868
  0.7 67.6 %copy-start.24 = (bf16[256,256]{1,0:T(8,128)(2,1)S(1)}, bf16[256,256]{1,0:T(8,128)(2,1)}, u32[]{:S(2)}) copy-start(bf16[256,256]{1,0:T(8,128)(2,1)} %param.26) | copy-start | bytes 393220
  30.3 38.0 %copy-start.16 = (f32[1024,256]{1,0:T(8,128)S(1)}, f32[1024,256]{1,0:T(8,128)}, u32[]{:S(2)}) copy-start(f32[1024,256]{1,0:T(8,128)} %get-tuple-element.36.x1_ref) | copy-start | bytes 3145732
  30.3 40.5 %copy-start.82 = (bf16[256]{0:T(256)(128)(2,1)S(1)}, bf16[256]{0:T(256)(128)(2,1)}, u32[]{:S(2)}) copy-start(bf16[256]{0:T(256)(128)(2,1)} %param.27) | copy-start | bytes 1540
  30.3 40.5 %copy-start.21 = (bf16[256,512]{1,0:T(8,128)(2,1)S(1)}, bf16[256,512]{1,0:T(8,128)(2,1)}, u32[]{:S(2)}) copy-start(bf16[256,512]{1,0:T(8,128)(2,1)} %param.28) | copy-start | bytes 786436
  70.2 6.7 %copy-start.73 = (s32[1,4]{1,0:T(1,128)S(1)}, s32[1,4]{1,0:T(1,128)}, u32[]{:S(2)}) copy-start(s32[1,4]{1,0:T(1,128)} %len_ref.5) | copy-start | bytes 52
  70.8 6.1 %copy-start.36 = (f32[256]{0:T(256)}, f32[256]{0:T(256)S(1)}, u32[]{:S(2)}) copy-start(f32[256]{0:T(256)S(1)} %convert_element_type.189) | copy-start | bytes 3076
  70.8 7.8 %copy-start.26 = (bf16[32,256]{1,0:T(8,128)(2,1)S(1)}, bf16[32,256]{1,0:T(8,128)(2,1)}, u32[]{:S(2)}) copy-start(bf16[32,256]{1,0:T(8,128)(2,1)} %param.29) | copy-start | bytes 49156
  70.8 11.2 %copy-start.78 = (bf16[256]{0:T(256)(128)(2,1)S(1)}, bf16[256]{0:T(256)(128)(2,1)}, u32[]{:S(2)}) copy-start(bf16[256]{0:T(256)(128)(2,1)} %param.30) | copy-start | bytes 1540
  70.8 11.7 %copy-start.83 = (bf16[256]{0:T(256)(128)(2,1)S(1)}, bf16[256]{0:T(256)(128)(2,1)}, u32[]{:S(2)}) copy-start(bf16[256]{0:T(256)(128)(2,1)} %param.31) | copy-start | bytes 1540
  70.8 12.3 %copy-start.84 = (bf16[256]{0:T(256)(128)(2,1)S(1)}, bf16[256]{0:T(256)(128)(2,1)}, u32[]{:S(2)}) copy-start(bf16[256]{0:T(256)(128)(2,1)} %param.33) | copy-start | bytes 1540
  70.8 12.8 %copy-start.85 = (bf16[256]{0:T(256)(128)(2,1)S(1)}, bf16[256]{0:T(256)(128)(2,1)}, u32[]{:S(2)}) copy-start(bf16[256]{0:T(256)(128)(2,1)} %param.36) | copy-start | bytes 1540
  73.0 11.9 %collective-permute-start = (bf16[16,256]{1,0:T(8,128)(2,1)S(1)}, bf16[16,256]{1,0:T(8,128)(2,1)S(1)}, u32[]{:S(2)}, u32[]{:S(2)}) collective-permute-start(bf16[16,256]{1,0:T(8,128)(2,1)S(1)} %get-tuple-element.113), channel_id=1, source_target_pairs={{0,1},{1,2},{2,3},{4,5},{5,6},{6,7},{8,9},{9,10},{10,11},{12,13},{... | collective-permute-start | bytes 24584 | tf_op jit(solution)/shard_map/ppermute | solution.py:751
  75.5 10.0 %collective-permute-start.1 = (bf16[16,256]{1,0:T(8,128)(2,1)S(1)}, bf16[16,256]{1,0:T(8,128)(2,1)}, u32[]{:S(2)}, u32[]{:S(2)}) collective-permute-start(bf16[16,256]{1,0:T(8,128)(2,1)S(1)} %get-tuple-element.114), channel_id=1, source_target_pairs={{1,0},{2,1},{3,2},{5,4},{6,5},{7,6},{9,8},{10,9},{11,10},{13,12},{... | collective-permute-start | bytes 24584 | tf_op jit(solution)/shard_map/ppermute | solution.py:752
  86.3 25.5 %copy-start.77 = (f32[256]{0:T(256)S(1)}, f32[256]{0:T(256)}, u32[]{:S(2)}) copy-start(f32[256]{0:T(256)} %convert_element_type.228) | copy-start | bytes 3076
  86.3 25.5 %copy-start.81 = (bf16[256,256]{1,0:T(8,128)(2,1)S(1)}, bf16[256,256]{1,0:T(8,128)(2,1)}, u32[]{:S(2)}) copy-start(bf16[256,256]{1,0:T(8,128)(2,1)} %param.32) | copy-start | bytes 393220
  86.3 25.5 %copy-start.86 = (f32[256]{0:T(256)S(1)}, f32[256]{0:T(256)}, u32[]{:S(2)}) copy-start(f32[256]{0:T(256)} %convert_element_type.229) | copy-start | bytes 3076
  113.6 8.5 %copy-start.3 = (f32[1024,256]{1,0:T(8,128)}, f32[1024,256]{1,0:T(8,128)S(1)}, u32[]{:S(2)}) copy-start(f32[1024,256]{1,0:T(8,128)S(1)} %get-tuple-element.193) | copy-start | bytes 3145732
  123.4 16.8 %copy-start.79 = (bf16[256]{0:T(256)(128)(2,1)S(1)}, bf16[256]{0:T(256)(128)(2,1)}, u32[]{:S(2)}) copy-start(bf16[256]{0:T(256)(128)(2,1)} %param.30) | copy-start | bytes 1540
  149.1 4.4 %copy-start.10 = (bf16[1024,1024]{1,0:T(8,128)(2,1)S(1)}, bf16[1024,1024]{1,0:T(8,128)(2,1)}, u32[]{:S(2)}) copy-start(bf16[1024,1024]{1,0:T(8,128)(2,1)} %copy-done.9) | copy-start | bytes 6291460
  150.2 4.7 %collective-permute-start.2 = (bf16[16,256]{1,0:T(8,128)(2,1)S(1)}, bf16[16,256]{1,0:T(8,128)(2,1)S(1)}, u32[]{:S(2)}, u32[]{:S(2)}) collective-permute-start(bf16[16,256]{1,0:T(8,128)(2,1)S(1)} %get-tuple-element.111), channel_id=1, source_target_pairs={{0,1},{1,2},{2,3},{4,5},{5,6},{6,7},{8,9},{9,10},{10,11},{12,13},{... | collective-permute-start | bytes 24584 | tf_op jit(solution)/shard_map/ppermute | solution.py:751
  152.1 4.6 %collective-permute-start.3 = (bf16[16,256]{1,0:T(8,128)(2,1)S(1)}, bf16[16,256]{1,0:T(8,128)(2,1)S(1)}, u32[]{:S(2)}, u32[]{:S(2)}) collective-permute-start(bf16[16,256]{1,0:T(8,128)(2,1)S(1)} %get-tuple-element.112), channel_id=1, source_target_pairs={{1,0},{2,1},{3,2},{5,4},{6,5},{7,6},{9,8},{10,9},{11,10},{13,12},{... | collective-permute-start | bytes 24584 | tf_op jit(solution)/shard_map/ppermute | solution.py:752
  169.4 58.0 %copy-start.5 = (f32[1024,256]{1,0:T(8,128)}, f32[1024,256]{1,0:T(8,128)S(1)}, u32[]{:S(2)}) copy-start(f32[1024,256]{1,0:T(8,128)S(1)} %add_add_fusion.3.grad_x2) | copy-start | bytes 3145732
  322.7 7.6 %copy-start.23 = (bf16[1024,256]{1,0:T(8,128)(2,1)S(1)}, bf16[1024,256]{1,0:T(8,128)(2,1)}, u32[]{:S(2)}) copy-start(bf16[1024,256]{1,0:T(8,128)(2,1)} %get-tuple-element.43) | copy-start | bytes 1572868
  (67 other events, 174.3 us)

commit v3 on v2

--- a/solution.py
+++ b/solution.py
@@ -143,13 +143,13 @@
         rows = rows_at(c, chunk)
         x = tok[rows, :].astype(F32)
         hat, _ = norm_parts(x)
-        n1 = (hat * gain1[...].astype(F32)).astype(BF16)
+        n1 = (hat * row_of(gain1)).astype(BF16)
         a = dg(n1, w_in[...], 1, 0)
         s = (a * sigmoid(a)).astype(BF16)
         x1 = x + 0.5 * dg(s, w_out[...], 1, 0)
         x1_ref[rows, :] = x1
         hat, _ = norm_parts(x1)
-        n2 = (hat * gain2[...].astype(F32)).astype(BF16)
+        n2 = (hat * row_of(gain2)).astype(BF16)
         n2_ref[rows, :] = n2
         joined = dg(w_qkv[...], n2, 1, 1)
         sine, cosine = sine_cosine(
@@ -329,6 +329,469 @@
       compiler_params=pltpu.CompilerParams(vmem_limit_bytes=VMEM_LIMIT),name="attend_back")(lengths,x,o,lse,do)
 
 
+def row_of(ref):
+    return ref[...].astype(F32).reshape(1, ref.shape[0])
+
+
+def halves_of(ref, rows):
+    return jnp.concatenate([ref[0, rows, :], ref[1, rows, :]], axis=1)
+
+
+def combine(entries):
+    count = sum(e[2] for e in entries)
+    safe = jnp.maximum(count, 1.0)
+    mean = sum(e[2] * e[0] for e in entries) / safe
+    spread = sum(e[1] + e[2] * (e[0] - mean) * (e[0] - mean) for e in entries)
+    return mean, spread, count
+
+
+def pick(ref):
+    return ref[0:1, :], ref[1:2, :], ref[2:3, :]
+
+
+def total(entries):
+    return tuple(sum(e[i] for e in entries) for i in range(3))
+
+
+def middle_kernel(
+    sp, dp, items, taps, chunk, block, len_ref, parts, x1_ref, cot, gain3, gain4, gain5, w_out, w_point1,
+    depthwise, bn_gain, bn_bias, w_point2, w_in, w_down,
+    out_ref, grad_x2, heads, mid, small, bn_grads,
+    ctx, x2_ref, n3_keep, point, glu, conv, low_lim, high_lim, act, hidden, n4_keep, branch, swish, branch2,
+    grad_x3, grad_y, grad_conv, grad_glu, grad_point, branch3, back_parts, tap_sums, edge_out, edge_in,
+    send_box, near_box, far_box, sums,
+    send, recv, local, back_send, back_recv, back_local, rim_send, rim_recv, box_send, box_recv,
+):
+    me, me_dp = lax.axis_index("sp"), lax.axis_index("dp")
+    frames, width = x1_ref.shape
+    lanes = width // 2
+    reach = taps // 2
+    count = frames // chunk
+    peers = sp_peers(sp)
+    far_peers = [(lax.rem(me_dp + step, dp), me) for step in range(1, dp)]
+    greeted = peers + far_peers
+    barrier = pltpu.get_barrier_semaphore()
+    length = sp * frames
+    ends = ends_of(len_ref, items)
+    first_frame = me * frames
+
+    def limits(b, carry):
+        rows = rows_at(b, chunk)
+        frame = first_frame + b * chunk + lax.broadcasted_iota(I32, (chunk, lanes), 0)
+        low, high = jnp.zeros_like(frame), jnp.full_like(frame, length)
+        for end in ends:
+            low = jnp.where(frame >= end, end, low)
+        for end in reversed(ends):
+            high = jnp.where(frame < end, end, high)
+        low_lim[rows, :] = low - frame
+        high_lim[rows, :] = high - 1 - frame
+        return carry
+
+    for ref in (glu, grad_conv):
+        for h in range(2):
+            ref[h, 0:reach, :] = jnp.zeros((reach, lanes), F32)
+            ref[h, reach + frames :, :] = jnp.zeros((reach, lanes), F32)
+    edge_in[...] = jnp.zeros_like(edge_in)
+    send_box[...] = jnp.zeros_like(send_box)
+    for device in greeted:
+        pl.semaphore_signal(barrier, inc=1, device_id=device, device_id_type=MESH)
+    lax.fori_loop(0, count, limits, 0)
+    tap_sums[...] = jnp.zeros_like(tap_sums)
+    sums[...] = jnp.zeros_like(sums)
+    pl.semaphore_wait(barrier, len(greeted))
+
+    def moves(c, source, target, send_sems, recv_sems, local_sems):
+        cols = rows_at(c, chunk)
+        out = [
+            pltpu.make_async_remote_copy(
+                src_ref=source.at[peer[1], :, cols],
+                dst_ref=target.at[me, :, cols],
+                send_sem=send_sems.at[i, c],
+                recv_sem=recv_sems.at[i, c],
+                device_id=peer,
+                device_id_type=MESH,
+            )
+            for i, peer in enumerate(peers)
+        ]
+        return out + [pltpu.make_async_copy(source.at[me, :, cols], target.at[me, :, cols], local_sems.at[c])]
+
+    def context_moves(c):
+        return moves(c, parts, ctx, send, recv, local)
+
+    def begin(c, carry):
+        for copy in context_moves(c):
+            copy.start()
+        return carry
+
+    lax.fori_loop(0, count, begin, 0)
+
+    def open_step(c, carry):
+        rows = rows_at(c, chunk)
+        for copy in context_moves(c):
+            copy.wait()
+        context = ctx[:, :, rows].reshape(width, chunk)
+        x2 = x1_ref[rows, :] + dg(context, w_out[...], 0, 0)
+        x2_ref[rows, :] = x2
+        hat, _ = norm_parts(x2)
+        n3 = (hat * row_of(gain3)).astype(BF16)
+        n3_keep[rows, :] = n3
+        pair = dg(n3, w_point1[...], 1, 0)
+        point[rows, :] = pair
+        gated = (pair[:, :width] * sigmoid(pair[:, width:])).astype(BF16).astype(F32)
+        where = pl.ds(pl.multiple_of(reach + c * chunk, 8), chunk)
+        glu[0, where, :] = gated[:, :lanes]
+        glu[1, where, :] = gated[:, lanes:]
+        return carry
+
+    lax.fori_loop(0, count, open_step, 0)
+
+    def rim_copies(call, side, source, target):
+        peer = (me_dp, me - 1 if side == 0 else me + 1)
+        return pltpu.make_async_remote_copy(
+            src_ref=source, dst_ref=target, send_sem=rim_send.at[call, side], recv_sem=rim_recv.at[call, side],
+            device_id=peer, device_id_type=MESH,
+        )
+
+    def swap_rims(call, sources, targets):
+        @pl.when(me > 0)
+        def _():
+            rim_copies(call, 0, sources[0], targets[1]).start()
+
+        @pl.when(me < sp - 1)
+        def _():
+            rim_copies(call, 1, sources[1], targets[0]).start()
+
+    def await_rims(call, sources, targets):
+        @pl.when(me > 0)
+        def _():
+            rim_copies(call, 0, sources[0], targets[1]).wait_send()
+            rim_copies(call, 1, sources[1], targets[0]).wait_recv()
+
+        @pl.when(me < sp - 1)
+        def _():
+            rim_copies(call, 1, sources[1], targets[0]).wait_send()
+            rim_copies(call, 0, sources[0], targets[1]).wait_recv()
+
+    for side, rows in ((0, slice(reach, 2 * reach)), (1, slice(frames, frames + reach))):
+        for h in range(2):
+            edge_out[side, 0:reach, h * lanes : (h + 1) * lanes] = glu[h, rows, :]
+    glu_rims = (
+        [edge_out.at[0, 0:reach, :], edge_out.at[1, 0:reach, :]],
+        [edge_in.at[0, 0:reach, :], edge_in.at[1, 0:reach, :]],
+    )
+    swap_rims(0, *glu_rims)
+
+    zero = jnp.zeros((block, lanes), F32)
+
+    def conv_step(b, carry):
+        low, high = low_lim[rows_at(b, block), :], high_lim[rows_at(b, block), :]
+        start = pl.multiple_of(b * block, block)
+        result = [zero, zero]
+        for tap in range(taps):
+            shift = tap - reach
+            inside = (low <= shift) if shift < 0 else (high >= shift)
+            for h in range(2):
+                view = glu.at[h, pl.ds(start, block + 2 * reach), :]
+                term = jnp.where(inside, view[tap : tap + block, :], 0.0)
+                result[h] = result[h] + depthwise[tap : tap + 1, h * lanes : (h + 1) * lanes].astype(F32) * term
+        valid = (first_frame + start + lax.broadcasted_iota(I32, (block, lanes), 0)) < ends[-1]
+        for h in range(2):
+            conv[h, rows_at(b, block), :] = result[h]
+            sums[0:1, h * lanes : (h + 1) * lanes] += jnp.sum(jnp.where(valid, result[h], 0.0), axis=0, keepdims=True)
+        return carry
+
+    blocks = frames // block
+    lax.fori_loop(1, blocks - 1, conv_step, 0)
+    await_rims(0, *glu_rims)
+    for h in range(2):
+        glu[h, 0:reach, :] = edge_in[0, 0:reach, h * lanes : (h + 1) * lanes]
+        glu[h, reach + frames :, :] = edge_in[1, 0:reach, h * lanes : (h + 1) * lanes]
+    conv_step(0, 0)
+    conv_step(blocks - 1, 0)
+
+    own_count = jnp.clip(ends[-1] - first_frame, 0, frames).astype(F32)
+    own_mean = sums[0:1, :] / jnp.maximum(own_count, 1.0)
+    sums[0:1, :] = jnp.zeros((1, width), F32)
+
+    def spread_step(c, carry):
+        rows = rows_at(c, chunk)
+        valid = (first_frame + c * chunk + lax.broadcasted_iota(I32, (chunk, width), 0)) < ends[-1]
+        apart = jnp.where(valid, halves_of(conv, rows) - own_mean, 0.0)
+        sums[1:2, :] += jnp.sum(apart * apart, axis=0, keepdims=True)
+        return carry
+
+    lax.fori_loop(0, count, spread_step, 0)
+
+    def box_copies(call, stage):
+        group = peers if stage == 0 else far_peers
+        target = near_box if stage == 0 else far_box
+        base = 0 if stage == 0 else sp - 1
+        return [
+            pltpu.make_async_remote_copy(
+                src_ref=send_box.at[call, stage],
+                dst_ref=target.at[call, i],
+                send_sem=box_send.at[call, base + i],
+                recv_sem=box_recv.at[call, base + i],
+                device_id=peer,
+                device_id_type=MESH,
+            )
+            for i, peer in enumerate(group)
+        ]
+
+    def box_begin(call, stage, rows):
+        for i, row in enumerate(rows):
+            send_box[call, stage, i : i + 1, :] = row
+        for copy in box_copies(call, stage):
+            copy.start()
+
+    def box_end(call, stage, rows, merge):
+        target = near_box if stage == 0 else far_box
+        copies = box_copies(call, stage)
+        for copy in copies:
+            copy.wait()
+        return merge([rows] + [pick(target[call, i]) for i in range(len(copies))])
+
+    stats = (own_mean, sums[1:2, :], jnp.full((1, width), 1.0, F32) * own_count)
+    sums[1:2, :] = jnp.zeros((1, width), F32)
+    box_begin(0, 0, stats)
+    stats = box_end(0, 0, stats, combine)
+    box_begin(0, 1, stats)
+    mean, spread, frame_count = box_end(0, 1, stats, combine)
+    inv_std = lax.rsqrt(spread / frame_count + EPS)
+    norm_gain, norm_bias = row_of(bn_gain), row_of(bn_bias)
+
+    def heart_step(c, carry):
+        rows = rows_at(c, chunk)
+        normed = (halves_of(conv, rows) - mean) * inv_std
+        y = normed * norm_gain + norm_bias
+        sig_y = sigmoid(y)
+        w = (y * sig_y).astype(BF16)
+        swish[rows, :] = w
+        x3 = x2_ref[rows, :] + dg(w, w_point2[...], 1, 0)
+        hat4, inv4 = norm_parts(x3)
+        g4 = row_of(gain4)
+        n4 = (hat4 * g4).astype(BF16)
+        n4_keep[rows, :] = n4
+        a = dg(n4, w_in[...], 1, 0)
+        sig = sigmoid(a)
+        s = (a * sig).astype(BF16)
+        act[rows, :] = s
+        x4 = x3 + 0.5 * dg(s, w_down[...], 1, 0)
+        hat5, inv5 = norm_parts(x4)
+        g5 = row_of(gain5)
+        out_ref[rows, :] = (hat5 * g5).astype(BF16)
+        top = cot[rows, :].astype(F32)
+        small[4:5, :] += jnp.sum(top * hat5, axis=0, keepdims=True)
+        grad_x4 = norm_back(top, hat5, inv5, g5)
+        low_grad = (0.5 * grad_x4).astype(BF16)
+        branch[rows, :] = low_grad
+        grad = dg(low_grad, w_down[...], 1, 1)
+        low_hidden = (grad * (sig * (1.0 + a * (1.0 - sig)))).astype(BF16)
+        hidden[rows, :] = low_hidden
+        grad = dg(low_hidden, w_in[...], 1, 1)
+        small[3:4, :] += jnp.sum(grad * hat4, axis=0, keepdims=True)
+        grad3 = grad_x4 + norm_back(grad, hat4, inv4, g4)
+        grad_x3[rows, :] = grad3
+        low_grad = grad3.astype(BF16)
+        branch2[rows, :] = low_grad
+        grad = dg(low_grad, w_point2[...], 1, 1) * (sig_y * (1.0 + y * (1.0 - sig_y)))
+        grad_y[0, rows, :] = grad[:, :lanes]
+        grad_y[1, rows, :] = grad[:, lanes:]
+        sums[2:3, :] += jnp.sum(grad, axis=0, keepdims=True)
+        sums[3:4, :] += jnp.sum(grad * normed, axis=0, keepdims=True)
+        return carry
+
+    small[...] = jnp.zeros_like(small)
+    lax.fori_loop(0, count, heart_step, 0)
+
+    pair = (sums[2:3, :], sums[3:4, :], jnp.zeros((1, width), F32))
+    box_begin(1, 0, pair)
+    for side, rows in ((0, slice(0, reach)), (1, slice(frames - reach, frames))):
+        for h in range(2):
+            cols = slice(h * lanes, (h + 1) * lanes)
+            edge_out[side, reach : 2 * reach, cols] = grad_y[h, rows, :]
+            edge_out[side, 2 * reach : 3 * reach, cols] = conv[h, rows, :]
+    grad_rims = (
+        [edge_out.at[0, reach : 3 * reach, :], edge_out.at[1, reach : 3 * reach, :]],
+        [edge_in.at[0, reach : 3 * reach, :], edge_in.at[1, reach : 3 * reach, :]],
+    )
+    swap_rims(1, *grad_rims)
+    unit = 4 * width
+    for j in range(4):
+        cols = slice(j * width, (j + 1) * width)
+        mid[unit + j * width : unit + (j + 1) * width, :] = dg(act[:, cols], branch[...], 0, 0)
+    pair = box_end(1, 0, pair, total)
+    box_begin(1, 1, pair)
+    for j in range(4):
+        cols = slice(j * width, (j + 1) * width)
+        mid[j * width : (j + 1) * width, :] = dg(n4_keep[...], hidden[:, cols], 0, 0)
+    mid[2 * unit + 2 * width : 2 * unit + 3 * width, :] = dg(swish[...], branch2[...], 0, 0)
+    await_rims(1, *grad_rims)
+    bias_sum, gain_sum, _ = box_end(1, 1, pair, total)
+    bn_grads[0:1, :] = gain_sum
+    bn_grads[1:2, :] = bias_sum
+    bn_grads[2:8, :] = jnp.zeros((6, width), F32)
+
+    scale = norm_gain * inv_std
+    slope = -inv_std * inv_std * norm_gain * gain_sum / frame_count
+    shift_all = -inv_std * norm_gain * bias_sum / frame_count
+
+    def conv_grad(grad, value, frame, h):
+        cols = slice(h * lanes, (h + 1) * lanes)
+        extra = (value - mean[:, cols]) * slope[:, cols] + shift_all[:, cols]
+        return grad * scale[:, cols] + jnp.where(frame < ends[-1], extra, 0.0)
+
+    def grad_conv_step(c, carry):
+        rows = rows_at(c, chunk)
+        frame = first_frame + c * chunk + lax.broadcasted_iota(I32, (chunk, lanes), 0)
+        where = pl.ds(pl.multiple_of(reach + c * chunk, 8), chunk)
+        for h in range(2):
+            grad_conv[h, where, :] = conv_grad(grad_y[h, rows, :], conv[h, rows, :], frame, h)
+        return carry
+
+    lax.fori_loop(0, count, grad_conv_step, 0)
+    for side, rows, begin_frame in (
+        (0, slice(0, reach), first_frame - reach),
+        (1, slice(reach + frames, 2 * reach + frames), first_frame + frames),
+    ):
+        frame = begin_frame + lax.broadcasted_iota(I32, (reach, lanes), 0)
+        for h in range(2):
+            cols = slice(h * lanes, (h + 1) * lanes)
+            grad_conv[h, rows, :] = conv_grad(
+                edge_in[side, reach : 2 * reach, cols], edge_in[side, 2 * reach : 3 * reach, cols], frame, h
+            )
+
+    def conv_back_step(b, carry):
+        low, high = low_lim[rows_at(b, block), :], high_lim[rows_at(b, block), :]
+        start = pl.multiple_of(b * block, block)
+        result = [zero, zero]
+        here = [glu[h, pl.ds(pl.multiple_of(reach + start, 8), block), :] for h in range(2)]
+        for tap in range(taps):
+            shift = reach - tap
+            inside = (low <= shift) if shift < 0 else (high >= shift)
+            at = reach + shift
+            for h in range(2):
+                view = grad_conv.at[h, pl.ds(start, block + 2 * reach), :]
+                term = jnp.where(inside, view[at : at + block, :], 0.0)
+                result[h] = result[h] + depthwise[tap : tap + 1, h * lanes : (h + 1) * lanes].astype(F32) * term
+                tap_sums[tap, h] += jnp.sum((here[h] * term).reshape(block // 8, 8, lanes), axis=0)
+        for h in range(2):
+            grad_glu[h, rows_at(b, block), :] = result[h]
+        return carry
+
+    lax.fori_loop(0, blocks, conv_back_step, 0)
+
+    def back_moves(c):
+        return moves(c, back_parts, heads, back_send, back_recv, back_local)
+
+    def close_step(c, carry):
+        rows = rows_at(c, chunk)
+        grad = halves_of(grad_glu, rows)
+        value, gate = point[rows, :width], sigmoid(point[rows, width:])
+        low_grad = jnp.concatenate([grad * gate, grad * value * gate * (1.0 - gate)], axis=1).astype(BF16)
+        grad_point[rows, :] = low_grad
+        grad = dg(low_grad, w_point1[...], 1, 1)
+        hat, inv = norm_parts(x2_ref[rows, :])
+        small[2:3, :] += jnp.sum(grad * hat, axis=0, keepdims=True)
+        grad2 = grad_x3[rows, :] + norm_back(grad, hat, inv, row_of(gain3))
+        grad_x2[rows, :] = grad2
+        low_grad = grad2.astype(BF16)
+        branch3[rows, :] = low_grad
+        back_parts[:, :, rows] = dg(w_out[...], low_grad, 1, 1).astype(BF16).reshape(sp, width // sp, chunk)
+        for copy in back_moves(c):
+            copy.start()
+        return carry
+
+    lax.fori_loop(0, count, close_step, 0)
+    for j in range(2):
+        mid[2 * unit + j * width : 2 * unit + (j + 1) * width, :] = dg(
+            n3_keep[...], grad_point[:, j * width : (j + 1) * width], 0, 0
+        )
+    mid[2 * unit + 3 * width : 3 * unit, :] = dg(ctx[...].reshape(width, frames), branch3[...], 1, 0)
+    for tap in range(taps):
+        for h in range(2):
+            small[8 + tap : 9 + tap, h * lanes : (h + 1) * lanes] = jnp.sum(tap_sums[tap, h], axis=0, keepdims=True)
+
+    def finish(c, carry):
+        for copy in back_moves(c):
+            copy.wait()
+        return carry
+
+    lax.fori_loop(0, count, finish, 0)
+
+
+def middle(
+    lengths, parts, x1, cot, gain3, gain4, gain5, w_out, w_point1, depthwise, bn_gain, bn_bias, w_point2,
+    w_in, w_down, dp,
+):
+    frames, width = x1.shape
+    sp = parts.shape[0]
+    wide = w_in.shape[1]
+    taps = depthwise.shape[0]
+    reach = taps // 2
+    chunk = min(256, frames)
+    count = frames // chunk
+    lanes = width // 2
+    keep, low_keep = pltpu.VMEM((frames, width), F32), pltpu.VMEM((frames, width), BF16)
+    split = pltpu.VMEM((2, frames, lanes), F32)
+    rimmed = pltpu.VMEM((2, frames + 2 * reach, lanes), F32)
+    rims = pltpu.VMEM((2, 3 * reach, width), F32)
+    moves = [DMA((sp - 1, count)), DMA((sp - 1, count)), DMA((count,))]
+    return pl.pallas_call(
+        functools.partial(middle_kernel, sp, dp, lengths.shape[1], taps, chunk, 32),
+        out_shape=[
+            jax.ShapeDtypeStruct((frames, width), BF16),
+            jax.ShapeDtypeStruct((frames, width), F32),
+            jax.ShapeDtypeStruct(parts.shape, BF16),
+            jax.ShapeDtypeStruct((12 * width, width), F32),
+            jax.ShapeDtypeStruct((64, width), F32),
+            jax.ShapeDtypeStruct((8, width), F32),
+        ],
+        in_specs=[SMEM, pl.BlockSpec(memory_space=pl.ANY)] + [VMEM] * 13,
+        out_specs=[VMEM] * 6,
+        scratch_shapes=[
+            pltpu.VMEM(parts.shape, BF16),
+            keep,
+            low_keep,
+            pltpu.VMEM((frames, 2 * width), F32),
+            rimmed,
+            split,
+            pltpu.VMEM((frames, lanes), I32),
+            pltpu.VMEM((frames, lanes), I32),
+            pltpu.VMEM((frames, wide), BF16),
+            pltpu.VMEM((frames, wide), BF16),
+            low_keep,
+            low_keep,
+            low_keep,
+            low_keep,
+            keep,
+            split,
+            rimmed,
+            split,
+            pltpu.VMEM((frames, 2 * width), BF16),
+            low_keep,
+            pltpu.VMEM(parts.shape, BF16),
+            pltpu.VMEM((taps, 2, 8, lanes), F32),
+            rims,
+            rims,
+            pltpu.VMEM((2, 2, 8, width), F32),
+            pltpu.VMEM((2, sp - 1, 8, width), F32),
+            pltpu.VMEM((2, dp - 1, 8, width), F32),
+            pltpu.VMEM((8, width), F32),
+        ]
+        + moves
+        + moves
+        + [DMA((2, 2)), DMA((2, 2)), DMA((2, sp + dp - 2)), DMA((2, sp + dp - 2))],
+        compiler_params=pltpu.CompilerParams(
+            collective_id=1, has_side_effects=True, vmem_limit_bytes=VMEM_LIMIT
+        ),
+        name="middle",
+    )(
+        lengths, parts, x1, cot, gain3, gain4, gain5, w_out, w_point1, depthwise, bn_gain, bn_bias, w_point2,
+        w_in, w_down,
+    )
+
+
 def axis_bits():
     bits = []
     for axis in ("sp", "dp"):
@@ -541,11 +1004,11 @@
         grad = dg(joined[:, rows], w_qkv[...], 0, 0)
         hat, inv = norm_parts(x1_ref[rows, :])
         gains[1:2, :] += jnp.sum(grad * hat, axis=0, keepdims=True)
-        grad_x1 = grad_x2[rows, :] + norm_back(grad, hat, inv, gain2[...].astype(F32))
+        grad_x1 = grad_x2[rows, :] + norm_back(grad, hat, inv, row_of(gain2))
         low_grad = (0.5 * grad_x1).astype(BF16)
         branch[rows, :] = low_grad
         hat, inv = norm_parts(tok[rows, :].astype(F32))
-        gain = gain1[...].astype(F32)
+        gain = row_of(gain1)
         n1 = (hat * gain).astype(BF16)
         n1_keep[rows, :] = n1
         a = dg(n1, w_in[...], 1, 0)
@@ -666,244 +1129,37 @@
     )(full)
 
 
-def exchange_kernel(sp, parts, heads, send, recv, local):
-    me = lax.axis_index("sp")
-    peers = sp_peers(sp)
-    greet(peers)
-    copies = [
-        pltpu.make_async_remote_copy(
-            src_ref=parts.at[peer[1]],
-            dst_ref=heads.at[me],
-            send_sem=send.at[i],
-            recv_sem=recv.at[i],
-            device_id=peer,
-            device_id_type=MESH,
-        )
-        for i, peer in enumerate(peers)
-    ]
-    for copy in copies:
-        copy.start()
-    own = pltpu.make_async_copy(parts.at[me], heads.at[me], local)
-    own.start()
-    own.wait()
-    for copy in copies:
-        copy.wait()
-
-
-def exchange(parts, call):
-    sp = parts.shape[0]
-    anywhere = pl.BlockSpec(memory_space=pl.ANY)
-    return pl.pallas_call(
-        functools.partial(exchange_kernel, sp),
-        out_shape=jax.ShapeDtypeStruct(parts.shape, parts.dtype),
-        in_specs=[anywhere],
-        out_specs=anywhere,
-        scratch_shapes=[DMA((sp - 1,)), DMA((sp - 1,)), DMA],
-        compiler_params=pltpu.CompilerParams(collective_id=call, has_side_effects=True),
-        name="exchange",
-    )(parts)
-
-
-def gather_kernel(sp, dp, x_ref, all_ref, send, recv):
-    me_d, me_s = lax.axis_index("dp"), lax.axis_index("sp")
-    total = sp * dp
-    me = me_d * sp + me_s
-    peers = []
-    for step in range(1, total):
-        peer = lax.rem(me + step, total)
-        peers.append((peer // sp, lax.rem(peer, sp)))
-    greet(peers)
-    copies = [
-        pltpu.make_async_remote_copy(
-            src_ref=x_ref,
-            dst_ref=all_ref.at[i + 1],
-            send_sem=send.at[i],
-            recv_sem=recv.at[i],
-            device_id=peer,
-            device_id_type=MESH,
-        )
-        for i, peer in enumerate(peers)
-    ]
-    for copy in copies:
-        copy.start()
-    all_ref[0] = x_ref[...]
-    for copy in copies:
-        copy.wait()
-
-
-def gather_all(x, sp, dp, call):
-    total = sp * dp
-    return pl.pallas_call(
-        functools.partial(gather_kernel, sp, dp),
-        out_shape=jax.ShapeDtypeStruct((total,) + x.shape, x.dtype),
-        in_specs=[VMEM],
-        out_specs=VMEM,
-        scratch_shapes=[DMA((total - 1,)), DMA((total - 1,))],
-        compiler_params=pltpu.CompilerParams(collective_id=call, has_side_effects=True),
-        name="gather_all",
-    )(x)
-
-
-def with_halo(block, width):
-    count = lax.axis_size("sp")
-    forward = [(i, i + 1) for i in range(count - 1)]
-    backward = [(target, source) for source, target in forward]
-    low = lax.ppermute(block[-width:], "sp", forward)
-    high = lax.ppermute(block[:width], "sp", backward)
-    return jnp.concatenate([low, block, high], axis=0)
-
-
-def layer_norm(rows, gain):
-    centre = rows - jnp.mean(rows, axis=-1, keepdims=True)
-    spread = jnp.mean(centre * centre, axis=-1, keepdims=True)
-    return centre * lax.rsqrt(spread + EPS) * gain
-
-
-def segment_of(index, item_ends):
-    return jnp.sum((index[:, None] >= item_ends[None, :]).astype(jnp.int32), axis=1)
-
-
-def gated_unit(joined):
-    half = joined.shape[1] // 2
-    return joined[:, :half] * jax.nn.sigmoid(joined[:, half:])
-
-
-def feed_forward(rows, gain, w_in, w_out):
-    normed, back = jax.vjp(layer_norm, rows, gain)
-    normed_low = normed.astype(BF16)
-    hidden = dg(normed_low, w_in, 1, 0)
-    activated, act_back = jax.vjp(jax.nn.silu, hidden)
-    act_low = activated.astype(BF16)
-    return rows + 0.5 * dg(act_low, w_out, 1, 0), (back, normed_low, act_low, act_back)
-
-
-def feed_back(grad_rows, kept, w_in, w_out):
-    back, normed_low, act_low, act_back = kept
-    grad_branch = (0.5 * grad_rows).astype(BF16)
-    grad_w_out = dg(act_low, grad_branch, 0, 0)
-    grad_act = dg(grad_branch, w_out, 1, 1)
-    grad_hidden = act_back(grad_act)[0].astype(BF16)
-    grad_w_in = dg(normed_low, grad_hidden, 0, 0)
-    grad_normed = dg(grad_hidden, w_in, 1, 1)
-    grad_input, grad_gain = back(grad_normed)
-    return grad_rows + grad_input, grad_gain, grad_w_in, grad_w_out
-
-
 def on_device(
     tokens, ln1_gain, ffn1_in, ffn1_out, ln2_gain, w_qkv, w_out, ln3_gain, w_point1, depthwise,
     bn_gain, bn_bias, w_point2, ln4_gain, ffn2_in, ffn2_out, ln5_gain, lengths, cotangent,
 ):
-    frames, width = tokens.shape[1:]
+    width = tokens.shape[2]
     sp, dp = lax.axis_size("sp"), lax.axis_size("dp")
     assert HEADS == sp
     head_dim = width // HEADS
     half = head_dim // 2
-    items = lengths.shape[1]
     taps = depthwise.shape[0]
-    reach = taps // 2
-    offset = lax.axis_index("sp") * frames
-    item_ends = jnp.cumsum(lengths[0])
-    local_segment = segment_of(offset + jnp.arange(frames, dtype=I32), item_ends)
-    rim_segment = segment_of(offset - reach + jnp.arange(frames + 2 * reach, dtype=I32), item_ends)
-    valid_rows = (local_segment < items).astype(F32)[:, None]
-    tap_masks = [
-        (rim_segment[j : j + frames] == local_segment).astype(F32)[:, None] for j in range(taps + 1)
-    ]
-    gain_one, gain_two, gain_three, gain_four, gain_five = (
-        g.astype(F32) for g in (ln1_gain, ln2_gain, ln3_gain, ln4_gain, ln5_gain)
-    )
-    norm_gain, norm_bias, kernel = (g.astype(F32) for g in (bn_gain, bn_bias, depthwise))
     turns = 10000.0 ** (-np.arange(half, dtype=np.float64) / half) / (2 * np.pi)
     high = np.round(turns * 4096.0) / 4096.0
     freq = jnp.asarray(np.stack([high, turns - high], axis=1), F32)
     qkv_rows = w_qkv.T.reshape(3, HEADS, head_dim, width).transpose(1, 0, 2, 3).reshape(3 * width, width)
-
-    after_first, attn_low, trig, heads = front(
-        lengths, tokens[0], ln1_gain[None], ffn1_in, ffn1_out, ln2_gain[None], qkv_rows, freq, sp
+    x1, n2, trig, heads = front(
+        lengths, tokens[0], ln1_gain, ffn1_in, ffn1_out, ln2_gain, qkv_rows, freq, sp
     )
     context, raw_context, log_sums = attend(heads, lengths)
-    context = exchange(context, 1).reshape(width, frames)
-    after_attn = after_first + dg(context, w_out, 0, 0)
-    conv_normed, conv_norm_back = jax.vjp(layer_norm, after_attn, gain_three)
-    conv_low = conv_normed.astype(BF16)
-    point_out = dg(conv_low, w_point1, 1, 0)
-    gated_rows, gated_back = jax.vjp(gated_unit, point_out)
-    rim_gated = with_halo(gated_rows.astype(BF16), reach).astype(F32)
-    conv_out = jnp.zeros((frames, width), F32)
-    for tap in range(taps):
-        conv_out = conv_out + kernel[tap][None, :] * rim_gated[tap : tap + frames] * tap_masks[tap]
-    own_count = jnp.sum(valid_rows)
-    own_mean = jnp.sum(valid_rows * conv_out, axis=0) / jnp.maximum(own_count, 1.0)
-    own_spread = jnp.sum(valid_rows * (conv_out - own_mean) ** 2, axis=0)
-    rows = jnp.stack([own_mean, own_spread, jnp.broadcast_to(own_count, (width,))])
-    every = gather_all(jnp.concatenate([rows, jnp.zeros((5, width), F32)]), sp, dp, 2)
-    counts = every[:, 2]
-    frame_count = jnp.sum(counts, axis=0)
-    bn_mean = jnp.sum(counts * every[:, 0], axis=0) / frame_count
-    variance = (
-        jnp.sum(every[:, 1], axis=0) + jnp.sum(counts * (every[:, 0] - bn_mean) ** 2, axis=0)
-    ) / frame_count
-    centered = conv_out - bn_mean
-    inv_std = lax.rsqrt(variance + EPS)
-    normed = centered * inv_std
-    swished, swish_back = jax.vjp(jax.nn.silu, normed * norm_gain + norm_bias)
-    swish_low = swished.astype(BF16)
-    after_conv = after_attn + dg(swish_low, w_point2, 1, 0)
-    after_second, second_kept = feed_forward(after_conv, gain_four, ffn2_in, ffn2_out)
-    output, final_back = jax.vjp(layer_norm, after_second, gain_five)
-    grad_second, grad_gain_five = final_back(cotangent[0].astype(F32))
-    grad_conv_rows, grad_gain_four, grad_in_two, grad_out_two = feed_back(
-        grad_second, second_kept, ffn2_in, ffn2_out
+    output, grad_x2, grad_context, mid, small, bn_grads = middle(
+        lengths, context, x1, cotangent[0], ln3_gain, ln4_gain, ln5_gain, w_out, w_point1, depthwise,
+        bn_gain, bn_bias, w_point2, ffn2_in, ffn2_out, dp,
     )
-    grad_branch = grad_conv_rows.astype(BF16)
-    grad_point_two = dg(swish_low, grad_branch, 0, 0)
-    grad_norm_out = swish_back(dg(grad_branch, w_point2, 1, 1))[0]
-    sums = jnp.stack([jnp.sum(grad_norm_out, axis=0), jnp.sum(grad_norm_out * normed, axis=0)])
-    every = gather_all(jnp.concatenate([sums, jnp.zeros((6, width), F32)]), sp, dp, 3)
-    grad_norm_bias, grad_norm_gain = jnp.sum(every[:, 0], axis=0), jnp.sum(every[:, 1], axis=0)
-    grad_variance = -0.5 * inv_std * inv_std * norm_gain * grad_norm_gain
-    grad_mean = -inv_std * norm_gain * grad_norm_bias
-    grad_conv = (
-        grad_norm_out * norm_gain * inv_std
-        + valid_rows * (2.0 * centered * grad_variance + grad_mean) / frame_count
-    )
-    rim_grad = with_halo(grad_conv.astype(BF16), reach).astype(F32)
-    grad_gated = jnp.zeros((frames, width), F32)
-    for tap in range(taps):
-        mirror = 2 * reach - tap
-        grad_gated = (
-            grad_gated + kernel[tap][None, :] * rim_grad[mirror : mirror + frames] * tap_masks[mirror]
-        )
-    grad_kernel = jnp.stack(
-        [jnp.sum(grad_conv * rim_gated[j : j + frames] * tap_masks[j], axis=0) for j in range(taps)]
-    )
-    grad_point_out = gated_back(grad_gated)[0].astype(BF16)
-    grad_point_one = dg(conv_low, grad_point_out, 0, 0)
-    grad_conv_input, grad_gain_three = conv_norm_back(dg(grad_point_out, w_point1, 1, 1))
-    grad_attn_rows = grad_conv_rows + grad_conv_input
-    grad_attn_out = grad_attn_rows.astype(BF16)
-    grad_out_weight = dg(context, grad_attn_out, 1, 0)
-    grad_context = dg(w_out, grad_attn_out, 1, 1).astype(BF16).reshape(sp, head_dim, frames)
-    grad_heads = attend_back(heads, lengths, raw_context, log_sums, exchange(grad_context, 4))
-    def blocks(matrix):
-        return [matrix[:, k : k + width] for k in range(0, matrix.shape[1], width)]
-
-    mid = jnp.concatenate(
-        blocks(grad_in_two) + [grad_out_two] + blocks(grad_point_one) + [grad_point_two, grad_out_weight]
-    )
-    zero = jnp.zeros((1, width), F32)
-    small = jnp.concatenate(
-        [zero, zero, grad_gain_three[None], grad_gain_four[None], grad_gain_five[None], zero, zero, zero]
-        + [grad_kernel, jnp.zeros((56 - taps, width), F32)]
-    )
-    grad_start, full = back(
-        grad_heads, trig, tokens[0], after_first, attn_low, grad_attn_rows, ln1_gain[None], ln2_gain[None],
-        ffn1_in, ffn1_out, qkv_rows, mid, small,
+    grad_heads = attend_back(heads, lengths, raw_context, log_sums, grad_context)
+    input_grad, full = back(
+        grad_heads, trig, tokens[0], x1, n2, grad_x2, ln1_gain, ln2_gain, ffn1_in, ffn1_out, qkv_rows,
+        mid, small,
     )
     in_two, out_two, point_one, point_two, out_weight, qkv, in_one, out_one, small = unpack(full)
     return (
-        output[None].astype(BF16), grad_start[None], small[0], in_one, out_one, small[1], qkv, out_weight,
-        small[2], point_one, small[8 : 8 + taps], grad_norm_gain, grad_norm_bias, point_two, small[3],
+        output[None], input_grad[None], small[0], in_one, out_one, small[1], qkv, out_weight,
+        small[2], point_one, small[8 : 8 + taps], bn_grads[0], bn_grads[1], point_two, small[3],
         in_two, out_two, small[4],
     )
 

time: 332 us -> 262 us (0.79)
  other arithmetic: 39.9 us -> 0 us
  matrix products: 16.5 us -> 0 us
  local copies, waits for them, and re-layouts: 21.8 us -> 7.74 us
  Pallas kernels: 241 us -> 253 us
  starting transfers between devices: 7.02 us -> 0 us
    reduce_sum x20 -> x0, other arithmetic: 24.9 us -> none  [the longest x4 8.76 us: on_device(): jnp.sum(grad_conv * rim_gated[j:j + frames] * tap_masks[j], axis=0)]
    dot_general x15 -> x0, matrix products: 16.5 us -> none  [dg(): lax.dot_general(left, right, (((left_dim,), (right_dim,)), ((), ())), pre...]
    pallas_call x4 -> x1, Pallas kernels: 44.5 us -> 58.7 us  [middle(): pl.pallas_call(functools.partial(middle_kernel, sp, dp, lengths.shape[1],...]
    mul x3 -> x0, other arithmetic: 8.08 us -> none  [the longest x2 8.07 us: gated_unit(): return joined[:, :half] * jax.nn.sigmoid(joined[:, half:])]
    ppermute x4 -> x0, starting transfers between devices: 7.02 us -> none  [the longest x2 4.44 us: with_halo(): low = lax.ppermute(block[-width:], 'sp', forward)]
    unnamed x182 -> x7, local copies, waits for them, and re-layouts: 9.24 us -> 2.76 us
    concatenate x6 -> x0, local copies, waits for them, and re-layouts: 5.14 us -> none  [the longest x3 3.7 us: on_device(): jnp.concatenate([zero, zero, grad_gain_three[None], grad_gain_four[None],...]
    convert_element_type x10 -> x0, other arithmetic: 4.76 us -> none  [the longest x5 2.26 us: on_device(): g.astype(F32)]
  transfers between devices with their start and end apart: 4 -> 0, of which waited for: 1 -> 0; matrix products, arithmetic and copies ran while one was open for 3% -> 0% of each run, Pallas kernels for 0% -> 0%
where the time goes in v3:
time: 262 us; the launch traced here: 261 us
  Pallas kernels  253 us (97%)
  local copies, waits for them, and re-layouts  7.74 us (3%)
    pallas_call x1, Pallas kernels, back(): pl.pallas_call(functools.partial(back_kernel, sp, chunk), out_shape=[jax....  88.8 us
    pallas_call x1, Pallas kernels, middle(): pl.pallas_call(functools.partial(middle_kernel, sp, dp, lengths.shape[1],...  58.7 us
    pallas_call x1, Pallas kernels, attend_back(): pl.pallas_call(functools.partial(bwd_kernel, lengths.shape[1], bq, bk), o...  45.8 us
    pallas_call x1, Pallas kernels, attend(): pl.pallas_call(functools.partial(fwd_kernel, lengths.shape[1], min(bq, fr...  29.4 us
    pallas_call x1, Pallas kernels, front(): pl.pallas_call(functools.partial(front_kernel, sp, lengths.shape[1], chun...  25.2 us

profile of v3, /device:TPU:0, one launch (start us, length us, event | category | flops | bytes accessed | tf_op | source)
XLA Modules:
  0.0 261.1 jit_solution(14456530530564008457)
XLA Ops:
  0.7 1.2 copy.39
  1.8 0.8 copy.40
  2.6 25.2 %front.1 = (f32[1024,256]{1,0:T(8,128)}, bf16[1024,256]{1,0:T(8,128)(2,1)}, f32[64,1024]{1,0:T(8,128)}, bf16[4,192,1024]{2,1,0:T(8,128)(2,1)}) custom-call(s32[1,4]{1,0:T(1,128)} %len_ref.7, bf16[1024,256]{1,0:T(8,128)(2,1)} %bitcast.19, bf16[256]{0:T(256)(128)(2,1)} %gain1.3, bf16[256,1024]{1,0:T(8,128)(2,1)} %w_in.5, bf16[1024,256]{1,0:T(8,128)(2,1)} %w_out.5, ...), custom_call_target="tpu_custom_call" | custom-call | tf_op jit(solution)/shard_map/front/pallas_call | solution.py:196
  27.9 29.4 %attend.1 = (bf16[4,64,1024]{2,1,0:T(8,128)(2,1)}, f32[4,64,1024]{2,1,0:T(8,128)}, f32[1,4096]{1,0:T(1,128)}) custom-call(s32[1,4]{1,0:T(1,128)} %len_ref.7, bf16[4,192,1024]{2,1,0:T(8,128)(2,1)} %get-tuple-element.42.x_ref), custom_call_target="tpu_custom_call" | custom-call | tf_op jit(solution)/shard_map/attend/pallas_call | solution.py:261
  57.2 58.7 %middle.1 = (bf16[1024,256]{1,0:T(8,128)(2,1)}, f32[1024,256]{1,0:T(8,128)}, bf16[4,64,1024]{2,1,0:T(8,128)(2,1)}, f32[3072,256]{1,0:T(8,128)}, f32[64,256]{1,0:T(8,128)}, /*index=5*/f32[8,256]{1,0:T(8,128)}) custom-call(s32[1,4]{1,0:T(1,128)} %len_ref.7, bf16[4,64,1024]{2,1,0:T(8,128)(2,1)} %get-tuple-element.43.parts, ...), custom_call_target="tpu_custom_call" | custom-call | tf_op jit(solution)/shard_map/middle/pallas_call | solution.py:740
  116.0 45.8 %attend_back.1.parts = bf16[4,192,1024]{2,1,0:T(8,128)(2,1)} custom-call(s32[1,4]{1,0:T(1,128)} %len_ref.7, bf16[4,192,1024]{2,1,0:T(8,128)(2,1)} %get-tuple-element.42.x_ref, f32[4,64,1024]{2,1,0:T(8,128)} %get-tuple-element.46.o_ref, f32[1,4096]{1,0:T(1,128)} %get-tuple-element.47.lse_ref, bf16[4,64,1024]{2,1,0:T(8,128)(2,1)} %get-tuple-element.48.do_ref), custom_call_target="tpu_custom_call" | custom-call | tf_op jit(solution)/shard_map/attend_back/pallas_call | solution.py:324
  161.7 88.8 %back.1 = (bf16[1024,256]{1,0:T(8,128)(2,1)}, bf16[6144,256]{1,0:T(8,128)(2,1)}) custom-call(bf16[4,192,1024]{2,1,0:T(8,128)(2,1)} %attend_back.1.parts, f32[64,1024]{1,0:T(8,128)} %get-tuple-element.49.trig, bf16[1024,256]{1,0:T(8,128)(2,1)} %bitcast.20, f32[1024,256]{1,0:T(8,128)} %get-tuple-element.44.x1_ref, bf16[1024,256]{1,0:T(8,128)(2,1)} %get-tuple-element.50.n2_ref, ...), custom_call_target="tpu_custom_call" | custom-call | tf_op jit(solution)/shard_map/back/pallas_call | solution.py:1055
  250.6 0.0 copy-start
  250.6 0.0 copy-start.1
  250.6 1.4 fusion.1
  252.0 4.7 %unpack.1 = (f32[256,1024]{1,0:T(8,128)}, f32[1024,256]{1,0:T(8,128)}, f32[256,512]{1,0:T(8,128)}, f32[256,256]{1,0:T(8,128)}, f32[256,256]{1,0:T(8,128)}, /*ind...) custom-call(bf16[6144,256]{1,0:T(8,128)(2,1)} %get-tuple-element.55.full), custom_call_target="tpu_custom_call" | custom-call | tf_op jit(solution)/shard_map/unpack/pallas_call | solution.py:1122
  256.7 1.5 fusion
  258.1 1.4 slice.27
  259.5 0.0 copy-done
  259.5 0.8 copy.43
  260.3 0.0 copy-done.1
  260.3 0.8 copy.44
Async XLA Ops:
  250.6 8.9 %copy-start = (bf16[1024,256]{1,0:T(8,128)(2,1)S(1)}, bf16[1024,256]{1,0:T(8,128)(2,1)}, u32[]{:S(2)}) copy-start(bf16[1024,256]{1,0:T(8,128)(2,1)} %get-tuple-element.45) | copy-start | bytes 1572868
  250.6 9.7 %copy-start.1 = (bf16[1024,256]{1,0:T(8,128)(2,1)S(1)}, bf16[1024,256]{1,0:T(8,128)(2,1)}, u32[]{:S(2)}) copy-start(bf16[1024,256]{1,0:T(8,128)(2,1)} %get-tuple-element.54) | copy-start | bytes 1572868

commit v4 on v3

v4 whole, which is shorter than its diff:
```python
import functools

import jax
import jax.numpy as jnp
import numpy as np
from jax import lax
from jax.experimental import pallas as pl
from jax.experimental.pallas import tpu as pltpu
from jax.sharding import PartitionSpec as P

HEADS = 4
EPS = 1e-05
NEG = -1e30
LN2 = float(np.log(2.0))
F32 = jnp.float32
BF16 = jnp.bfloat16
I32 = jnp.int32
MESH = pl.DeviceIdType.MESH
VMEM = pl.BlockSpec(memory_space=pltpu.VMEM)
SMEM = pl.BlockSpec(memory_space=pltpu.SMEM)
DMA = pltpu.SemaphoreType.DMA
VMEM_LIMIT = 56 * 2**20


def dg(left, right, left_dim, right_dim):
    return lax.dot_general(
        left, right, (((left_dim,), (right_dim,)), ((), ())), preferred_element_type=F32
    )


def rows_at(index, count):
    return pl.ds(pl.multiple_of(index * count, count), count)


def greet(devices):
    for device in devices:
        pl.semaphore_signal(pltpu.get_barrier_semaphore(), inc=1, device_id=device, device_id_type=MESH)


def await_greetings(devices):
    pl.semaphore_wait(pltpu.get_barrier_semaphore(), len(devices))


def flipped(axis, mask):
    me, step = lax.axis_index(axis), 1
    out = me
    while step <= mask:
        if mask & step:
            out = out + step - 2 * step * lax.rem(me // step, 2)
        step *= 2
    return out


def peer_at(sp_mask, dp_mask):
    return (flipped("dp", dp_mask), flipped("sp", sp_mask))


def sp_peers(count):
    return [peer_at(mask, 0) for mask in range(1, count)]


def row_of(ref):
    return ref[...].astype(F32).reshape(1, ref.shape[0])


def frame_cols(device, frames, c, chunk):
    return pl.ds(pl.multiple_of(device * frames + c * chunk, chunk), chunk)


def ends_of(len_ref, items):
    ends, total = [], 0
    for item in range(items):
        total = total + len_ref[0, item]
        ends.append(total)
    return ends


def segment_row(first, count, ends):
    frame = first + lax.broadcasted_iota(I32, (1, count), 1)
    segment = jnp.zeros((1, count), I32)
    for end in ends:
        segment = segment + (frame >= end).astype(I32)
    return segment


def position_row(first, count, ends):
    frame = first + lax.broadcasted_iota(I32, (1, count), 1)
    start = jnp.zeros((1, count), I32)
    for end in ends:
        start = jnp.where(frame >= end, end, start)
    return (frame - start).astype(F32)


def block_bounds(first, count, ends, length):
    low, high = 0, length
    for end in ends:
        low = jnp.where(first >= end, end, low)
    for end in reversed(ends):
        high = jnp.where(first + count - 1 < end, end, high)
    return low, high


def onehot_rows(segment, items, other, same):
    row = lax.broadcasted_iota(I32, (16, segment.shape[1]), 0)
    return jnp.where(row <= items, jnp.where(row == segment, same, other), 0.0)


def norm_parts(rows):
    centre = rows - jnp.mean(rows, axis=-1, keepdims=True)
    inv = lax.rsqrt(jnp.mean(centre * centre, axis=-1, keepdims=True) + EPS)
    return centre * inv, inv


def norm_back(grad, hat, inv, gain):
    scaled = grad * gain
    first = jnp.mean(scaled, axis=-1, keepdims=True)
    second = jnp.mean(scaled * hat, axis=-1, keepdims=True)
    return inv * (scaled - first - hat * second)


def sigmoid(x):
    return 1.0 / (1.0 + jnp.exp(-x))


def sine_cosine(position, freq_hi, freq_lo):
    turns = position * freq_hi
    turns = turns - jnp.round(turns) + position * freq_lo
    turns = turns - jnp.round(turns)
    x = turns * float(np.pi)
    x2 = x * x
    s = x * (1 + x2 * (-1 / 6 + x2 * (1 / 120 + x2 * (-1 / 5040 + x2 * (1 / 362880 - x2 / 39916800)))))
    c = 1 + x2 * (-1 / 2 + x2 * (1 / 24 + x2 * (-1 / 720 + x2 * (1 / 40320 + x2 * (-1 / 3628800 + x2 / 479001600)))))
    return 2 * s * c, 1 - 2 * s * s


def front_kernel(
    sp, items, chunk, len_ref, tok, gain1, w_in, w_out, gain2, w_qkv, freq,
    x1_ref, n2_ref, trig, heads, parts, turned, send, recv, local,
):
    me = lax.axis_index("sp")
    frames = tok.shape[0]
    width = tok.shape[1]
    half = trig.shape[0] // 2
    peers = sp_peers(sp)
    greet(peers)
    turned[...] = w_qkv[...].T
    ends = ends_of(len_ref, items)
    scale = float(np.log2(np.e)) * (2 * half) ** -0.5

    def copies(c):
        cols = rows_at(c, chunk)
        out = [
            pltpu.make_async_remote_copy(
                src_ref=parts.at[peer[1], :, cols],
                dst_ref=heads.at[:, frame_cols(me, frames, c, chunk)],
                send_sem=send.at[i, c],
                recv_sem=recv.at[i, c],
                device_id=peer,
                device_id_type=MESH,
            )
            for i, peer in enumerate(peers)
        ]
        own = pltpu.make_async_copy(
            parts.at[me, :, cols], heads.at[:, frame_cols(me, frames, c, chunk)], local.at[c]
        )
        return out, own

    def step(c, carry):
        rows = rows_at(c, chunk)
        x = tok[rows, :].astype(F32)
        hat, _ = norm_parts(x)
        n1 = (hat * row_of(gain1)).astype(BF16)
        a = dg(n1, w_in[...], 1, 0)
        s = (a * sigmoid(a)).astype(BF16)
        x1 = x + 0.5 * dg(s, w_out[...], 1, 0)
        x1_ref[rows, :] = x1
        hat, _ = norm_parts(x1)
        n2 = (hat * row_of(gain2)).astype(BF16)
        n2_ref[rows, :] = n2
        joined = dg(turned[...], n2, 1, 1)
        sine, cosine = sine_cosine(
            position_row(me * frames + c * chunk, chunk, ends), freq[:, 0:1], freq[:, 1:2]
        )
        trig[0:half, rows] = sine
        trig[half:, rows] = cosine
        for head in range(sp):
            base = head * 2 * half
            for part, factor in ((0, scale), (1, 1.0)):
                low = part * width + base
                first, second = joined[low : low + half], joined[low + half : low + 2 * half]
                low = part * 2 * half
                parts[head, low : low + half, rows] = ((first * cosine - second * sine) * factor).astype(BF16)
                parts[head, low + half : low + 2 * half, rows] = (
                    (first * sine + second * cosine) * factor
                ).astype(BF16)
            low = 2 * width + base
            parts[head, 4 * half : 6 * half, rows] = joined[low : low + 2 * half].astype(BF16)

        @pl.when(c == 0)
        def _():
            await_greetings(peers)

        out, own = copies(c)
        for copy in out:
            copy.start()
        own.start()
        return carry

    lax.fori_loop(0, frames // chunk, step, 0)

    def finish(c, carry):
        out, own = copies(c)
        for copy in out:
            copy.wait()
        own.wait()
        return carry

    lax.fori_loop(0, frames // chunk, finish, 0)


def front(lengths, tok, gain1, w_in, w_out, gain2, w_qkv, freq, sp):
    frames, width = tok.shape
    chunk = min(256, frames)
    count = frames // chunk
    head_width = w_qkv.shape[1] // sp
    half = freq.shape[0]
    return pl.pallas_call(
        functools.partial(front_kernel, sp, lengths.shape[1], chunk),
        out_shape=[
            jax.ShapeDtypeStruct((frames, width), F32),
            jax.ShapeDtypeStruct((frames, width), BF16),
            jax.ShapeDtypeStruct((2 * half, frames), F32),
            jax.ShapeDtypeStruct((head_width, sp * frames), BF16),
        ],
        in_specs=[SMEM] + [VMEM] * 7,
        out_specs=[VMEM] * 4,
        scratch_shapes=[
            pltpu.VMEM((sp, head_width, frames), BF16),
            pltpu.VMEM((3 * width, width), BF16),
            DMA((sp - 1, count)),
            DMA((sp - 1, count)),
            DMA((count,)),
        ],
        compiler_params=pltpu.CompilerParams(
            collective_id=0, has_side_effects=True, vmem_limit_bytes=VMEM_LIMIT
        ),
        name="front",
    )(lengths, tok, gain1, w_in, w_out, gain2, w_qkv, freq)


def split_rows(value):
    row = lax.broadcasted_iota(I32, (16, value.shape[1]), 0)
    first = value.astype(BF16).astype(F32)
    second = (value - first).astype(BF16).astype(F32)
    third = value - first - second
    picked = jnp.where(row == 0, first, jnp.where(row == 1, second, third))
    return jnp.where(row < 3, picked, 0.0).astype(BF16)


def first_rows(count, columns):
    row = lax.broadcasted_iota(I32, (16, columns), 0)
    return jnp.where(row < count, 1.0, 0.0).astype(BF16)


def in_pieces(low, high, sizes, body, carry):
    for size in sizes:
        pieces = (high - low) // size
        carry = lax.fori_loop(
            0, pieces, lambda i, c, low=low, size=size: body(pl.multiple_of(low + i * size, sizes[-1]), size, c), carry
        )
        low = low + pieces * size
    return carry


def over_blocks(len_ref, ends, items, length, outer, sizes, body):
    unit = sizes[-1]
    start, stop, longest = 0, ends[0], len_ref[0, 0]
    for item in range(1, items):
        more = len_ref[0, item] > longest
        start = jnp.where(more, ends[item - 1], start)
        stop = jnp.where(more, ends[item], stop)
        longest = jnp.where(more, len_ref[0, item], longest)
    start, stop = start // unit * unit, (stop + unit - 1) // unit * unit

    def part(index, carry):
        low = jnp.where(index == 0, 0, jnp.where(index == 1, start, stop))
        high = jnp.where(index == 0, start, jnp.where(index == 1, stop, length))

        def block(at, size, carry):
            first, last = block_bounds(at, size, ends, length)
            body(at, size, first // unit * unit, (last + unit - 1) // unit * unit)
            return carry

        return in_pieces(low, high, outer, block, carry)

    lax.fori_loop(0, 3, part, 0)


def attend_kernel(items, outer, sizes, len_ref, x_ref, ctx_ref, o_ref, lse_ref, qa, ka, va):
    dim, length = x_ref.shape[0] // 3, x_ref.shape[1]
    ends = ends_of(len_ref, items)
    frames = min(1024, length)
    pad = jnp.zeros((dim - 32, frames), BF16)
    for first in range(0, length, frames):
        cols = slice(first, first + frames)
        segment = segment_row(first, frames, ends)
        query, key = x_ref[0:dim, cols], x_ref[dim : 2 * dim, cols]
        own = jnp.sum(query.astype(F32) * key.astype(F32), axis=0, keepdims=True)
        lse_ref[:, cols] = own
        qa[0:dim, cols] = query
        qa[dim : dim + 16, cols] = onehot_rows(segment, items, 0.0, 1.0).astype(BF16)
        qa[dim + 16 : dim + 32, cols] = split_rows(-own)
        qa[dim + 32 :, cols] = pad
        ka[cols, :] = jnp.concatenate(
            [key, onehot_rows(segment, items, NEG, 0.0).astype(BF16), first_rows(3, frames), pad], axis=0
        ).T
        va[0:dim, cols] = x_ref[2 * dim :, cols]
        va[dim:, cols] = first_rows(1, frames)

    def block_step(start, block, low, high):
        where = pl.ds(start, block)
        query = qa[:, where]

        def piece(at, size, acc):
            powers = jnp.exp2(dg(ka[pl.ds(at, size), :], query, 1, 0)).astype(BF16)
            return acc + dg(va[:, pl.ds(at, size)], powers, 1, 0)

        def store(acc, shift):
            total = acc[dim : dim + 1, :]
            value = acc[0:dim, :] / total
            ctx_ref[:, where] = value.astype(BF16)
            o_ref[:, where] = value
            lse_ref[:, where] = shift + jnp.log2(total)

        acc = in_pieces(low, high, sizes, piece, jnp.zeros((dim + 16, block), F32))
        own = lse_ref[:, where]
        store(acc, own)
        fits = jnp.min(jnp.where(acc[dim : dim + 1, :] < 2.0**60, 1.0, 0.0)) > 0.5

        @pl.when(jnp.logical_not(fits))
        def _():
            def maximum(at, size, top):
                return jnp.maximum(top, jnp.max(dg(ka[pl.ds(at, size), :], query, 1, 0), axis=0, keepdims=True))

            top = in_pieces(low, high, sizes[-1:], maximum, jnp.zeros((1, block), F32))

            def careful(at, size, acc):
                powers = jnp.exp2(dg(ka[pl.ds(at, size), :], query, 1, 0) - top).astype(BF16)
                return acc + dg(va[:, pl.ds(at, size)], powers, 1, 0)

            store(in_pieces(low, high, sizes[-1:], careful, jnp.zeros((dim + 16, block), F32)), own + top)

    over_blocks(len_ref, ends, items, length, outer, sizes, block_step)


def attend(x, lengths, outer=(1024, 512, 256), sizes=(2048, 1024, 512, 256)):
    rows, length = x.shape
    dim = rows // 3
    return pl.pallas_call(
        functools.partial(attend_kernel, lengths.shape[1], outer, sizes),
        out_shape=[
            jax.ShapeDtypeStruct((dim, length), BF16),
            jax.ShapeDtypeStruct((dim, length), F32),
            jax.ShapeDtypeStruct((1, length), F32),
        ],
        in_specs=[SMEM, VMEM],
        out_specs=[VMEM] * 3,
        scratch_shapes=[
            pltpu.VMEM((2 * dim, length), BF16),
            pltpu.VMEM((length, 2 * dim), BF16),
            pltpu.VMEM((dim + 16, length), BF16),
        ],
        compiler_params=pltpu.CompilerParams(vmem_limit_bytes=VMEM_LIMIT),
        name="attend",
    )(lengths, x)


def attend_back_kernel(
    items, outer, sizes, sub, len_ref, x_ref, o_ref, lse_ref, do_ref, g_ref, qa, ka, da, va, dq, dk, dv
):
    dim, length = x_ref.shape[0] // 3, x_ref.shape[1]
    ends = ends_of(len_ref, items)
    frames = min(1024, length)
    pad, wide_pad = jnp.zeros((dim - 32, frames), BF16), jnp.zeros((dim - 16, frames), BF16)
    for first in range(0, length, frames):
        cols = slice(first, first + frames)
        segment = segment_row(first, frames, ends)
        qa[cols, :] = jnp.concatenate(
            [
                x_ref[0:dim, cols],
                onehot_rows(segment, items, 0.0, 1.0).astype(BF16),
                split_rows(-lse_ref[:, cols]),
                pad,
            ],
            axis=0,
        ).T
        ka[0:dim, cols] = x_ref[dim : 2 * dim, cols]
        ka[dim : dim + 16, cols] = onehot_rows(segment, items, NEG, 0.0).astype(BF16)
        ka[dim + 16 : dim + 32, cols] = first_rows(3, frames)
        ka[dim + 32 :, cols] = pad
        grad = do_ref[:, cols]
        row_dot = jnp.sum(grad.astype(F32) * o_ref[:, cols], axis=0, keepdims=True)
        da[cols, :] = jnp.concatenate([grad, split_rows(-row_dot), wide_pad], axis=0).T
        va[0:dim, cols] = x_ref[2 * dim :, cols]
        va[dim : dim + 16, cols] = first_rows(3, frames)
        va[dim + 16 :, cols] = wide_pad
        dq[:, cols] = jnp.zeros((dim, frames), F32)

    def block_step(start, block, low, high):
        where = pl.ds(start, block)
        dk[...] = jnp.zeros_like(dk)
        dv[...] = jnp.zeros_like(dv)

        def piece(at, size, carry):
            rows = pl.ds(at, size)

            def score(u):
                cols = pl.ds(pl.multiple_of(start + u * sub, sub), sub)
                return dg(qa[rows, :], ka[:, cols], 1, 0), dg(da[rows, :], va[:, cols], 1, 0)

            count = block // sub
            grads = []
            ready = score(0)
            for u in range(count):
                scores, grad_probs = ready
                if u + 1 < count:
                    ready = score(u + 1)
                probs = jnp.exp2(scores)
                grad = (probs * grad_probs).astype(BF16)
                cols = slice(u * sub, (u + 1) * sub)
                dv[:, cols] += dg(do_ref[:, rows], probs.astype(BF16), 1, 0)
                dk[:, cols] += dg(x_ref[0:dim, rows], grad, 1, 0)
                grads.append(grad)
            dq[:, rows] += dg(ka[0:dim, where], jnp.concatenate(grads, axis=1), 1, 1)
            return carry

        in_pieces(low, high, sizes, piece, 0)
        g_ref[dim : 2 * dim, where] = (dk[:, 0:block] * LN2).astype(BF16)
        g_ref[2 * dim :, where] = dv[:, 0:block].astype(BF16)

    over_blocks(len_ref, ends, items, length, outer, sizes, block_step)
    for first in range(0, length, frames):
        cols = slice(first, first + frames)
        g_ref[0:dim, cols] = (dq[:, cols] * dim**-0.5).astype(BF16)


def attend_back(x, lengths, o, lse, do, outer=(512, 256), sizes=(2048, 1024, 512, 256), sub=256):
    rows, length = x.shape
    dim = rows // 3
    return pl.pallas_call(
        functools.partial(attend_back_kernel, lengths.shape[1], outer, sizes, sub),
        out_shape=jax.ShapeDtypeStruct(x.shape, BF16),
        in_specs=[SMEM] + [VMEM] * 4,
        out_specs=VMEM,
        scratch_shapes=[
            pltpu.VMEM((length, 2 * dim), BF16),
            pltpu.VMEM((2 * dim, length), BF16),
            pltpu.VMEM((length, 2 * dim), BF16),
            pltpu.VMEM((2 * dim, length), BF16),
            pltpu.VMEM((dim, length), F32),
            pltpu.VMEM((dim, outer[0]), F32),
            pltpu.VMEM((dim, outer[0]), F32),
        ],
        compiler_params=pltpu.CompilerParams(vmem_limit_bytes=VMEM_LIMIT),
        name="attend_back",
    )(lengths, x, o, lse, do)


def axis_steps(axis):
    steps, step = [], 1
    while step < lax.axis_size(axis):
        steps.append((axis, step))
        step *= 2
    assert step == lax.axis_size(axis)
    return steps


def stage_plans():
    sp_steps, dp_steps = axis_steps("sp"), axis_steps("dp")
    plane, rest = sp_steps[1:] + dp_steps[:1], dp_steps[1:]

    def groups(steps):
        return [steps[i : i + 2] for i in range(0, len(steps), 2)]

    plans = [sp_steps[:1]] + groups(plane) + groups(rest), [sp_steps[:1]] + groups(rest) + groups(plane)
    return tuple([stage for stage in plan if stage] for plan in plans)


def stage_masks(stage):
    masks = []
    for number in range(1, 1 << len(stage)):
        mask = {"sp": 0, "dp": 0}
        for i, (axis, step) in enumerate(stage):
            if number & (1 << i):
                mask[axis] += step
        masks.append((mask["sp"], mask["dp"]))
    return masks


def place_in(stage, number):
    place = 0
    for i, (axis, step) in enumerate(stage):
        bit = lax.rem(lax.axis_index(axis) // step, 2)
        place = place + (1 << i) * (1 - bit if number & (1 << i) else bit)
    return place


def exchange_plan(rows, stages, offset=0):
    sizes, size = [], rows
    for stage in stages:
        group = 1 << len(stage)
        splits = size % (16 * group) == 0
        size = size // group if splits else size
        sizes.append((splits, size, offset))
        offset += (group - 1) * size
    return sizes, offset, size


class Reduction:
    def __init__(self, base, rows, staged, stages, acc, stage, land, full, send, recv):
        self.stages, self.acc, self.stage, self.land, self.full = stages, acc, stage, land, full
        self.send, self.recv, self.low = send, recv, base
        self.sizes, _, self.own = exchange_plan(rows, stages, staged)
        self.first_sem = [sum((1 << len(s)) - 1 for s in stages[:k]) for k in range(len(stages))]

    def at(self, low, size):
        return pl.ds(pl.multiple_of(low, 16), size)

    def slot(self, k, i):
        _, size, offset = self.sizes[k]
        return slice(offset + i * size, offset + (i + 1) * size)

    def copies(self, way, k):
        splits, size, _ = self.sizes[k]
        out = []
        for i, masks in enumerate(stage_masks(self.stages[k])):
            if way == 0:
                source = self.stage.at[self.slot(k, i if splits else 0), :]
                target = self.land.at[self.slot(k, i), :]
            else:
                source = target = self.full.at[self.at(self.low, size), :]
            out.append(
                pltpu.make_async_remote_copy(
                    src_ref=source,
                    dst_ref=target,
                    send_sem=self.send.at[way, self.first_sem[k] + i],
                    recv_sem=self.recv.at[way, self.first_sem[k] + i],
                    device_id=peer_at(*masks),
                    device_id_type=MESH,
                )
            )
        return out

    def sum_send(self, k):
        splits, size, _ = self.sizes[k]
        copies = self.copies(0, k)
        for i, copy in enumerate(copies):
            if splits:
                away = self.low + place_in(self.stages[k], i + 1) * size
                self.stage[self.slot(k, i), :] = self.acc[self.at(away, size), :].astype(BF16)
            elif i == 0:
                self.stage[self.slot(k, 0), :] = self.acc[self.at(self.low, size), :].astype(BF16)
            copy.start()

    def sum_recv(self, k):
        splits, size, _ = self.sizes[k]
        copies = self.copies(0, k)
        for copy in copies:
            copy.wait()
        values = [self.land[self.slot(k, i), :].astype(F32) for i in range(len(copies))]
        if splits:
            self.low = self.low + place_in(self.stages[k], 0) * size
            values = [self.acc[self.at(self.low, size), :]] + values
        else:
            values = [self.stage[self.slot(k, 0), :].astype(F32)] + values
        while len(values) > 1:
            values = [values[i] + values[i + 1] for i in range(0, len(values), 2)]
        self.acc[self.at(self.low, size), :] = values[0]

    def close(self):
        where = self.at(self.low, self.own)
        self.full[where, :] = self.acc[where, :].astype(BF16)

    def share_send(self, k):
        if self.sizes[k][0]:
            for copy in self.copies(1, k):
                copy.start()

    def share_recv(self, k):
        splits, size, _ = self.sizes[k]
        if splits:
            for copy in self.copies(1, k):
                copy.wait()
            self.low = self.low - place_in(self.stages[k], 0) * size


def advance(streams, position):
    for stream in streams:
        n = len(stream.stages)
        if 0 < position <= n:
            stream.sum_recv(position - 1)
        if position < n:
            stream.sum_send(position)
        else:
            if position == n:
                stream.close()
            else:
                stream.share_recv(2 * n - position)
            if position < 2 * n:
                stream.share_send(2 * n - 1 - position)


def reduction_scratch(rows_list):
    plan, _ = stage_plans()
    staged = sum(max(exchange_plan(rows, stages)[1] for stages in stage_plans()) for rows in rows_list)
    sems = sum((1 << len(stage)) - 1 for stage in plan)
    return staged, (len(rows_list), 2, sems)


def make_streams(items, acc, stage, land, full, send, recv):
    streams, staged = [], 0
    for i, (base, rows, order) in enumerate(items):
        stages = stage_plans()[order]
        streams.append(
            Reduction(base, rows, staged, stages, acc, stage, land, full, send.at[i], recv.at[i])
        )
        staged += max(exchange_plan(rows, plan)[1] for plan in stage_plans())
    return streams


def all_masks(sp):
    masks = [(mask, 0) for mask in range(1, sp)]
    for plan in stage_plans():
        for stage in plan:
            masks += [m for m in stage_masks(stage) if m not in masks]
    return masks


def halves_of(ref, rows):
    return jnp.concatenate([ref[0, rows, :], ref[1, rows, :]], axis=1)


def combine(entries):
    count = sum(e[2] for e in entries)
    safe = jnp.maximum(count, 1.0)
    mean = sum(e[2] * e[0] for e in entries) / safe
    spread = sum(e[1] + e[2] * (e[0] - mean) * (e[0] - mean) for e in entries)
    return mean, spread, count


def pick(ref):
    return ref[0:1, :], ref[1:2, :], ref[2:3, :]


def total(entries):
    return tuple(sum(e[i] for e in entries) for i in range(3))


def middle_kernel(
    sp, dp, items, taps, chunk, block, len_ref, parts, x1_ref, cot, gain3, gain4, gain5, w_out, w_point1,
    depthwise, bn_gain, bn_bias, w_point2, w_in, w_down,
    out_ref, grad_x2, heads, mid, point_two, bn_grads, full,
    ctx, x2_ref, n3_keep, point, glu, conv, low_lim, high_lim, act, hidden, n4_keep, branch, swish, branch2,
    grad_x3, grad_y, grad_conv, grad_glu, grad_point, branch3, back_parts, tap_sums, edge_out, edge_in,
    send_box, near_box, far_box, sums, acc, stage, land,
    send, recv, local, back_send, back_recv, back_local, rim_send, rim_recv, box_send, box_recv,
    sum_send, sum_recv,
):
    me, me_dp = lax.axis_index("sp"), lax.axis_index("dp")
    frames, width = x1_ref.shape
    lanes = width // 2
    reach = taps // 2
    count = frames // chunk
    peers = sp_peers(sp)
    far_peers = [peer_at(0, mask) for mask in range(1, dp)]
    masks = all_masks(sp)
    masks += [(0, mask) for mask in range(1, dp) if (0, mask) not in masks]
    greeted = [peer_at(*mask) for mask in masks]
    length = sp * frames
    ends = ends_of(len_ref, items)
    first_frame = me * frames

    def limits(b, carry):
        rows = rows_at(b, chunk)
        frame = first_frame + b * chunk + lax.broadcasted_iota(I32, (chunk, lanes), 0)
        low, high = jnp.zeros_like(frame), jnp.full_like(frame, length)
        for end in ends:
            low = jnp.where(frame >= end, end, low)
        for end in reversed(ends):
            high = jnp.where(frame < end, end, high)
        low_lim[rows, :] = low - frame
        high_lim[rows, :] = high - 1 - frame
        return carry

    for ref in (glu, grad_conv):
        for h in range(2):
            ref[h, 0:reach, :] = jnp.zeros((reach, lanes), F32)
            ref[h, reach + frames :, :] = jnp.zeros((reach, lanes), F32)
    edge_in[...] = jnp.zeros_like(edge_in)
    send_box[...] = jnp.zeros_like(send_box)
    greet(greeted)
    lax.fori_loop(0, count, limits, 0)
    tap_sums[...] = jnp.zeros_like(tap_sums)
    sums[...] = jnp.zeros_like(sums)
    await_greetings(greeted)

    def moves(c, source, target, send_sems, recv_sems, local_sems):
        out = [
            pltpu.make_async_remote_copy(
                src_ref=source(peer[1], c),
                dst_ref=target(me, c),
                send_sem=send_sems.at[i, c],
                recv_sem=recv_sems.at[i, c],
                device_id=peer,
                device_id_type=MESH,
            )
            for i, peer in enumerate(peers)
        ]
        return out + [pltpu.make_async_copy(source(me, c), target(me, c), local_sems.at[c])]

    def by_frames(ref):
        return lambda device, c: ref.at[:, frame_cols(device, frames, c, chunk)]

    def by_head(ref):
        return lambda device, c: ref.at[device, :, rows_at(c, chunk)]

    def context_moves(c):
        return moves(c, by_frames(parts), by_head(ctx), send, recv, local)

    def begin(c, carry):
        for copy in context_moves(c):
            copy.start()
        return carry

    lax.fori_loop(0, count, begin, 0)

    def open_step(c, carry):
        rows = rows_at(c, chunk)
        for copy in context_moves(c):
            copy.wait()
        context = ctx[:, :, rows].reshape(width, chunk)
        x2 = x1_ref[rows, :] + dg(context, w_out[...], 0, 0)
        x2_ref[rows, :] = x2
        hat, _ = norm_parts(x2)
        n3 = (hat * row_of(gain3)).astype(BF16)
        n3_keep[rows, :] = n3
        pair = dg(n3, w_point1[...], 1, 0)
        point[rows, :] = pair
        gated = (pair[:, :width] * sigmoid(pair[:, width:])).astype(BF16).astype(F32)
        where = pl.ds(pl.multiple_of(reach + c * chunk, 8), chunk)
        glu[0, where, :] = gated[:, :lanes]
        glu[1, where, :] = gated[:, lanes:]
        return carry

    lax.fori_loop(0, count, open_step, 0)

    def rim_copies(call, side, source, target):
        peer = (me_dp, me - 1 if side == 0 else me + 1)
        return pltpu.make_async_remote_copy(
            src_ref=source, dst_ref=target, send_sem=rim_send.at[call, side], recv_sem=rim_recv.at[call, side],
            device_id=peer, device_id_type=MESH,
        )

    def swap_rims(call, sources, targets):
        @pl.when(me > 0)
        def _():
            rim_copies(call, 0, sources[0], targets[1]).start()

        @pl.when(me < sp - 1)
        def _():
            rim_copies(call, 1, sources[1], targets[0]).start()

    def await_rims(call, sources, targets):
        @pl.when(me > 0)
        def _():
            rim_copies(call, 0, sources[0], targets[1]).wait_send()
            rim_copies(call, 1, sources[1], targets[0]).wait_recv()

        @pl.when(me < sp - 1)
        def _():
            rim_copies(call, 1, sources[1], targets[0]).wait_send()
            rim_copies(call, 0, sources[0], targets[1]).wait_recv()

    for side, rows in ((0, slice(reach, 2 * reach)), (1, slice(frames, frames + reach))):
        for h in range(2):
            edge_out[side, 0:reach, h * lanes : (h + 1) * lanes] = glu[h, rows, :]
    glu_rims = (
        [edge_out.at[0, 0:reach, :], edge_out.at[1, 0:reach, :]],
        [edge_in.at[0, 0:reach, :], edge_in.at[1, 0:reach, :]],
    )
    swap_rims(0, *glu_rims)

    zero = jnp.zeros((block, lanes), F32)

    def conv_step(b, carry):
        low, high = low_lim[rows_at(b, block), :], high_lim[rows_at(b, block), :]
        start = pl.multiple_of(b * block, block)
        result = [zero, zero]
        for tap in range(taps):
            shift = tap - reach
            inside = (low <= shift) if shift < 0 else (high >= shift)
            for h in range(2):
                view = glu.at[h, pl.ds(start, block + 2 * reach), :]
                term = jnp.where(inside, view[tap : tap + block, :], 0.0)
                result[h] = result[h] + depthwise[tap : tap + 1, h * lanes : (h + 1) * lanes].astype(F32) * term
        valid = (first_frame + start + lax.broadcasted_iota(I32, (block, lanes), 0)) < ends[-1]
        for h in range(2):
            conv[h, rows_at(b, block), :] = result[h]
            sums[0:1, h * lanes : (h + 1) * lanes] += jnp.sum(jnp.where(valid, result[h], 0.0), axis=0, keepdims=True)
        return carry

    blocks = frames // block
    lax.fori_loop(1, blocks - 1, conv_step, 0)
    await_rims(0, *glu_rims)
    for h in range(2):
        glu[h, 0:reach, :] = edge_in[0, 0:reach, h * lanes : (h + 1) * lanes]
        glu[h, reach + frames :, :] = edge_in[1, 0:reach, h * lanes : (h + 1) * lanes]
    conv_step(0, 0)
    conv_step(blocks - 1, 0)

    own_count = jnp.clip(ends[-1] - first_frame, 0, frames).astype(F32)
    own_mean = sums[0:1, :] / jnp.maximum(own_count, 1.0)
    sums[0:1, :] = jnp.zeros((1, width), F32)

    def spread_step(c, carry):
        rows = rows_at(c, chunk)
        valid = (first_frame + c * chunk + lax.broadcasted_iota(I32, (chunk, width), 0)) < ends[-1]
        apart = jnp.where(valid, halves_of(conv, rows) - own_mean, 0.0)
        sums[1:2, :] += jnp.sum(apart * apart, axis=0, keepdims=True)
        return carry

    lax.fori_loop(0, count, spread_step, 0)

    def box_copies(call, stage):
        group = peers if stage == 0 else far_peers
        target = near_box if stage == 0 else far_box
        base = 0 if stage == 0 else sp - 1
        return [
            pltpu.make_async_remote_copy(
                src_ref=send_box.at[call, stage],
                dst_ref=target.at[call, i],
                send_sem=box_send.at[call, base + i],
                recv_sem=box_recv.at[call, base + i],
                device_id=peer,
                device_id_type=MESH,
            )
            for i, peer in enumerate(group)
        ]

    def box_begin(call, stage, rows):
        for i, row in enumerate(rows):
            send_box[call, stage, i : i + 1, :] = row
        for copy in box_copies(call, stage):
            copy.start()

    def box_end(call, stage, rows, merge):
        target = near_box if stage == 0 else far_box
        copies = box_copies(call, stage)
        for copy in copies:
            copy.wait()
        return merge([rows] + [pick(target[call, i]) for i in range(len(copies))])

    stats = (own_mean, sums[1:2, :], jnp.full((1, width), 1.0, F32) * own_count)
    sums[1:2, :] = jnp.zeros((1, width), F32)
    box_begin(0, 0, stats)
    stats = box_end(0, 0, stats, combine)
    box_begin(0, 1, stats)
    mean, spread, frame_count = box_end(0, 1, stats, combine)
    inv_std = lax.rsqrt(spread / frame_count + EPS)
    norm_gain, norm_bias = row_of(bn_gain), row_of(bn_bias)

    def heart_step(c, carry):
        rows = rows_at(c, chunk)
        normed = (halves_of(conv, rows) - mean) * inv_std
        y = normed * norm_gain + norm_bias
        sig_y = sigmoid(y)
        w = (y * sig_y).astype(BF16)
        swish[rows, :] = w
        x3 = x2_ref[rows, :] + dg(w, w_point2[...], 1, 0)
        hat4, inv4 = norm_parts(x3)
        g4 = row_of(gain4)
        n4 = (hat4 * g4).astype(BF16)
        n4_keep[rows, :] = n4
        a = dg(n4, w_in[...], 1, 0)
        sig = sigmoid(a)
        s = (a * sig).astype(BF16)
        act[rows, :] = s
        x4 = x3 + 0.5 * dg(s, w_down[...], 1, 0)
        hat5, inv5 = norm_parts(x4)
        g5 = row_of(gain5)
        out_ref[rows, :] = (hat5 * g5).astype(BF16)
        top = cot[rows, :].astype(F32)
        mid[3 * width + 4 : 3 * width + 5, :] += jnp.sum(top * hat5, axis=0, keepdims=True)
        grad_x4 = norm_back(top, hat5, inv5, g5)
        low_grad = (0.5 * grad_x4).astype(BF16)
        branch[rows, :] = low_grad
        grad = dg(low_grad, w_down[...], 1, 1)
        low_hidden = (grad * (sig * (1.0 + a * (1.0 - sig)))).astype(BF16)
        hidden[rows, :] = low_hidden
        grad = dg(low_hidden, w_in[...], 1, 1)
        mid[3 * width + 3 : 3 * width + 4, :] += jnp.sum(grad * hat4, axis=0, keepdims=True)
        grad3 = grad_x4 + norm_back(grad, hat4, inv4, g4)
        grad_x3[rows, :] = grad3
        low_grad = grad3.astype(BF16)
        branch2[rows, :] = low_grad
        grad = dg(low_grad, w_point2[...], 1, 1) * (sig_y * (1.0 + y * (1.0 - sig_y)))
        grad_y[0, rows, :] = grad[:, :lanes]
        grad_y[1, rows, :] = grad[:, lanes:]
        sums[2:3, :] += jnp.sum(grad, axis=0, keepdims=True)
        sums[3:4, :] += jnp.sum(grad * normed, axis=0, keepdims=True)
        return carry

    mid[3 * width :, :] = jnp.zeros((width, width), F32)
    lax.fori_loop(0, count, heart_step, 0)

    pair = (sums[2:3, :], sums[3:4, :], jnp.zeros((1, width), F32))
    box_begin(1, 0, pair)
    for side, rows in ((0, slice(0, reach)), (1, slice(frames - reach, frames))):
        for h in range(2):
            cols = slice(h * lanes, (h + 1) * lanes)
            edge_out[side, reach : 2 * reach, cols] = grad_y[h, rows, :]
            edge_out[side, 2 * reach : 3 * reach, cols] = conv[h, rows, :]
    grad_rims = (
        [edge_out.at[0, reach : 3 * reach, :], edge_out.at[1, reach : 3 * reach, :]],
        [edge_in.at[0, reach : 3 * reach, :], edge_in.at[1, reach : 3 * reach, :]],
    )
    swap_rims(1, *grad_rims)
    wide = w_in.shape[1]
    streams = make_streams(
        [(0, wide, 0), (wide, wide, 1)], acc, stage, land, full, sum_send, sum_recv
    )
    steps = len(stage_plans()[0])
    for j in range(0, wide, width):
        acc[j : j + width, :] = dg(act[:, j : j + width], branch[...], 0, 0)
    advance(streams[:1], 0)
    pair = box_end(1, 0, pair, total)
    box_begin(1, 1, pair)
    for j in range(0, wide, width):
        acc[wide + j : wide + j + width, :] = dg(n4_keep[...], hidden[:, j : j + width], 0, 0)
    advance(streams[1:], 0)
    advance(streams[:1], 1)
    point_two[...] = dg(swish[...], branch2[...], 0, 0)
    advance(streams[1:], 1)
    await_rims(1, *grad_rims)
    bias_sum, gain_sum, _ = box_end(1, 1, pair, total)
    bn_grads[0:1, :] = gain_sum
    bn_grads[1:2, :] = bias_sum
    bn_grads[2:8, :] = jnp.zeros((6, width), F32)

    scale = norm_gain * inv_std
    slope = -inv_std * inv_std * norm_gain * gain_sum / frame_count
    shift_all = -inv_std * norm_gain * bias_sum / frame_count

    def conv_grad(grad, value, frame, h):
        cols = slice(h * lanes, (h + 1) * lanes)
        extra = (value - mean[:, cols]) * slope[:, cols] + shift_all[:, cols]
        return grad * scale[:, cols] + jnp.where(frame < ends[-1], extra, 0.0)

    def grad_conv_step(c, carry):
        rows = rows_at(c, chunk)
        frame = first_frame + c * chunk + lax.broadcasted_iota(I32, (chunk, lanes), 0)
        where = pl.ds(pl.multiple_of(reach + c * chunk, 8), chunk)
        for h in range(2):
            grad_conv[h, where, :] = conv_grad(grad_y[h, rows, :], conv[h, rows, :], frame, h)
        return carry

    lax.fori_loop(0, count, grad_conv_step, 0)
    for side, rows, begin_frame in (
        (0, slice(0, reach), first_frame - reach),
        (1, slice(reach + frames, 2 * reach + frames), first_frame + frames),
    ):
        frame = begin_frame + lax.broadcasted_iota(I32, (reach, lanes), 0)
        for h in range(2):
            cols = slice(h * lanes, (h + 1) * lanes)
            grad_conv[h, rows, :] = conv_grad(
                edge_in[side, reach : 2 * reach, cols], edge_in[side, 2 * reach : 3 * reach, cols], frame, h
            )

    def conv_back_step(b, carry):
        low, high = low_lim[rows_at(b, block), :], high_lim[rows_at(b, block), :]
        start = pl.multiple_of(b * block, block)
        result = [zero, zero]
        here = [glu[h, pl.ds(pl.multiple_of(reach + start, 8), block), :] for h in range(2)]
        for tap in range(taps):
            shift = reach - tap
            inside = (low <= shift) if shift < 0 else (high >= shift)
            at = reach + shift
            for h in range(2):
                view = grad_conv.at[h, pl.ds(start, block + 2 * reach), :]
                term = jnp.where(inside, view[at : at + block, :], 0.0)
                result[h] = result[h] + depthwise[tap : tap + 1, h * lanes : (h + 1) * lanes].astype(F32) * term
                tap_sums[tap, h] += jnp.sum((here[h] * term).reshape(block // 8, 8, lanes), axis=0)
        for h in range(2):
            grad_glu[h, rows_at(b, block), :] = result[h]
        return carry

    points = list(range(2, 2 * steps + 1))
    advance(streams, points.pop(0))
    lax.fori_loop(0, blocks // 2, conv_back_step, 0)
    advance(streams, points.pop(0))
    lax.fori_loop(blocks // 2, blocks, conv_back_step, 0)
    advance(streams, points.pop(0))

    def back_moves(c):
        return moves(c, by_head(back_parts), by_frames(heads), back_send, back_recv, back_local)

    def close_step(c, carry):
        rows = rows_at(c, chunk)
        grad = halves_of(grad_glu, rows)
        value, gate = point[rows, :width], sigmoid(point[rows, width:])
        low_grad = jnp.concatenate([grad * gate, grad * value * gate * (1.0 - gate)], axis=1).astype(BF16)
        grad_point[rows, :] = low_grad
        grad = dg(low_grad, w_point1[...], 1, 1)
        hat, inv = norm_parts(x2_ref[rows, :])
        mid[3 * width + 2 : 3 * width + 3, :] += jnp.sum(grad * hat, axis=0, keepdims=True)
        grad2 = grad_x3[rows, :] + norm_back(grad, hat, inv, row_of(gain3))
        grad_x2[rows, :] = grad2
        low_grad = grad2.astype(BF16)
        branch3[rows, :] = low_grad
        back_parts[:, :, rows] = dg(w_out[...], low_grad, 1, 1).astype(BF16).reshape(sp, width // sp, chunk)
        for copy in back_moves(c):
            copy.start()
        return carry

    lax.fori_loop(0, count // 2, close_step, 0)
    advance(streams, points.pop(0))
    lax.fori_loop(count // 2, count, close_step, 0)
    for j in range(2):
        mid[j * width : (j + 1) * width, :] = dg(n3_keep[...], grad_point[:, j * width : (j + 1) * width], 0, 0)
    mid[2 * width : 3 * width, :] = dg(ctx[...].reshape(width, frames), branch3[...], 1, 0)
    for tap in range(taps):
        row = 3 * width + 8 + tap
        for h in range(2):
            mid[row : row + 1, h * lanes : (h + 1) * lanes] = jnp.sum(tap_sums[tap, h], axis=0, keepdims=True)
    while points:
        advance(streams, points.pop(0))

    def finish(c, carry):
        for copy in back_moves(c):
            copy.wait()
        return carry

    lax.fori_loop(0, count, finish, 0)


def middle(
    lengths, parts, x1, cot, gain3, gain4, gain5, w_out, w_point1, depthwise, bn_gain, bn_bias, w_point2,
    w_in, w_down, dp,
):
    frames, width = x1.shape
    length = parts.shape[1]
    sp = length // frames
    wide = w_in.shape[1]
    taps = depthwise.shape[0]
    reach = taps // 2
    chunk = min(256, frames)
    count = frames // chunk
    lanes = width // 2
    staged, sems = reduction_scratch([wide, wide])
    keep, low_keep = pltpu.VMEM((frames, width), F32), pltpu.VMEM((frames, width), BF16)
    split = pltpu.VMEM((2, frames, lanes), F32)
    rimmed = pltpu.VMEM((2, frames + 2 * reach, lanes), F32)
    rims = pltpu.VMEM((2, 3 * reach, width), F32)
    moves = [DMA((sp - 1, count)), DMA((sp - 1, count)), DMA((count,))]
    return pl.pallas_call(
        functools.partial(middle_kernel, sp, dp, lengths.shape[1], taps, chunk, 32),
        out_shape=[
            jax.ShapeDtypeStruct((frames, width), BF16),
            jax.ShapeDtypeStruct((frames, width), F32),
            jax.ShapeDtypeStruct(parts.shape, BF16),
            jax.ShapeDtypeStruct((4 * width, width), F32),
            jax.ShapeDtypeStruct((width, width), F32),
            jax.ShapeDtypeStruct((8, width), F32),
            jax.ShapeDtypeStruct((2 * wide, width), BF16),
        ],
        in_specs=[SMEM, pl.BlockSpec(memory_space=pl.ANY)] + [VMEM] * 13,
        out_specs=[VMEM] * 7,
        scratch_shapes=[
            pltpu.VMEM((sp, width // sp, frames), BF16),
            keep,
            low_keep,
            pltpu.VMEM((frames, 2 * width), F32),
            rimmed,
            split,
            pltpu.VMEM((frames, lanes), I32),
            pltpu.VMEM((frames, lanes), I32),
            pltpu.VMEM((frames, wide), BF16),
            pltpu.VMEM((frames, wide), BF16),
            low_keep,
            low_keep,
            low_keep,
            low_keep,
            keep,
            split,
            rimmed,
            split,
            pltpu.VMEM((frames, 2 * width), BF16),
            low_keep,
            pltpu.VMEM((sp, width // sp, frames), BF16),
            pltpu.VMEM((taps, 2, 8, lanes), F32),
            rims,
            rims,
            pltpu.VMEM((2, 2, 8, width), F32),
            pltpu.VMEM((2, sp - 1, 8, width), F32),
            pltpu.VMEM((2, dp - 1, 8, width), F32),
            pltpu.VMEM((8, width), F32),
            pltpu.VMEM((2 * wide, width), F32),
            pltpu.VMEM((staged, width), BF16),
            pltpu.VMEM((staged, width), BF16),
        ]
        + moves
        + moves
        + [DMA((2, 2)), DMA((2, 2)), DMA((2, sp + dp - 2)), DMA((2, sp + dp - 2)), DMA(sems), DMA(sems)],
        compiler_params=pltpu.CompilerParams(
            collective_id=1, has_side_effects=True, vmem_limit_bytes=VMEM_LIMIT
        ),
        name="middle",
    )(
        lengths, parts, x1, cot, gain3, gain4, gain5, w_out, w_point1, depthwise, bn_gain, bn_bias, w_point2,
        w_in, w_down,
    )


def back_kernel(
    sp, chunk, parts, trig, tok, x1_ref, n2_ref, grad_x2, gain1, gain2, w_in, w_out, w_qkv, mid, point_two,
    grad_ref, full, heads, joined, n1_keep, hat_keep, branch, act, slope, hidden, grad_x1, gains, acc, stage, land,
    send, recv, local, sum_send, sum_recv,
):
    me = lax.axis_index("sp")
    frames, width = tok.shape
    wide = w_in.shape[1]
    half = trig.shape[0] // 2
    dim = 2 * half
    count = frames // chunk
    peers = sp_peers(sp)
    greeted = [peer_at(*mask) for mask in all_masks(sp)]
    greet(greeted)
    unit = 4 * width
    last = 4 * unit
    streams = make_streams(
        [(0, unit, 1), (unit, unit, 1), (2 * unit, unit, 0), (3 * unit, unit, 0), (last, 16, 0)],
        acc, stage, land, full, sum_send, sum_recv,
    )
    early, qkv, down, up, rest = ([stream] for stream in streams)
    acc[0:unit, :] = mid[...]
    acc[last : last + 16, :] = jnp.zeros((16, width), F32)
    gains[...] = jnp.zeros_like(gains)
    await_greetings(greeted)

    def copies(c):
        out = [
            pltpu.make_async_remote_copy(
                src_ref=parts.at[:, frame_cols(peer[1], frames, c, chunk)],
                dst_ref=heads.at[me, :, rows_at(c, chunk)],
                send_sem=send.at[i, c],
                recv_sem=recv.at[i, c],
                device_id=peer,
                device_id_type=MESH,
            )
            for i, peer in enumerate(peers)
        ]
        own = pltpu.make_async_copy(
            parts.at[:, frame_cols(me, frames, c, chunk)], heads.at[me, :, rows_at(c, chunk)], local.at[c]
        )
        return out + [own]

    def begin(c, carry):
        for copy in copies(c):
            copy.start()
        return carry

    lax.fori_loop(0, count, begin, 0)
    advance(early, 0)

    def again(c, carry):
        rows = rows_at(c, chunk)
        hat, inv = norm_parts(tok[rows, :].astype(F32))
        hat_keep[rows, :] = hat
        n1 = (hat * row_of(gain1)).astype(BF16)
        n1_keep[rows, :] = n1
        a = dg(n1, w_in[...], 1, 0)
        sig = sigmoid(a)
        act[rows, :] = (a * sig).astype(BF16)
        slope[rows, :] = sig * (1.0 + a * (1.0 - sig))
        return carry

    lax.fori_loop(0, count // 2, again, 0)
    advance(early, 1)
    lax.fori_loop(count // 2, count, again, 0)

    def arrive(c, carry):
        rows = rows_at(c, chunk)
        for copy in copies(c):
            copy.wait()
        sine, cosine = trig[0:half, rows], trig[half:, rows]
        for head in range(sp):
            for part in range(2):
                first = heads[head, part * dim : part * dim + half, rows].astype(F32)
                second = heads[head, part * dim + half : (part + 1) * dim, rows].astype(F32)
                low = part * width + head * dim
                joined[low : low + half, rows] = (first * cosine + second * sine).astype(BF16)
                joined[low + half : low + dim, rows] = (second * cosine - first * sine).astype(BF16)
            low = 2 * width + head * dim
            joined[low : low + dim, rows] = heads[head, 2 * dim : 3 * dim, rows]
        grad = dg(joined[:, rows], w_qkv[...], 0, 1)
        hat, inv = norm_parts(x1_ref[rows, :])
        gains[1:2, :] += jnp.sum(grad * hat, axis=0, keepdims=True)
        grad = grad_x2[rows, :] + norm_back(grad, hat, inv, row_of(gain2))
        grad_x1[rows, :] = grad
        branch[rows, :] = (0.5 * grad).astype(BF16)
        return carry

    steps = len(stage_plans()[0])
    points = list(range(2, 2 * steps + 1))
    for c in range(count):
        if c > 0 and points:
            advance(early, points.pop(0))
        lax.fori_loop(c, c + 1, arrive, 0)
    for j in range(0, wide, width):
        acc[2 * unit + j : 2 * unit + j + width, :] = dg(act[:, j : j + width], branch[...], 0, 0)
    advance(down, 0)
    acc[unit : unit + 3 * width, :] = dg(joined[...], n2_ref[...], 1, 0)
    acc[unit + 3 * width : 2 * unit, :] = point_two[...]
    advance(qkv, 0)

    def through(c, carry):
        rows = rows_at(c, chunk)
        grad = dg(branch[rows, :], w_out[...], 1, 1)
        low_hidden = (grad * slope[rows, :]).astype(BF16)
        hidden[rows, :] = low_hidden
        grad = dg(low_hidden, w_in[...], 1, 1)
        hat = hat_keep[rows, :]
        gains[0:1, :] += jnp.sum(grad * hat, axis=0, keepdims=True)
        _, inv = norm_parts(tok[rows, :].astype(F32))
        grad_ref[rows, :] = (grad_x1[rows, :] + norm_back(grad, hat, inv, row_of(gain1))).astype(BF16)
        return carry

    lax.fori_loop(0, count, through, 0)
    for j in range(0, wide, width):
        acc[3 * unit + j : 3 * unit + j + width, :] = dg(n1_keep[...], hidden[:, j : j + width], 0, 0)
    advance(up, 0)
    acc[last : last + 8, :] = gains[...]
    advance(rest, 0)
    while points:
        advance(early, points.pop(0))
    for position in range(1, 2 * steps + 1):
        advance(down + qkv + up + rest, position)


def back(parts, trig, tok, x1, n2, grad_x2, gain1, gain2, w_in, w_out, w_qkv, mid, point_two):
    frames, width = tok.shape
    head_width, length = parts.shape
    sp = length // frames
    chunk = min(256, frames)
    count = frames // chunk
    wide = w_in.shape[1]
    rows = 16 * width + 16
    staged, sems = reduction_scratch([4 * width] * 4 + [16])
    low_keep, keep = pltpu.VMEM((frames, width), BF16), pltpu.VMEM((frames, width), F32)
    return pl.pallas_call(
        functools.partial(back_kernel, sp, chunk),
        out_shape=[
            jax.ShapeDtypeStruct((frames, width), BF16),
            jax.ShapeDtypeStruct((rows, width), BF16),
        ],
        in_specs=[pl.BlockSpec(memory_space=pl.ANY)] + [VMEM] * 12,
        out_specs=[VMEM] * 2,
        scratch_shapes=[
            pltpu.VMEM((sp, head_width, frames), BF16),
            pltpu.VMEM((3 * width, frames), BF16),
            low_keep,
            keep,
            low_keep,
            pltpu.VMEM((frames, wide), BF16),
            pltpu.VMEM((frames, wide), F32),
            pltpu.VMEM((frames, wide), BF16),
            keep,
            pltpu.VMEM((8, width), F32),
            pltpu.VMEM((rows, width), F32),
            pltpu.VMEM((staged, width), BF16),
            pltpu.VMEM((staged, width), BF16),
            DMA((sp - 1, count)),
            DMA((sp - 1, count)),
            DMA((count,)),
            DMA(sems),
            DMA(sems),
        ],
        compiler_params=pltpu.CompilerParams(
            collective_id=2, has_side_effects=True, vmem_limit_bytes=VMEM_LIMIT
        ),
        name="back",
    )(parts, trig, tok, x1, n2, grad_x2, gain1, gain2, w_in, w_out, w_qkv, mid, point_two)


def unpack_kernel(
    taps, full_two, full, bn_grads, output, input_grad,
    output_to, input_to, gain1_to, in_one_to, out_one_to, gain2_to, qkv_to, out_weight_to, gain3_to, point_one_to,
    depthwise_to, bn_gain_to, bn_bias_to, point_two_to, gain4_to, in_two_to, out_two_to, gain5_to,
    in_one, out_one, qkv, point_one, point_two, out_weight, in_two, out_two, depthwise, sems,
):
    width = full.shape[1]
    unit = 4 * width
    copies = []

    def send(source, target):
        copies.append(pltpu.make_async_copy(source, target, sems.at[len(copies)]))
        copies[-1].start()

    def block(ref, base):
        return ref[base : base + width, :].astype(F32)

    send(output, output_to)
    send(input_grad, input_to)
    for j in range(0, unit, width):
        out_two[j : j + width, :] = block(full_two, j)
    send(out_two, out_two_to)
    for j in range(0, unit, width):
        in_two[:, j : j + width] = block(full_two, unit + j)
    send(in_two, in_two_to)
    for j in range(0, unit, width):
        out_one[j : j + width, :] = block(full, 2 * unit + j)
    send(out_one, out_one_to)
    for j in range(0, unit, width):
        in_one[:, j : j + width] = block(full, 3 * unit + j)
    send(in_one, in_one_to)
    for j in range(0, 2 * width, width):
        point_one[:, j : j + width] = block(full, j)
    send(point_one, point_one_to)
    out_weight[...] = block(full, 2 * width)
    send(out_weight, out_weight_to)
    point_two[...] = block(full, unit + 3 * width)
    send(point_two, point_two_to)
    for j in range(0, 3 * width, width):
        qkv[:, j : j + width] = block(full, unit + j).T
    send(qkv, qkv_to)
    small = full[3 * width : 3 * width + 64, :].astype(F32)
    depthwise[...] = small[8 : 8 + taps]
    send(depthwise, depthwise_to)
    rest = full[4 * unit : 4 * unit + 16, :].astype(F32)
    for ref, row in (
        (gain1_to, rest[0]), (gain2_to, rest[1]), (gain3_to, small[2]), (gain4_to, small[3]), (gain5_to, small[4]),
        (bn_gain_to, bn_grads[0, :]), (bn_bias_to, bn_grads[1, :]),
    ):
        ref[...] = row
    for copy in copies:
        copy.wait()


def unpack(full_two, full, bn_grads, output, input_grad, taps):
    width = full.shape[1]
    row, square, tall, flat = (width,), (width, width), (4 * width, width), (width, 4 * width)
    thrice, twice = (width, 3 * width), (width, 2 * width)
    anywhere = pl.BlockSpec(memory_space=pl.ANY)
    shapes = [
        output.shape, input_grad.shape, row, flat, tall, row, thrice, square, row, twice, (taps, width), row, row,
        square, row, flat, tall, row,
    ]
    return pl.pallas_call(
        functools.partial(unpack_kernel, taps),
        out_shape=[jax.ShapeDtypeStruct(shape, F32 if i > 1 else BF16) for i, shape in enumerate(shapes)],
        in_specs=[VMEM] * 5,
        out_specs=[VMEM if shape == row else anywhere for shape in shapes],
        scratch_shapes=[
            pltpu.VMEM(shape, F32)
            for shape in (flat, tall, thrice, twice, square, square, flat, tall, (taps, width))
        ]
        + [DMA((11,))],
        compiler_params=pltpu.CompilerParams(vmem_limit_bytes=VMEM_LIMIT),
        name="unpack",
    )(full_two, full, bn_grads, output, input_grad)


def on_device(
    tokens, ln1_gain, ffn1_in, ffn1_out, ln2_gain, w_qkv, w_out, ln3_gain, w_point1, depthwise,
    bn_gain, bn_bias, w_point2, ln4_gain, ffn2_in, ffn2_out, ln5_gain, lengths, cotangent,
):
    width = tokens.shape[2]
    sp, dp = lax.axis_size("sp"), lax.axis_size("dp")
    assert HEADS == sp and ffn1_in.shape[1] == ffn2_in.shape[1] == 4 * width
    half = width // HEADS // 2
    turns = 10000.0 ** (-np.arange(half, dtype=np.float64) / half) / (2 * np.pi)
    high = np.round(turns * 4096.0) / 4096.0
    freq = jnp.asarray(np.stack([high, turns - high], axis=1), F32)
    x1, n2, trig, heads = front(lengths, tokens[0], ln1_gain, ffn1_in, ffn1_out, ln2_gain, w_qkv, freq, sp)
    context, raw_context, log_sums = attend(heads, lengths)
    output, grad_x2, grad_context, mid, point_two, bn_grads, full_two = middle(
        lengths, context, x1, cotangent[0], ln3_gain, ln4_gain, ln5_gain, w_out, w_point1, depthwise,
        bn_gain, bn_bias, w_point2, ffn2_in, ffn2_out, dp,
    )
    grad_heads = attend_back(heads, lengths, raw_context, log_sums, grad_context)
    input_grad, full = back(
        grad_heads, trig, tokens[0], x1, n2, grad_x2, ln1_gain, ln2_gain, ffn1_in, ffn1_out, w_qkv, mid, point_two
    )
    results = unpack(full_two, full, bn_grads, output, input_grad, depthwise.shape[0])
    return (results[0][None], results[1][None]) + tuple(results[2:])


def solution(mesh):
    split = P("dp", "sp", None)
    return jax.shard_map(
        on_device,
        mesh=mesh,
        in_specs=(split,) + (P(),) * 16 + (P("dp", None), split),
        out_specs=(split, split) + (P(),) * 16,
        check_vma=False,
    )
```

time: 262 us -> 220 us (0.84)
  Pallas kernels: 253 us -> 219 us
  local copies, waits for them, and re-layouts: 7.74 us -> 0 us
    pallas_call x1, Pallas kernels: 88.8 us -> 62.1 us  [back(): pl.pallas_call(functools.partial(back_kernel, sp, chunk), out_shape=[jax....]
    pallas_call x3, Pallas kernels: 79.9 us -> 64.1 us  [the longest x1 39.5 us: attend_back(): pl.pallas_call(functools.partial(attend_back_kernel, lengths.shape[1], ou...]
    pallas_call x1, Pallas kernels: 58.7 us -> 68 us  [middle(): pl.pallas_call(functools.partial(middle_kernel, sp, dp, lengths.shape[1],...]
    slice x3 -> x0, local copies, waits for them, and re-layouts: 4.2 us -> none  [the longest x1 1.46 us: on_device(): small[4]]
    unnamed x7 -> x0, local copies, waits for them, and re-layouts: 2.76 us -> none
where the time goes in v4:
time: 220 us
  Pallas kernels  219 us (100%)
    pallas_call x1, Pallas kernels, middle(): pl.pallas_call(functools.partial(middle_kernel, sp, dp, lengths.shape[1],...  68 us
    pallas_call x1, Pallas kernels, back(): pl.pallas_call(functools.partial(back_kernel, sp, chunk), out_shape=[jax....  62.1 us
    pallas_call x1, Pallas kernels, attend_back(): pl.pallas_call(functools.partial(attend_back_kernel, lengths.shape[1], ou...  39.5 us
    pallas_call x1, Pallas kernels, front(): pl.pallas_call(functools.partial(front_kernel, sp, lengths.shape[1], chun...  24.7 us
    pallas_call x1, Pallas kernels, attend(): pl.pallas_call(functools.partial(attend_kernel, lengths.shape[1], outer,...  18.9 us
    pallas_call x1, Pallas kernels, unpack(): pl.pallas_call(functools.partial(unpack_kernel, taps), out_shape=[jax.Sha...  5.76 us

profile of v4, /device:TPU:0, one launch (start us, length us, event | category | flops | bytes accessed | tf_op | source)
XLA Modules:
  0.0 219.7 jit_solution(13071132800887862085)
XLA Ops:
  0.7 24.7 %front.1 = (f32[1024,256]{1,0:T(8,128)}, bf16[1024,256]{1,0:T(8,128)(2,1)}, f32[64,1024]{1,0:T(8,128)}, bf16[192,4096]{1,0:T(8,128)(2,1)}) custom-call(s32[1,4]{1,0:T(1,128)} %len_ref.7, bf16[1024,256]{1,0:T(8,128)(2,1)} %bitcast.4, bf16[256]{0:T(256)(128)(2,1)} %gain1.3, bf16[256,1024]{1,0:T(8,128)(2,1)} %w_in.5, bf16[1024,256]{1,0:T(8,128)(2,1)} %w_out.5, ...), custom_call_target="tpu_custom_call" | custom-call | tf_op jit(solution)/shard_map/front/pallas_call | solution.py:227
  25.3 18.9 %attend.1 = (bf16[64,4096]{1,0:T(8,128)(2,1)}, f32[64,4096]{1,0:T(8,128)}, f32[1,4096]{1,0:T(1,128)}) custom-call(s32[1,4]{1,0:T(1,128)} %len_ref.7, bf16[192,4096]{1,0:T(8,128)(2,1)} %get-tuple-element.52.x_ref), custom_call_target="tpu_custom_call" | custom-call | tf_op jit(solution)/shard_map/attend/pallas_call | solution.py:359
  44.2 68.0 %middle.1 = (bf16[1024,256]{1,0:T(8,128)(2,1)}, f32[1024,256]{1,0:T(8,128)}, bf16[64,4096]{1,0:T(8,128)(2,1)}, f32[1024,256]{1,0:T(8,128)}, f32[256,256]{1,0:T(8...) custom-call(s32[1,4]{1,0:T(1,128)} %len_ref.7, bf16[64,4096]{1,0:T(8,128)(2,1)} %get-tuple-element.53.parts, ...), custom_call_target="tpu_custom_call" | custom-call | tf_op jit(solution)/shard_map/middle/pallas_call | solution.py:1065
  112.2 39.5 %attend_back.1.parts = bf16[192,4096]{1,0:T(8,128)(2,1)} custom-call(s32[1,4]{1,0:T(1,128)} %len_ref.7, bf16[192,4096]{1,0:T(8,128)(2,1)} %get-tuple-element.52.x_ref, f32[64,4096]{1,0:T(8,128)} %get-tuple-element.56.o_ref, f32[1,4096]{1,0:T(1,128)} %get-tuple-element.57.lse_ref, bf16[64,4096]{1,0:T(8,128)(2,1)} %get-tuple-element.58.do_ref), custom_call_target="tpu_custom_call" | custom-call | tf_op jit(solution)/shard_map/attend_back/pallas_call | solution.py:450
  151.7 62.1 %back.1 = (bf16[1024,256]{1,0:T(8,128)(2,1)}, bf16[4112,256]{1,0:T(8,128)(2,1)}) custom-call(bf16[192,4096]{1,0:T(8,128)(2,1)} %attend_back.1.parts, f32[64,1024]{1,0:T(8,128)} %get-tuple-element.59.trig, bf16[1024,256]{1,0:T(8,128)(2,1)} %bitcast.5, f32[1024,256]{1,0:T(8,128)} %get-tuple-element.54.x1_ref, bf16[1024,256]{1,0:T(8,128)(2,1)} %get-tuple-element.60.n2_ref, ...), custom_call_target="tpu_custom_call" | custom-call | tf_op jit(solution)/shard_map/back/pallas_call | solution.py:1260
  213.8 5.8 %unpack.1 = (bf16[1024,256]{1,0:T(8,128)(2,1)}, bf16[1024,256]{1,0:T(8,128)(2,1)}, f32[256]{0:T(256)}, f32[256,1024]{1,0:T(8,128)}, f32[1024,256]{1,0:T(8,128)},...) custom-call(bf16[2048,256]{1,0:T(8,128)(2,1)} %get-tuple-element.55., ...), custom_call_target="tpu_custom_call" | custom-call | tf_op jit(solution)/shard_map/unpack/pallas_call | solution.py:1358

commit v5 on v4

--- a/solution.py
+++ b/solution.py
@@ -91,15 +91,6 @@
     return (frame - start).astype(F32)
 
 
-def block_bounds(first, count, ends, length):
-    low, high = 0, length
-    for end in ends:
-        low = jnp.where(first >= end, end, low)
-    for end in reversed(ends):
-        high = jnp.where(first + count - 1 < end, end, high)
-    return low, high
-
-
 def onehot_rows(segment, items, other, same):
     row = lax.broadcasted_iota(I32, (16, segment.shape[1]), 0)
     return jnp.where(row <= items, jnp.where(row == segment, same, other), 0.0)
@@ -133,37 +124,81 @@
     return 2 * s * c, 1 - 2 * s * s
 
 
+def split_rows(value):
+    row = lax.broadcasted_iota(I32, (16, value.shape[1]), 0)
+    first = value.astype(BF16).astype(F32)
+    second = (value - first).astype(BF16).astype(F32)
+    third = value - first - second
+    picked = jnp.where(row == 0, first, jnp.where(row == 1, second, third))
+    return jnp.where(row < 3, picked, 0.0).astype(BF16)
+
+
+def first_rows(count, columns):
+    row = lax.broadcasted_iota(I32, (16, columns), 0)
+    return jnp.where(row < count, 1.0, 0.0).astype(BF16)
+
+
+def query_rows(query, segment, items, shift):
+    pad = jnp.zeros((query.shape[0] - 32, query.shape[1]), BF16)
+    return jnp.concatenate([query, onehot_rows(segment, items, 0.0, 1.0).astype(BF16), split_rows(shift), pad], axis=0)
+
+
+def key_rows(key, segment, items):
+    pad = jnp.zeros((key.shape[0] - 32, key.shape[1]), BF16)
+    return jnp.concatenate(
+        [key, onehot_rows(segment, items, NEG, 0.0).astype(BF16), first_rows(3, key.shape[1]), pad], axis=0
+    )
+
+
+def lay_queries(near, slot, frames, first, ends, items, dim, qa, lse):
+    cols = slice(slot * frames, (slot + 1) * frames)
+    segment = segment_row(first, frames, ends)
+    for h in range(2):
+        query = near[slot, h * dim : (h + 1) * dim, :]
+        key = near[slot, (2 + h) * dim : (3 + h) * dim, :]
+        own = jnp.sum(query.astype(F32) * key.astype(F32), axis=0, keepdims=True)
+        lse[h : h + 1, cols] = own
+        qa[h, :, cols] = query_rows(query, segment, items, -own)
+
+
+def lay_keys(key, value, rows, first, ends, items, h, ka, va):
+    dim, count = key.shape
+    ka[h, rows, :] = key_rows(key, segment_row(first, count, ends), items).T
+    va[h, 0:dim, rows] = value
+    va[h, dim:, rows] = first_rows(1, count)
+
+
 def front_kernel(
-    sp, items, chunk, len_ref, tok, gain1, w_in, w_out, gain2, w_qkv, freq,
-    x1_ref, n2_ref, trig, heads, parts, turned, send, recv, local,
+    items, chunk, block, len_ref, tok, gain1, w_in, w_out, gain2, w_qkv, freq,
+    x1_ref, n2_ref, trig, act, slope, near, far, ctx, o_ref, lse, flag,
+    parts, turned, qa, ka, va, acc, send, recv,
 ):
     me = lax.axis_index("sp")
-    frames = tok.shape[0]
-    width = tok.shape[1]
+    core, pair = lax.rem(me, 2), me // 2
+    frames, width = tok.shape
     half = trig.shape[0] // 2
-    peers = sp_peers(sp)
+    dim = 2 * half
+    count = frames // chunk
+    peers = [peer_at(mask, 0) for mask in (1, 2, 3)]
     greet(peers)
     turned[...] = w_qkv[...].T
     ends = ends_of(len_ref, items)
-    scale = float(np.log2(np.e)) * (2 * half) ** -0.5
+    scale = float(np.log2(np.e)) * dim**-0.5
 
     def copies(c):
         cols = rows_at(c, chunk)
-        out = [
+        ways = (
+            (parts.at[1 - core, :, cols], near.at[core, :, cols]),
+            (parts.at[core, 2 * dim :, cols], far.at[core, :, cols]),
+            (parts.at[1 - core, 2 * dim :, cols], far.at[core, :, cols]),
+        )
+        return [
             pltpu.make_async_remote_copy(
-                src_ref=parts.at[peer[1], :, cols],
-                dst_ref=heads.at[:, frame_cols(me, frames, c, chunk)],
-                send_sem=send.at[i, c],
-                recv_sem=recv.at[i, c],
-                device_id=peer,
-                device_id_type=MESH,
+                src_ref=source, dst_ref=target, send_sem=send.at[i, c], recv_sem=recv.at[i, c],
+                device_id=peers[i], device_id_type=MESH,
             )
-            for i, peer in enumerate(peers)
+            for i, (source, target) in enumerate(ways)
         ]
-        own = pltpu.make_async_copy(
-            parts.at[me, :, cols], heads.at[:, frame_cols(me, frames, c, chunk)], local.at[c]
-        )
-        return out, own
 
     def step(c, carry):
         rows = rows_at(c, chunk)
@@ -171,7 +206,10 @@
         hat, _ = norm_parts(x)
         n1 = (hat * row_of(gain1)).astype(BF16)
         a = dg(n1, w_in[...], 1, 0)
-        s = (a * sigmoid(a)).astype(BF16)
+        sig = sigmoid(a)
+        s = (a * sig).astype(BF16)
+        act[rows, :] = s
+        slope[rows, :] = (sig * (1.0 + a * (1.0 - sig))).astype(BF16)
         x1 = x + 0.5 * dg(s, w_out[...], 1, 0)
         x1_ref[rows, :] = x1
         hat, _ = norm_parts(x1)
@@ -183,63 +221,121 @@
         )
         trig[0:half, rows] = sine
         trig[half:, rows] = cosine
-        for head in range(sp):
-            base = head * 2 * half
-            for part, factor in ((0, scale), (1, 1.0)):
-                low = part * width + base
-                first, second = joined[low : low + half], joined[low + half : low + 2 * half]
-                low = part * 2 * half
-                parts[head, low : low + half, rows] = ((first * cosine - second * sine) * factor).astype(BF16)
-                parts[head, low + half : low + 2 * half, rows] = (
-                    (first * sine + second * cosine) * factor
-                ).astype(BF16)
-            low = 2 * width + base
-            parts[head, 4 * half : 6 * half, rows] = joined[low : low + 2 * half].astype(BF16)
+        for p in range(2):
+            for j in range(2):
+                for part, factor in ((0, scale), (1, 1.0)):
+                    low = part * width + (2 * p + j) * dim
+                    first, second = joined[low : low + half], joined[low + half : low + dim]
+                    low = (2 * part + j) * dim
+                    parts[p, low : low + half, rows] = ((first * cosine - second * sine) * factor).astype(BF16)
+                    parts[p, low + half : low + dim, rows] = (
+                        (first * sine + second * cosine) * factor
+                    ).astype(BF16)
+                low = 2 * width + (2 * p + j) * dim
+                parts[p, (4 + j) * dim : (5 + j) * dim, rows] = joined[low : low + dim].astype(BF16)
 
         @pl.when(c == 0)
         def _():
             await_greetings(peers)
 
-        out, own = copies(c)
-        for copy in out:
+        for copy in copies(c):
             copy.start()
-        own.start()
-        return carry
-
-    lax.fori_loop(0, frames // chunk, step, 0)
-
-    def finish(c, carry):
-        out, own = copies(c)
-        for copy in out:
+        near[core, :, rows] = parts[core, :, rows]
+        return carry
+
+    lax.fori_loop(0, count, step, 0)
+
+    def near_arrives(c, carry):
+        copies(c)[0].wait()
+        return carry
+
+    lax.fori_loop(0, count, near_arrives, 0)
+    reach = 2 * frames
+    for slot in range(2):
+        first = (2 * pair + slot) * frames
+        lay_queries(near, slot, frames, first, ends, items, dim, qa, lse)
+        for h in range(2):
+            lay_keys(
+                near[slot, (2 + h) * dim : (3 + h) * dim, :], near[slot, (4 + h) * dim : (5 + h) * dim, :],
+                slice(slot * frames, (slot + 1) * frames), first, ends, items, h, ka, va,
+            )
+
+    def near_step(i, carry):
+        h, cols = i // (reach // block), rows_at(lax.rem(i, reach // block), block)
+        powers = jnp.exp2(dg(ka[h, 0:reach, :], qa[h, :, cols], 1, 0)).astype(BF16)
+        acc[h, :, cols] = dg(va[h, :, 0:reach], powers, 1, 0)
+        return carry
+
+    lax.fori_loop(0, 2 * reach // block, near_step, 0)
+    wide = min(1024, reach)
+
+    def far_step(c, carry):
+        for copy in copies(c)[1:]:
             copy.wait()
-        own.wait()
-        return carry
-
-    lax.fori_loop(0, frames // chunk, finish, 0)
-
-
-def front(lengths, tok, gain1, w_in, w_out, gain2, w_qkv, freq, sp):
+        cols = rows_at(c, chunk)
+        for slot in range(2):
+            first = (2 * (1 - pair) + slot) * frames + c * chunk
+            rows = pl.ds(pl.multiple_of(reach + (2 * c + slot) * chunk, chunk), chunk)
+            for h in range(2):
+                lay_keys(
+                    far[slot, h * dim : (h + 1) * dim, cols], far[slot, (2 + h) * dim : (3 + h) * dim, cols],
+                    rows, first, ends, items, h, ka, va,
+                )
+        rows = pl.ds(pl.multiple_of(reach + 2 * c * chunk, 2 * chunk), 2 * chunk)
+
+        def inner(i, carry):
+            h, cols = i // (reach // wide), rows_at(lax.rem(i, reach // wide), wide)
+            powers = jnp.exp2(dg(ka[h, rows, :], qa[h, :, cols], 1, 0)).astype(BF16)
+            acc[h, :, cols] += dg(va[h, :, rows], powers, 1, 0)
+            return carry
+
+        return lax.fori_loop(0, 2 * reach // wide, inner, carry)
+
+    lax.fori_loop(0, count, far_step, 0)
+    bad = jnp.zeros((1, reach), F32)
+    for h in range(2):
+        total = acc[h, dim : dim + 1, :]
+        value = acc[h, 0:dim, :] / total
+        ctx[h] = value.astype(BF16)
+        o_ref[h] = value
+        lse[h : h + 1, :] = lse[h : h + 1, :] + jnp.log2(total)
+        bad = jnp.maximum(bad, jnp.where(total < 2.0**60, 0.0, 1.0))
+    flag[...] = jnp.broadcast_to(jnp.max(bad, axis=1, keepdims=True), flag.shape)
+
+
+def front(lengths, tok, gain1, w_in, w_out, gain2, w_qkv, freq):
     frames, width = tok.shape
+    wide = w_in.shape[1]
     chunk = min(256, frames)
     count = frames // chunk
-    head_width = w_qkv.shape[1] // sp
-    half = freq.shape[0]
+    dim = width // HEADS
+    reach = 2 * frames
     return pl.pallas_call(
-        functools.partial(front_kernel, sp, lengths.shape[1], chunk),
+        functools.partial(front_kernel, lengths.shape[1], chunk, min(512, reach)),
         out_shape=[
             jax.ShapeDtypeStruct((frames, width), F32),
             jax.ShapeDtypeStruct((frames, width), BF16),
-            jax.ShapeDtypeStruct((2 * half, frames), F32),
-            jax.ShapeDtypeStruct((head_width, sp * frames), BF16),
+            jax.ShapeDtypeStruct((dim, frames), F32),
+            jax.ShapeDtypeStruct((frames, wide), BF16),
+            jax.ShapeDtypeStruct((frames, wide), BF16),
+            jax.ShapeDtypeStruct((2, 6 * dim, frames), BF16),
+            jax.ShapeDtypeStruct((2, 4 * dim, frames), BF16),
+            jax.ShapeDtypeStruct((2, dim, reach), BF16),
+            jax.ShapeDtypeStruct((2, dim, reach), F32),
+            jax.ShapeDtypeStruct((2, reach), F32),
+            jax.ShapeDtypeStruct((8, 128), F32),
         ],
         in_specs=[SMEM] + [VMEM] * 7,
-        out_specs=[VMEM] * 4,
+        out_specs=[VMEM] * 11,
         scratch_shapes=[
-            pltpu.VMEM((sp, head_width, frames), BF16),
+            pltpu.VMEM((2, 6 * dim, frames), BF16),
             pltpu.VMEM((3 * width, width), BF16),
-            DMA((sp - 1, count)),
-            DMA((sp - 1, count)),
-            DMA((count,)),
+            pltpu.VMEM((2, 2 * dim, reach), BF16),
+            pltpu.VMEM((2, 2 * reach, 2 * dim), BF16),
+            pltpu.VMEM((2, dim + 16, 2 * reach), BF16),
+            pltpu.VMEM((2, dim + 16, reach), F32),
+            DMA((3, count)),
+            DMA((3, count)),
         ],
         compiler_params=pltpu.CompilerParams(
             collective_id=0, has_side_effects=True, vmem_limit_bytes=VMEM_LIMIT
@@ -248,222 +344,96 @@
     )(lengths, tok, gain1, w_in, w_out, gain2, w_qkv, freq)
 
 
-def split_rows(value):
-    row = lax.broadcasted_iota(I32, (16, value.shape[1]), 0)
-    first = value.astype(BF16).astype(F32)
-    second = (value - first).astype(BF16).astype(F32)
-    third = value - first - second
-    picked = jnp.where(row == 0, first, jnp.where(row == 1, second, third))
-    return jnp.where(row < 3, picked, 0.0).astype(BF16)
-
-
-def first_rows(count, columns):
-    row = lax.broadcasted_iota(I32, (16, columns), 0)
-    return jnp.where(row < count, 1.0, 0.0).astype(BF16)
-
-
-def in_pieces(low, high, sizes, body, carry):
-    for size in sizes:
-        pieces = (high - low) // size
-        carry = lax.fori_loop(
-            0, pieces, lambda i, c, low=low, size=size: body(pl.multiple_of(low + i * size, sizes[-1]), size, c), carry
-        )
-        low = low + pieces * size
-    return carry
-
-
-def over_blocks(len_ref, ends, items, length, outer, sizes, body):
-    unit = sizes[-1]
-    start, stop, longest = 0, ends[0], len_ref[0, 0]
-    for item in range(1, items):
-        more = len_ref[0, item] > longest
-        start = jnp.where(more, ends[item - 1], start)
-        stop = jnp.where(more, ends[item], stop)
-        longest = jnp.where(more, len_ref[0, item], longest)
-    start, stop = start // unit * unit, (stop + unit - 1) // unit * unit
-
-    def part(index, carry):
-        low = jnp.where(index == 0, 0, jnp.where(index == 1, start, stop))
-        high = jnp.where(index == 0, start, jnp.where(index == 1, stop, length))
-
-        def block(at, size, carry):
-            first, last = block_bounds(at, size, ends, length)
-            body(at, size, first // unit * unit, (last + unit - 1) // unit * unit)
+def repair_kernel(
+    items, block, len_ref, flag, near_hbm, far_hbm, ctx_in, o_in, lse_in, ctx_hbm, o_hbm, lse_hbm,
+    near, far, ctx, o_ref, lse, qa, ka, va, sems,
+):
+    @pl.when(jnp.max(flag[...]) > 0.5)
+    def _():
+        pair = lax.axis_index("sp") // 2
+        frames, dim = near.shape[2], near.shape[1] // 6
+        reach = 2 * frames
+        ends = ends_of(len_ref, items)
+        loads = [
+            pltpu.make_async_copy(near_hbm, near, sems.at[0]),
+            pltpu.make_async_copy(far_hbm, far, sems.at[1]),
+        ]
+        for copy in loads:
+            copy.start()
+        for copy in loads:
+            copy.wait()
+        for slot in range(2):
+            first, other = (2 * pair + slot) * frames, (2 * (1 - pair) + slot) * frames
+            lay_queries(near, slot, frames, first, ends, items, dim, qa, lse)
+            for h in range(2):
+                lay_keys(
+                    near[slot, (2 + h) * dim : (3 + h) * dim, :], near[slot, (4 + h) * dim : (5 + h) * dim, :],
+                    slice(slot * frames, (slot + 1) * frames), first, ends, items, h, ka, va,
+                )
+                lay_keys(
+                    far[slot, h * dim : (h + 1) * dim, :], far[slot, (2 + h) * dim : (3 + h) * dim, :],
+                    slice(reach + slot * frames, reach + (slot + 1) * frames), other, ends, items, h, ka, va,
+                )
+
+        def step(i, carry):
+            h, cols = i // (reach // block), rows_at(lax.rem(i, reach // block), block)
+            query = qa[h, :, cols]
+
+            def highest(j, top):
+                scores = dg(ka[h, rows_at(j, block), :], query, 1, 0)
+                return jnp.maximum(top, jnp.max(scores, axis=0, keepdims=True))
+
+            top = lax.fori_loop(0, 2 * reach // block, highest, jnp.zeros((1, block), F32))
+
+            def add(j, total):
+                rows = rows_at(j, block)
+                powers = jnp.exp2(dg(ka[h, rows, :], query, 1, 0) - top).astype(BF16)
+                return total + dg(va[h, :, rows], powers, 1, 0)
+
+            total = lax.fori_loop(0, 2 * reach // block, add, jnp.zeros((dim + 16, block), F32))
+            value = total[0:dim, :] / total[dim : dim + 1, :]
+            ctx[h, :, cols] = value.astype(BF16)
+            o_ref[h, :, cols] = value
+            change = top + jnp.log2(total[dim : dim + 1, :])
+            row = lax.broadcasted_iota(I32, (2, block), 0)
+            lse[:, cols] = lse[:, cols] + jnp.where(row == h, change, 0.0)
             return carry
 
-        return in_pieces(low, high, outer, block, carry)
-
-    lax.fori_loop(0, 3, part, 0)
-
-
-def attend_kernel(items, outer, sizes, len_ref, x_ref, ctx_ref, o_ref, lse_ref, qa, ka, va):
-    dim, length = x_ref.shape[0] // 3, x_ref.shape[1]
-    ends = ends_of(len_ref, items)
-    frames = min(1024, length)
-    pad = jnp.zeros((dim - 32, frames), BF16)
-    for first in range(0, length, frames):
-        cols = slice(first, first + frames)
-        segment = segment_row(first, frames, ends)
-        query, key = x_ref[0:dim, cols], x_ref[dim : 2 * dim, cols]
-        own = jnp.sum(query.astype(F32) * key.astype(F32), axis=0, keepdims=True)
-        lse_ref[:, cols] = own
-        qa[0:dim, cols] = query
-        qa[dim : dim + 16, cols] = onehot_rows(segment, items, 0.0, 1.0).astype(BF16)
-        qa[dim + 16 : dim + 32, cols] = split_rows(-own)
-        qa[dim + 32 :, cols] = pad
-        ka[cols, :] = jnp.concatenate(
-            [key, onehot_rows(segment, items, NEG, 0.0).astype(BF16), first_rows(3, frames), pad], axis=0
-        ).T
-        va[0:dim, cols] = x_ref[2 * dim :, cols]
-        va[dim:, cols] = first_rows(1, frames)
-
-    def block_step(start, block, low, high):
-        where = pl.ds(start, block)
-        query = qa[:, where]
-
-        def piece(at, size, acc):
-            powers = jnp.exp2(dg(ka[pl.ds(at, size), :], query, 1, 0)).astype(BF16)
-            return acc + dg(va[:, pl.ds(at, size)], powers, 1, 0)
-
-        def store(acc, shift):
-            total = acc[dim : dim + 1, :]
-            value = acc[0:dim, :] / total
-            ctx_ref[:, where] = value.astype(BF16)
-            o_ref[:, where] = value
-            lse_ref[:, where] = shift + jnp.log2(total)
-
-        acc = in_pieces(low, high, sizes, piece, jnp.zeros((dim + 16, block), F32))
-        own = lse_ref[:, where]
-        store(acc, own)
-        fits = jnp.min(jnp.where(acc[dim : dim + 1, :] < 2.0**60, 1.0, 0.0)) > 0.5
-
-        @pl.when(jnp.logical_not(fits))
-        def _():
-            def maximum(at, size, top):
-                return jnp.maximum(top, jnp.max(dg(ka[pl.ds(at, size), :], query, 1, 0), axis=0, keepdims=True))
-
-            top = in_pieces(low, high, sizes[-1:], maximum, jnp.zeros((1, block), F32))
-
-            def careful(at, size, acc):
-                powers = jnp.exp2(dg(ka[pl.ds(at, size), :], query, 1, 0) - top).astype(BF16)
-                return acc + dg(va[:, pl.ds(at, size)], powers, 1, 0)
-
-            store(in_pieces(low, high, sizes[-1:], careful, jnp.zeros((dim + 16, block), F32)), own + top)
-
-    over_blocks(len_ref, ends, items, length, outer, sizes, block_step)
-
-
-def attend(x, lengths, outer=(1024, 512, 256), sizes=(2048, 1024, 512, 256)):
-    rows, length = x.shape
-    dim = rows // 3
+        lax.fori_loop(0, 2 * reach // block, step, 0)
+        stores = [
+            pltpu.make_async_copy(ctx, ctx_hbm, sems.at[2]),
+            pltpu.make_async_copy(o_ref, o_hbm, sems.at[3]),
+            pltpu.make_async_copy(lse, lse_hbm, sems.at[4]),
+        ]
+        for copy in stores:
+            copy.start()
+        for copy in stores:
+            copy.wait()
+
+
+def repair(lengths, flag, near, far, ctx, o, lse):
+    dim, reach = ctx.shape[1:]
+    anywhere = pl.BlockSpec(memory_space=pl.ANY)
     return pl.pallas_call(
-        functools.partial(attend_kernel, lengths.shape[1], outer, sizes),
-        out_shape=[
-            jax.ShapeDtypeStruct((dim, length), BF16),
-            jax.ShapeDtypeStruct((dim, length), F32),
-            jax.ShapeDtypeStruct((1, length), F32),
-        ],
-        in_specs=[SMEM, VMEM],
-        out_specs=[VMEM] * 3,
+        functools.partial(repair_kernel, lengths.shape[1], min(512, reach)),
+        out_shape=[jax.ShapeDtypeStruct(x.shape, x.dtype) for x in (ctx, o, lse)],
+        in_specs=[SMEM, VMEM] + [anywhere] * 5,
+        out_specs=[anywhere] * 3,
+        input_output_aliases={4: 0, 5: 1, 6: 2},
         scratch_shapes=[
-            pltpu.VMEM((2 * dim, length), BF16),
-            pltpu.VMEM((length, 2 * dim), BF16),
-            pltpu.VMEM((dim + 16, length), BF16),
+            pltpu.VMEM(near.shape, BF16),
+            pltpu.VMEM(far.shape, BF16),
+            pltpu.VMEM(ctx.shape, BF16),
+            pltpu.VMEM(o.shape, F32),
+            pltpu.VMEM(lse.shape, F32),
+            pltpu.VMEM((2, 2 * dim, reach), BF16),
+            pltpu.VMEM((2, 2 * reach, 2 * dim), BF16),
+            pltpu.VMEM((2, dim + 16, 2 * reach), BF16),
+            DMA((5,)),
         ],
         compiler_params=pltpu.CompilerParams(vmem_limit_bytes=VMEM_LIMIT),
-        name="attend",
-    )(lengths, x)
-
-
-def attend_back_kernel(
-    items, outer, sizes, sub, len_ref, x_ref, o_ref, lse_ref, do_ref, g_ref, qa, ka, da, va, dq, dk, dv
-):
-    dim, length = x_ref.shape[0] // 3, x_ref.shape[1]
-    ends = ends_of(len_ref, items)
-    frames = min(1024, length)
-    pad, wide_pad = jnp.zeros((dim - 32, frames), BF16), jnp.zeros((dim - 16, frames), BF16)
-    for first in range(0, length, frames):
-        cols = slice(first, first + frames)
-        segment = segment_row(first, frames, ends)
-        qa[cols, :] = jnp.concatenate(
-            [
-                x_ref[0:dim, cols],
-                onehot_rows(segment, items, 0.0, 1.0).astype(BF16),
-                split_rows(-lse_ref[:, cols]),
-                pad,
-            ],
-            axis=0,
-        ).T
-        ka[0:dim, cols] = x_ref[dim : 2 * dim, cols]
-        ka[dim : dim + 16, cols] = onehot_rows(segment, items, NEG, 0.0).astype(BF16)
-        ka[dim + 16 : dim + 32, cols] = first_rows(3, frames)
-        ka[dim + 32 :, cols] = pad
-        grad = do_ref[:, cols]
-        row_dot = jnp.sum(grad.astype(F32) * o_ref[:, cols], axis=0, keepdims=True)
-        da[cols, :] = jnp.concatenate([grad, split_rows(-row_dot), wide_pad], axis=0).T
-        va[0:dim, cols] = x_ref[2 * dim :, cols]
-        va[dim : dim + 16, cols] = first_rows(3, frames)
-        va[dim + 16 :, cols] = wide_pad
-        dq[:, cols] = jnp.zeros((dim, frames), F32)
-
-    def block_step(start, block, low, high):
-        where = pl.ds(start, block)
-        dk[...] = jnp.zeros_like(dk)
-        dv[...] = jnp.zeros_like(dv)
-
-        def piece(at, size, carry):
-            rows = pl.ds(at, size)
-
-            def score(u):
-                cols = pl.ds(pl.multiple_of(start + u * sub, sub), sub)
-                return dg(qa[rows, :], ka[:, cols], 1, 0), dg(da[rows, :], va[:, cols], 1, 0)
-
-            count = block // sub
-            grads = []
-            ready = score(0)
-            for u in range(count):
-                scores, grad_probs = ready
-                if u + 1 < count:
-                    ready = score(u + 1)
-                probs = jnp.exp2(scores)
-                grad = (probs * grad_probs).astype(BF16)
-                cols = slice(u * sub, (u + 1) * sub)
-                dv[:, cols] += dg(do_ref[:, rows], probs.astype(BF16), 1, 0)
-                dk[:, cols] += dg(x_ref[0:dim, rows], grad, 1, 0)
-                grads.append(grad)
-            dq[:, rows] += dg(ka[0:dim, where], jnp.concatenate(grads, axis=1), 1, 1)
-            return carry
-
-        in_pieces(low, high, sizes, piece, 0)
-        g_ref[dim : 2 * dim, where] = (dk[:, 0:block] * LN2).astype(BF16)
-        g_ref[2 * dim :, where] = dv[:, 0:block].astype(BF16)
-
-    over_blocks(len_ref, ends, items, length, outer, sizes, block_step)
-    for first in range(0, length, frames):
-        cols = slice(first, first + frames)
-        g_ref[0:dim, cols] = (dq[:, cols] * dim**-0.5).astype(BF16)
-
-
-def attend_back(x, lengths, o, lse, do, outer=(512, 256), sizes=(2048, 1024, 512, 256), sub=256):
-    rows, length = x.shape
-    dim = rows // 3
-    return pl.pallas_call(
-        functools.partial(attend_back_kernel, lengths.shape[1], outer, sizes, sub),
-        out_shape=jax.ShapeDtypeStruct(x.shape, BF16),
-        in_specs=[SMEM] + [VMEM] * 4,
-        out_specs=VMEM,
-        scratch_shapes=[
-            pltpu.VMEM((length, 2 * dim), BF16),
-            pltpu.VMEM((2 * dim, length), BF16),
-            pltpu.VMEM((length, 2 * dim), BF16),
-            pltpu.VMEM((2 * dim, length), BF16),
-            pltpu.VMEM((dim, length), F32),
-            pltpu.VMEM((dim, outer[0]), F32),
-            pltpu.VMEM((dim, outer[0]), F32),
-        ],
-        compiler_params=pltpu.CompilerParams(vmem_limit_bytes=VMEM_LIMIT),
-        name="attend_back",
-    )(lengths, x, o, lse, do)
+        name="repair",
+    )(lengths, flag, near, far, ctx, o, lse)
 
 
 def axis_steps(axis):
@@ -519,12 +489,17 @@
 class Reduction:
     def __init__(self, base, rows, staged, stages, acc, stage, land, full, send, recv):
         self.stages, self.acc, self.stage, self.land, self.full = stages, acc, stage, land, full
-        self.send, self.recv, self.low = send, recv, base
+        self.send, self.recv, self.base = send, recv, base
         self.sizes, _, self.own = exchange_plan(rows, stages, staged)
         self.first_sem = [sum((1 << len(s)) - 1 for s in stages[:k]) for k in range(len(stages))]
 
     def at(self, low, size):
         return pl.ds(pl.multiple_of(low, 16), size)
+
+    def low(self, k):
+        return self.base + sum(
+            place_in(self.stages[j], 0) * self.sizes[j][1] for j in range(k) if self.sizes[j][0]
+        )
 
     def slot(self, k, i):
         _, size, offset = self.sizes[k]
@@ -538,7 +513,7 @@
                 source = self.stage.at[self.slot(k, i if splits else 0), :]
                 target = self.land.at[self.slot(k, i), :]
             else:
-                source = target = self.full.at[self.at(self.low, size), :]
+                source = target = self.full.at[self.at(self.low(k + 1), size), :]
             out.append(
                 pltpu.make_async_remote_copy(
                     src_ref=source,
@@ -556,10 +531,10 @@
         copies = self.copies(0, k)
         for i, copy in enumerate(copies):
             if splits:
-                away = self.low + place_in(self.stages[k], i + 1) * size
+                away = self.low(k) + place_in(self.stages[k], i + 1) * size
                 self.stage[self.slot(k, i), :] = self.acc[self.at(away, size), :].astype(BF16)
             elif i == 0:
-                self.stage[self.slot(k, 0), :] = self.acc[self.at(self.low, size), :].astype(BF16)
+                self.stage[self.slot(k, 0), :] = self.acc[self.at(self.low(k), size), :].astype(BF16)
             copy.start()
 
     def sum_recv(self, k):
@@ -569,16 +544,15 @@
             copy.wait()
         values = [self.land[self.slot(k, i), :].astype(F32) for i in range(len(copies))]
         if splits:
-            self.low = self.low + place_in(self.stages[k], 0) * size
-            values = [self.acc[self.at(self.low, size), :]] + values
+            values = [self.acc[self.at(self.low(k + 1), size), :]] + values
         else:
             values = [self.stage[self.slot(k, 0), :].astype(F32)] + values
         while len(values) > 1:
             values = [values[i] + values[i + 1] for i in range(0, len(values), 2)]
-        self.acc[self.at(self.low, size), :] = values[0]
+        self.acc[self.at(self.low(k + 1), size), :] = values[0]
 
     def close(self):
-        where = self.at(self.low, self.own)
+        where = self.at(self.low(len(self.stages)), self.own)
         self.full[where, :] = self.acc[where, :].astype(BF16)
 
     def share_send(self, k):
@@ -587,11 +561,9 @@
                 copy.start()
 
     def share_recv(self, k):
-        splits, size, _ = self.sizes[k]
-        if splits:
+        if self.sizes[k][0]:
             for copy in self.copies(1, k):
                 copy.wait()
-            self.low = self.low - place_in(self.stages[k], 0) * size
 
 
 def advance(streams, position):
@@ -659,12 +631,11 @@
 def middle_kernel(
     sp, dp, items, taps, chunk, block, len_ref, parts, x1_ref, cot, gain3, gain4, gain5, w_out, w_point1,
     depthwise, bn_gain, bn_bias, w_point2, w_in, w_down,
-    out_ref, grad_x2, heads, mid, point_two, bn_grads, full,
+    out_ref, grad_x2, heads, mid, point_two, bn_grads, two,
     ctx, x2_ref, n3_keep, point, glu, conv, low_lim, high_lim, act, hidden, n4_keep, branch, swish, branch2,
     grad_x3, grad_y, grad_conv, grad_glu, grad_point, branch3, back_parts, tap_sums, edge_out, edge_in,
-    send_box, near_box, far_box, sums, acc, stage, land,
+    send_box, near_box, far_box, sums,
     send, recv, local, back_send, back_recv, back_local, rim_send, rim_recv, box_send, box_recv,
-    sum_send, sum_recv,
 ):
     me, me_dp = lax.axis_index("sp"), lax.axis_index("dp")
     frames, width = x1_ref.shape
@@ -673,9 +644,9 @@
     count = frames // chunk
     peers = sp_peers(sp)
     far_peers = [peer_at(0, mask) for mask in range(1, dp)]
-    masks = all_masks(sp)
-    masks += [(0, mask) for mask in range(1, dp) if (0, mask) not in masks]
-    greeted = [peer_at(*mask) for mask in masks]
+    greeted = peers + far_peers
+    core = lax.rem(me, 2)
+    sibling = peer_at(1, 0)
     length = sp * frames
     ends = ends_of(len_ref, items)
     first_frame = me * frames
@@ -705,24 +676,20 @@
     await_greetings(greeted)
 
     def moves(c, source, target, send_sems, recv_sems, local_sems):
-        out = [
+        return [
             pltpu.make_async_remote_copy(
-                src_ref=source(peer[1], c),
-                dst_ref=target(me, c),
-                send_sem=send_sems.at[i, c],
-                recv_sem=recv_sems.at[i, c],
-                device_id=peer,
-                device_id_type=MESH,
-            )
-            for i, peer in enumerate(peers)
+                src_ref=source(1 - core, c), dst_ref=target(core, c),
+                send_sem=send_sems.at[c], recv_sem=recv_sems.at[c],
+                device_id=sibling, device_id_type=MESH,
+            ),
+            pltpu.make_async_copy(source(core, c), target(core, c), local_sems.at[c]),
         ]
-        return out + [pltpu.make_async_copy(source(me, c), target(me, c), local_sems.at[c])]
 
     def by_frames(ref):
-        return lambda device, c: ref.at[:, frame_cols(device, frames, c, chunk)]
+        return lambda slot, c: ref.at[:, :, frame_cols(slot, frames, c, chunk)]
 
     def by_head(ref):
-        return lambda device, c: ref.at[device, :, rows_at(c, chunk)]
+        return lambda slot, c: ref.at[slot, :, :, rows_at(c, chunk)]
 
     def context_moves(c):
         return moves(c, by_frames(parts), by_head(ctx), send, recv, local)
@@ -738,7 +705,7 @@
         rows = rows_at(c, chunk)
         for copy in context_moves(c):
             copy.wait()
-        context = ctx[:, :, rows].reshape(width, chunk)
+        context = ctx[:, :, :, rows].reshape(width, chunk)
         x2 = x1_ref[rows, :] + dg(context, w_out[...], 0, 0)
         x2_ref[rows, :] = x2
         hat, _ = norm_parts(x2)
@@ -926,21 +893,13 @@
     )
     swap_rims(1, *grad_rims)
     wide = w_in.shape[1]
-    streams = make_streams(
-        [(0, wide, 0), (wide, wide, 1)], acc, stage, land, full, sum_send, sum_recv
-    )
-    steps = len(stage_plans()[0])
     for j in range(0, wide, width):
-        acc[j : j + width, :] = dg(act[:, j : j + width], branch[...], 0, 0)
-    advance(streams[:1], 0)
+        two[j : j + width, :] = dg(act[:, j : j + width], branch[...], 0, 0).astype(BF16)
     pair = box_end(1, 0, pair, total)
     box_begin(1, 1, pair)
     for j in range(0, wide, width):
-        acc[wide + j : wide + j + width, :] = dg(n4_keep[...], hidden[:, j : j + width], 0, 0)
-    advance(streams[1:], 0)
-    advance(streams[:1], 1)
+        two[wide + j : wide + j + width, :] = dg(n4_keep[...], hidden[:, j : j + width], 0, 0).astype(BF16)
     point_two[...] = dg(swish[...], branch2[...], 0, 0)
-    advance(streams[1:], 1)
     await_rims(1, *grad_rims)
     bias_sum, gain_sum, _ = box_end(1, 1, pair, total)
     bn_grads[0:1, :] = gain_sum
@@ -994,12 +953,7 @@
             grad_glu[h, rows_at(b, block), :] = result[h]
         return carry
 
-    points = list(range(2, 2 * steps + 1))
-    advance(streams, points.pop(0))
-    lax.fori_loop(0, blocks // 2, conv_back_step, 0)
-    advance(streams, points.pop(0))
-    lax.fori_loop(blocks // 2, blocks, conv_back_step, 0)
-    advance(streams, points.pop(0))
+    lax.fori_loop(0, blocks, conv_back_step, 0)
 
     def back_moves(c):
         return moves(c, by_head(back_parts), by_frames(heads), back_send, back_recv, back_local)
@@ -1017,14 +971,12 @@
         grad_x2[rows, :] = grad2
         low_grad = grad2.astype(BF16)
         branch3[rows, :] = low_grad
-        back_parts[:, :, rows] = dg(w_out[...], low_grad, 1, 1).astype(BF16).reshape(sp, width // sp, chunk)
+        back_parts[:, :, :, rows] = dg(w_out[...], low_grad, 1, 1).astype(BF16).reshape(2, 2, width // 4, chunk)
         for copy in back_moves(c):
             copy.start()
         return carry
 
-    lax.fori_loop(0, count // 2, close_step, 0)
-    advance(streams, points.pop(0))
-    lax.fori_loop(count // 2, count, close_step, 0)
+    lax.fori_loop(0, count, close_step, 0)
     for j in range(2):
         mid[j * width : (j + 1) * width, :] = dg(n3_keep[...], grad_point[:, j * width : (j + 1) * width], 0, 0)
     mid[2 * width : 3 * width, :] = dg(ctx[...].reshape(width, frames), branch3[...], 1, 0)
@@ -1032,8 +984,6 @@
         row = 3 * width + 8 + tap
         for h in range(2):
             mid[row : row + 1, h * lanes : (h + 1) * lanes] = jnp.sum(tap_sums[tap, h], axis=0, keepdims=True)
-    while points:
-        advance(streams, points.pop(0))
 
     def finish(c, carry):
         for copy in back_moves(c):
@@ -1048,20 +998,20 @@
     w_in, w_down, dp,
 ):
     frames, width = x1.shape
-    length = parts.shape[1]
-    sp = length // frames
+    sp = lax.axis_size("sp")
+    assert sp == HEADS == 4
+    paired = pltpu.VMEM((2, 2, width // 4, frames), BF16)
     wide = w_in.shape[1]
     taps = depthwise.shape[0]
     reach = taps // 2
     chunk = min(256, frames)
     count = frames // chunk
     lanes = width // 2
-    staged, sems = reduction_scratch([wide, wide])
     keep, low_keep = pltpu.VMEM((frames, width), F32), pltpu.VMEM((frames, width), BF16)
     split = pltpu.VMEM((2, frames, lanes), F32)
     rimmed = pltpu.VMEM((2, frames + 2 * reach, lanes), F32)
     rims = pltpu.VMEM((2, 3 * reach, width), F32)
-    moves = [DMA((sp - 1, count)), DMA((sp - 1, count)), DMA((count,))]
+    moves = [DMA((count,)), DMA((count,)), DMA((count,))]
     return pl.pallas_call(
         functools.partial(middle_kernel, sp, dp, lengths.shape[1], taps, chunk, 32),
         out_shape=[
@@ -1076,7 +1026,7 @@
         in_specs=[SMEM, pl.BlockSpec(memory_space=pl.ANY)] + [VMEM] * 13,
         out_specs=[VMEM] * 7,
         scratch_shapes=[
-            pltpu.VMEM((sp, width // sp, frames), BF16),
+            paired,
             keep,
             low_keep,
             pltpu.VMEM((frames, 2 * width), F32),
@@ -1096,7 +1046,7 @@
             split,
             pltpu.VMEM((frames, 2 * width), BF16),
             low_keep,
-            pltpu.VMEM((sp, width // sp, frames), BF16),
+            paired,
             pltpu.VMEM((taps, 2, 8, lanes), F32),
             rims,
             rims,
@@ -1104,13 +1054,10 @@
             pltpu.VMEM((2, sp - 1, 8, width), F32),
             pltpu.VMEM((2, dp - 1, 8, width), F32),
             pltpu.VMEM((8, width), F32),
-            pltpu.VMEM((2 * wide, width), F32),
-            pltpu.VMEM((staged, width), BF16),
-            pltpu.VMEM((staged, width), BF16),
         ]
         + moves
         + moves
-        + [DMA((2, 2)), DMA((2, 2)), DMA((2, sp + dp - 2)), DMA((2, sp + dp - 2)), DMA(sems), DMA(sems)],
+        + [DMA((2, 2)), DMA((2, 2)), DMA((2, sp + dp - 2)), DMA((2, sp + dp - 2))],
         compiler_params=pltpu.CompilerParams(
             collective_id=1, has_side_effects=True, vmem_limit_bytes=VMEM_LIMIT
         ),
@@ -1122,86 +1069,219 @@
 
 
 def back_kernel(
-    sp, chunk, parts, trig, tok, x1_ref, n2_ref, grad_x2, gain1, gain2, w_in, w_out, w_qkv, mid, point_two,
-    grad_ref, full, heads, joined, n1_keep, hat_keep, branch, act, slope, hidden, grad_x1, gains, acc, stage, land,
-    send, recv, local, sum_send, sum_recv,
+    sp, items, chunk, block, sub, len_ref, near, far, o_ref, lse_ref, do_ref, trig, gain1, gain2, two, mid, point_two,
+    tok_hbm, x1_hbm, n2_hbm, x2_hbm, act_hbm, slope_hbm, w_in_hbm, w_out_hbm, w_qkv_hbm,
+    grad_ref, full,
+    tok, x1_ref, n2_ref, grad_x2, act, slope, w_in, w_out, w_qkv,
+    qa, qt, ka, da, va, dq, far_out, near_out, dq_out, far_kv, near_kv, near_dq,
+    joined, branch, hidden, grad_x1, gains, acc, stage, land,
+    load_sems, far_send, far_recv, near_send, near_recv, sum_send, sum_recv,
 ):
-    me = lax.axis_index("sp")
+    me, dp = lax.axis_index("sp"), lax.axis_index("dp")
+    core, pair = lax.rem(me, 2), me // 2
+    sibling = peer_at(1, 0)
     frames, width = tok.shape
     wide = w_in.shape[1]
     half = trig.shape[0] // 2
     dim = 2 * half
     count = frames // chunk
-    peers = sp_peers(sp)
+    reach = 2 * frames
     greeted = [peer_at(*mask) for mask in all_masks(sp)]
     greet(greeted)
+    loads = [
+        pltpu.make_async_copy(source, target, load_sems.at[i])
+        for i, (source, target) in enumerate(
+            (
+                (x1_hbm, x1_ref), (x2_hbm, grad_x2), (w_qkv_hbm, w_qkv), (n2_hbm, n2_ref), (act_hbm, act),
+                (w_out_hbm, w_out), (slope_hbm, slope), (w_in_hbm, w_in), (tok_hbm, tok),
+            )
+        )
+    ]
+    for copy in loads:
+        copy.start()
     unit = 4 * width
-    last = 4 * unit
+    last = 6 * unit
     streams = make_streams(
-        [(0, unit, 1), (unit, unit, 1), (2 * unit, unit, 0), (3 * unit, unit, 0), (last, 16, 0)],
+        [
+            (0, unit, 1), (unit, unit, 1), (2 * unit, unit, 1),
+            (3 * unit, unit, 1), (4 * unit, unit, 0), (5 * unit, unit, 0), (last, 16, 0),
+        ],
         acc, stage, land, full, sum_send, sum_recv,
     )
-    early, qkv, down, up, rest = ([stream] for stream in streams)
-    acc[0:unit, :] = mid[...]
+    early, (qkv, down, up, rest) = streams[:3], ([stream] for stream in streams[3:])
+    steps = len(stage_plans()[0])
+    acc[0 : 2 * unit, :] = two[...].astype(F32)
+    acc[2 * unit : 3 * unit, :] = mid[...]
     acc[last : last + 16, :] = jnp.zeros((16, width), F32)
     gains[...] = jnp.zeros_like(gains)
+    ends = ends_of(len_ref, items)
+    wide_pad = jnp.zeros((dim - 16, frames), BF16)
+    for slot in range(2):
+        cols = slice(slot * frames, (slot + 1) * frames)
+        far_cols = slice(reach + slot * frames, reach + (slot + 1) * frames)
+        segment = segment_row((2 * pair + slot) * frames, frames, ends)
+        far_segment = segment_row((2 * (1 - pair) + slot) * frames, frames, ends)
+        for h in range(2):
+            query = near[slot, h * dim : (h + 1) * dim, :]
+            qt[h, :, cols] = query
+            qa[h, cols, :] = query_rows(query, segment, items, -lse_ref[h : h + 1, cols]).T
+            grad = do_ref[h, :, cols]
+            row_dot = jnp.sum(grad.astype(F32) * o_ref[h, :, cols], axis=0, keepdims=True)
+            da[h, cols, :] = jnp.concatenate([grad, split_rows(-row_dot), wide_pad], axis=0).T
+            ka[h, :, cols] = key_rows(near[slot, (2 + h) * dim : (3 + h) * dim, :], segment, items)
+            ka[h, :, far_cols] = key_rows(far[slot, h * dim : (h + 1) * dim, :], far_segment, items)
+            for where, value in (
+                (cols, near[slot, (4 + h) * dim : (5 + h) * dim, :]),
+                (far_cols, far[slot, (2 + h) * dim : (3 + h) * dim, :]),
+            ):
+                va[h, 0:dim, where] = value
+                va[h, dim : dim + 16, where] = first_rows(3, frames)
+                va[h, dim + 16 :, where] = wide_pad
+    for h in range(2):
+        dq[h] = jnp.zeros((dim, reach), F32)
     await_greetings(greeted)
 
-    def copies(c):
-        out = [
+    def attend_block(h, at):
+        dk, dv, grads = [], [], []
+
+        def score(u):
+            cols = pl.ds(pl.multiple_of(at + u * sub, sub), sub)
+            return dg(qa[h], ka[h, :, cols], 1, 0), dg(da[h], va[h, :, cols], 1, 0)
+
+        ready = score(0)
+        for u in range(block // sub):
+            scores, grad_probs = ready
+            if u + 1 < block // sub:
+                ready = score(u + 1)
+            probs = jnp.exp2(scores)
+            grad = (probs * grad_probs).astype(BF16)
+            dv.append(dg(do_ref[h], probs.astype(BF16), 1, 0).astype(BF16))
+            dk.append((dg(qt[h], grad, 1, 0) * LN2).astype(BF16))
+            grads.append(grad)
+        dq[h] += dg(ka[h, 0:dim, pl.ds(pl.multiple_of(at, block), block)], jnp.concatenate(grads, axis=1), 1, 1)
+        return jnp.concatenate(dk, axis=1), jnp.concatenate(dv, axis=1)
+
+    per = frames // block
+
+    def keep(ref, slot, h, cols, block_grads):
+        for i, value in enumerate(block_grads):
+            ref[slot, 2 * i + h, :, cols] = value
+
+    def far_copy(b):
+        cols = rows_at(lax.rem(b, per), block)
+        return pltpu.make_async_remote_copy(
+            src_ref=far_out.at[b // per, :, :, cols], dst_ref=far_kv.at[core, :, :, cols],
+            send_sem=far_send.at[b], recv_sem=far_recv.at[core, lax.rem(b, per)],
+            device_id=(dp, 2 * (1 - pair) + b // per), device_id_type=MESH,
+        )
+
+    def far_step(t, carry):
+        b, h = t // 2, lax.rem(t, 2)
+        cols = rows_at(lax.rem(b, per), block)
+        keep(far_out, b // per, h, cols, attend_block(h, reach + b * block))
+
+        @pl.when(h == 1)
+        def _():
+            far_copy(b).start()
+
+        for position in range(steps + 1):
+            @pl.when(t == 1 + position * 2)
+            def _():
+                advance(early, position)
+
+        return carry
+
+    lax.fori_loop(0, 4 * per, far_step, 0)
+
+    def near_copy(b):
+        cols = rows_at(b, block)
+        return pltpu.make_async_remote_copy(
+            src_ref=near_out.at[:, :, cols], dst_ref=near_kv.at[core, :, :, cols],
+            send_sem=near_send.at[b], recv_sem=near_recv.at[b], device_id=sibling, device_id_type=MESH,
+        )
+
+    def sibling_step(t, carry):
+        b, h = t // 2, lax.rem(t, 2)
+        block_grads = attend_block(h, (1 - core) * frames + b * block)
+        for i, value in enumerate(block_grads):
+            near_out[2 * i + h, :, rows_at(b, block)] = value
+
+        @pl.when(h == 1)
+        def _():
+            near_copy(b).start()
+
+        for position in range(steps + 1, 2 * steps):
+            @pl.when(t == 2 * (position - steps - 1))
+            def _():
+                advance(early, position)
+
+        return carry
+
+    lax.fori_loop(0, 2 * per, sibling_step, 0)
+
+    def own_step(t, carry):
+        b, h = t // 2, lax.rem(t, 2)
+        keep(near_kv, core, h, rows_at(b, block), attend_block(h, core * frames + b * block))
+
+        @pl.when(t == 0)
+        def _():
+            advance(early, 2 * steps)
+
+        return carry
+
+    lax.fori_loop(0, 2 * per, own_step, 0)
+    for h in range(2):
+        dq_out[h] = (dq[h, :, pl.ds(pl.multiple_of((1 - core) * frames, frames), frames)] * dim**-0.5).astype(BF16)
+    dq_copy = pltpu.make_async_remote_copy(
+        src_ref=dq_out, dst_ref=near_dq.at[core], send_sem=near_send.at[per], recv_sem=near_recv.at[per],
+        device_id=sibling, device_id_type=MESH,
+    )
+    dq_copy.start()
+    for h in range(2):
+        near_dq[core, h] = (dq[h, :, pl.ds(pl.multiple_of(core * frames, frames), frames)] * dim**-0.5).astype(BF16)
+    for copy in loads:
+        copy.wait()
+    for b in range(2 * per):
+        far_copy(b).wait_send()
+    for source in range(2):
+        for b in range(per):
             pltpu.make_async_remote_copy(
-                src_ref=parts.at[:, frame_cols(peer[1], frames, c, chunk)],
-                dst_ref=heads.at[me, :, rows_at(c, chunk)],
-                send_sem=send.at[i, c],
-                recv_sem=recv.at[i, c],
-                device_id=peer,
-                device_id_type=MESH,
-            )
-            for i, peer in enumerate(peers)
-        ]
-        own = pltpu.make_async_copy(
-            parts.at[:, frame_cols(me, frames, c, chunk)], heads.at[me, :, rows_at(c, chunk)], local.at[c]
-        )
-        return out + [own]
-
-    def begin(c, carry):
-        for copy in copies(c):
-            copy.start()
-        return carry
-
-    lax.fori_loop(0, count, begin, 0)
-    advance(early, 0)
-
-    def again(c, carry):
+                src_ref=far_out.at[0, :, :, rows_at(b, block)], dst_ref=far_kv.at[source, :, :, rows_at(b, block)],
+                send_sem=far_send.at[b], recv_sem=far_recv.at[source, b], device_id=sibling, device_id_type=MESH,
+            ).wait_recv()
+    for b in range(per):
+        near_copy(b).wait()
+
+    def turn_back(first, second, rows, low):
+        sine, cosine = trig[0:half, rows], trig[half:, rows]
+        joined[low : low + half, rows] = (first * cosine + second * sine).astype(BF16)
+        joined[low + half : low + dim, rows] = (second * cosine - first * sine).astype(BF16)
+
+    def keys_step(c, carry):
         rows = rows_at(c, chunk)
-        hat, inv = norm_parts(tok[rows, :].astype(F32))
-        hat_keep[rows, :] = hat
-        n1 = (hat * row_of(gain1)).astype(BF16)
-        n1_keep[rows, :] = n1
-        a = dg(n1, w_in[...], 1, 0)
-        sig = sigmoid(a)
-        act[rows, :] = (a * sig).astype(BF16)
-        slope[rows, :] = sig * (1.0 + a * (1.0 - sig))
-        return carry
-
-    lax.fori_loop(0, count // 2, again, 0)
-    advance(early, 1)
-    lax.fori_loop(count // 2, count, again, 0)
+        for p in range(2):
+            for h in range(2):
+                head = 2 * p + h
+
+                def both(i, low, high):
+                    return near_kv[p, i, low:high, rows].astype(F32) + far_kv[p, i, low:high, rows].astype(F32)
+
+                turn_back(both(h, 0, half), both(h, half, dim), rows, width + head * dim)
+                low = 2 * width + head * dim
+                joined[low : low + dim, rows] = both(2 + h, 0, dim).astype(BF16)
+        return carry
+
+    lax.fori_loop(0, count, keys_step, 0)
+    dq_copy.wait()
 
     def arrive(c, carry):
         rows = rows_at(c, chunk)
-        for copy in copies(c):
-            copy.wait()
-        sine, cosine = trig[0:half, rows], trig[half:, rows]
-        for head in range(sp):
-            for part in range(2):
-                first = heads[head, part * dim : part * dim + half, rows].astype(F32)
-                second = heads[head, part * dim + half : (part + 1) * dim, rows].astype(F32)
-                low = part * width + head * dim
-                joined[low : low + half, rows] = (first * cosine + second * sine).astype(BF16)
-                joined[low + half : low + dim, rows] = (second * cosine - first * sine).astype(BF16)
-            low = 2 * width + head * dim
-            joined[low : low + dim, rows] = heads[head, 2 * dim : 3 * dim, rows]
+        for p in range(2):
+            for h in range(2):
+                turn_back(
+                    near_dq[p, h, 0:half, rows].astype(F32), near_dq[p, h, half:dim, rows].astype(F32), rows,
+                    (2 * p + h) * dim,
+                )
         grad = dg(joined[:, rows], w_qkv[...], 0, 1)
         hat, inv = norm_parts(x1_ref[rows, :])
         gains[1:2, :] += jnp.sum(grad * hat, axis=0, keepdims=True)
@@ -1210,78 +1290,95 @@
         branch[rows, :] = (0.5 * grad).astype(BF16)
         return carry
 
-    steps = len(stage_plans()[0])
-    points = list(range(2, 2 * steps + 1))
-    for c in range(count):
-        if c > 0 and points:
-            advance(early, points.pop(0))
-        lax.fori_loop(c, c + 1, arrive, 0)
+    lax.fori_loop(0, count, arrive, 0)
     for j in range(0, wide, width):
-        acc[2 * unit + j : 2 * unit + j + width, :] = dg(act[:, j : j + width], branch[...], 0, 0)
+        acc[4 * unit + j : 4 * unit + j + width, :] = dg(act[:, j : j + width], branch[...], 0, 0)
     advance(down, 0)
-    acc[unit : unit + 3 * width, :] = dg(joined[...], n2_ref[...], 1, 0)
-    acc[unit + 3 * width : 2 * unit, :] = point_two[...]
+    acc[3 * unit : 3 * unit + 3 * width, :] = dg(joined[...], n2_ref[...], 1, 0)
+    acc[3 * unit + 3 * width : 4 * unit, :] = point_two[...]
     advance(qkv, 0)
 
     def through(c, carry):
         rows = rows_at(c, chunk)
         grad = dg(branch[rows, :], w_out[...], 1, 1)
-        low_hidden = (grad * slope[rows, :]).astype(BF16)
+        low_hidden = (grad * slope[rows, :].astype(F32)).astype(BF16)
         hidden[rows, :] = low_hidden
         grad = dg(low_hidden, w_in[...], 1, 1)
-        hat = hat_keep[rows, :]
+        hat, inv = norm_parts(tok[rows, :].astype(F32))
         gains[0:1, :] += jnp.sum(grad * hat, axis=0, keepdims=True)
-        _, inv = norm_parts(tok[rows, :].astype(F32))
-        grad_ref[rows, :] = (grad_x1[rows, :] + norm_back(grad, hat, inv, row_of(gain1))).astype(BF16)
+        gain = row_of(gain1)
+        grad_ref[rows, :] = (grad_x1[rows, :] + norm_back(grad, hat, inv, gain)).astype(BF16)
+        n2_ref[rows, :] = (hat * gain).astype(BF16)
         return carry
 
     lax.fori_loop(0, count, through, 0)
     for j in range(0, wide, width):
-        acc[3 * unit + j : 3 * unit + j + width, :] = dg(n1_keep[...], hidden[:, j : j + width], 0, 0)
+        acc[5 * unit + j : 5 * unit + j + width, :] = dg(n2_ref[...], hidden[:, j : j + width], 0, 0)
     advance(up, 0)
     acc[last : last + 8, :] = gains[...]
     advance(rest, 0)
-    while points:
-        advance(early, points.pop(0))
     for position in range(1, 2 * steps + 1):
         advance(down + qkv + up + rest, position)
 
 
-def back(parts, trig, tok, x1, n2, grad_x2, gain1, gain2, w_in, w_out, w_qkv, mid, point_two):
+def back(
+    lengths, near, far, o, lse, do, trig, gain1, gain2, two, mid, point_two,
+    tok, x1, n2, grad_x2, act, slope, w_in, w_out, w_qkv,
+):
     frames, width = tok.shape
-    head_width, length = parts.shape
-    sp = length // frames
+    sp = lax.axis_size("sp")
     chunk = min(256, frames)
-    count = frames // chunk
+    block = min(512, frames)
+    count, per = frames // chunk, frames // block
     wide = w_in.shape[1]
-    rows = 16 * width + 16
-    staged, sems = reduction_scratch([4 * width] * 4 + [16])
+    dim = width // HEADS
+    reach = 2 * frames
+    rows = 24 * width + 16
+    staged, sems = reduction_scratch([4 * width] * 6 + [16])
     low_keep, keep = pltpu.VMEM((frames, width), BF16), pltpu.VMEM((frames, width), F32)
     return pl.pallas_call(
-        functools.partial(back_kernel, sp, chunk),
+        functools.partial(back_kernel, sp, lengths.shape[1], chunk, block, min(256, block)),
         out_shape=[
             jax.ShapeDtypeStruct((frames, width), BF16),
             jax.ShapeDtypeStruct((rows, width), BF16),
         ],
-        in_specs=[pl.BlockSpec(memory_space=pl.ANY)] + [VMEM] * 12,
+        in_specs=[SMEM] + [VMEM] * 11 + [pl.BlockSpec(memory_space=pl.ANY)] * 9,
         out_specs=[VMEM] * 2,
         scratch_shapes=[
-            pltpu.VMEM((sp, head_width, frames), BF16),
-            pltpu.VMEM((3 * width, frames), BF16),
             low_keep,
             keep,
             low_keep,
+            keep,
             pltpu.VMEM((frames, wide), BF16),
-            pltpu.VMEM((frames, wide), F32),
+            pltpu.VMEM((frames, wide), BF16),
+            pltpu.VMEM(w_in.shape, BF16),
+            pltpu.VMEM(w_out.shape, BF16),
+            pltpu.VMEM(w_qkv.shape, BF16),
+            pltpu.VMEM((2, reach, 2 * dim), BF16),
+            pltpu.VMEM((2, dim, reach), BF16),
+            pltpu.VMEM((2, 2 * dim, 2 * reach), BF16),
+            pltpu.VMEM((2, reach, 2 * dim), BF16),
+            pltpu.VMEM((2, 2 * dim, 2 * reach), BF16),
+            pltpu.VMEM((2, dim, reach), F32),
+            pltpu.VMEM((2, 4, dim, frames), BF16),
+            pltpu.VMEM((4, dim, frames), BF16),
+            pltpu.VMEM((2, dim, frames), BF16),
+            pltpu.VMEM((2, 4, dim, frames), BF16),
+            pltpu.VMEM((2, 4, dim, frames), BF16),
+            pltpu.VMEM((2, 2, dim, frames), BF16),
+            pltpu.VMEM((3 * width, frames), BF16),
+            low_keep,
             pltpu.VMEM((frames, wide), BF16),
             keep,
             pltpu.VMEM((8, width), F32),
             pltpu.VMEM((rows, width), F32),
             pltpu.VMEM((staged, width), BF16),
             pltpu.VMEM((staged, width), BF16),
-            DMA((sp - 1, count)),
-            DMA((sp - 1, count)),
-            DMA((count,)),
+            DMA((9,)),
+            DMA((2 * per,)),
+            DMA((2, per)),
+            DMA((per + 1,)),
+            DMA((per + 1,)),
             DMA(sems),
             DMA(sems),
         ],
@@ -1289,11 +1386,14 @@
             collective_id=2, has_side_effects=True, vmem_limit_bytes=VMEM_LIMIT
         ),
         name="back",
-    )(parts, trig, tok, x1, n2, grad_x2, gain1, gain2, w_in, w_out, w_qkv, mid, point_two)
+    )(
+        lengths, near, far, o, lse, do, trig, gain1, gain2, two, mid, point_two,
+        tok, x1, n2, grad_x2, act, slope, w_in, w_out, w_qkv,
+    )
 
 
 def unpack_kernel(
-    taps, full_two, full, bn_grads, output, input_grad,
+    taps, full, bn_grads, output, input_grad,
     output_to, input_to, gain1_to, in_one_to, out_one_to, gain2_to, qkv_to, out_weight_to, gain3_to, point_one_to,
     depthwise_to, bn_gain_to, bn_bias_to, point_two_to, gain4_to, in_two_to, out_two_to, gain5_to,
     in_one, out_one, qkv, point_one, point_two, out_weight, in_two, out_two, depthwise, sems,
@@ -1312,31 +1412,31 @@
     send(output, output_to)
     send(input_grad, input_to)
     for j in range(0, unit, width):
-        out_two[j : j + width, :] = block(full_two, j)
+        out_two[j : j + width, :] = block(full, j)
     send(out_two, out_two_to)
     for j in range(0, unit, width):
-        in_two[:, j : j + width] = block(full_two, unit + j)
+        in_two[:, j : j + width] = block(full, unit + j)
     send(in_two, in_two_to)
     for j in range(0, unit, width):
-        out_one[j : j + width, :] = block(full, 2 * unit + j)
+        out_one[j : j + width, :] = block(full, 4 * unit + j)
     send(out_one, out_one_to)
     for j in range(0, unit, width):
-        in_one[:, j : j + width] = block(full, 3 * unit + j)
+        in_one[:, j : j + width] = block(full, 5 * unit + j)
     send(in_one, in_one_to)
     for j in range(0, 2 * width, width):
-        point_one[:, j : j + width] = block(full, j)
+        point_one[:, j : j + width] = block(full, 2 * unit + j)
     send(point_one, point_one_to)
-    out_weight[...] = block(full, 2 * width)
+    out_weight[...] = block(full, 2 * unit + 2 * width)
     send(out_weight, out_weight_to)
-    point_two[...] = block(full, unit + 3 * width)
+    point_two[...] = block(full, 3 * unit + 3 * width)
     send(point_two, point_two_to)
     for j in range(0, 3 * width, width):
-        qkv[:, j : j + width] = block(full, unit + j).T
+        qkv[:, j : j + width] = block(full, 3 * unit + j).T
     send(qkv, qkv_to)
-    small = full[3 * width : 3 * width + 64, :].astype(F32)
+    small = full[2 * unit + 3 * width : 2 * unit + 3 * width + 64, :].astype(F32)
     depthwise[...] = small[8 : 8 + taps]
     send(depthwise, depthwise_to)
-    rest = full[4 * unit : 4 * unit + 16, :].astype(F32)
+    rest = full[6 * unit : 6 * unit + 16, :].astype(F32)
     for ref, row in (
         (gain1_to, rest[0]), (gain2_to, rest[1]), (gain3_to, small[2]), (gain4_to, small[3]), (gain5_to, small[4]),
         (bn_gain_to, bn_grads[0, :]), (bn_bias_to, bn_grads[1, :]),
@@ -1346,7 +1446,7 @@
         copy.wait()
 
 
-def unpack(full_two, full, bn_grads, output, input_grad, taps):
+def unpack(full, bn_grads, output, input_grad, taps):
     width = full.shape[1]
     row, square, tall, flat = (width,), (width, width), (4 * width, width), (width, 4 * width)
     thrice, twice = (width, 3 * width), (width, 2 * width)
@@ -1358,7 +1458,7 @@
     return pl.pallas_call(
         functools.partial(unpack_kernel, taps),
         out_shape=[jax.ShapeDtypeStruct(shape, F32 if i > 1 else BF16) for i, shape in enumerate(shapes)],
-        in_specs=[VMEM] * 5,
+        in_specs=[VMEM] * 4,
         out_specs=[VMEM if shape == row else anywhere for shape in shapes],
         scratch_shapes=[
             pltpu.VMEM(shape, F32)
@@ -1367,7 +1467,7 @@
         + [DMA((11,))],
         compiler_params=pltpu.CompilerParams(vmem_limit_bytes=VMEM_LIMIT),
         name="unpack",
-    )(full_two, full, bn_grads, output, input_grad)
+    )(full, bn_grads, output, input_grad)
 
 
 def on_device(
@@ -1381,17 +1481,19 @@
     turns = 10000.0 ** (-np.arange(half, dtype=np.float64) / half) / (2 * np.pi)
     high = np.round(turns * 4096.0) / 4096.0
     freq = jnp.asarray(np.stack([high, turns - high], axis=1), F32)
-    x1, n2, trig, heads = front(lengths, tokens[0], ln1_gain, ffn1_in, ffn1_out, ln2_gain, w_qkv, freq, sp)
-    context, raw_context, log_sums = attend(heads, lengths)
-    output, grad_x2, grad_context, mid, point_two, bn_grads, full_two = middle(
+    x1, n2, trig, act, slope, near, far, context, raw_context, log_sums, flag = front(
+        lengths, tokens[0], ln1_gain, ffn1_in, ffn1_out, ln2_gain, w_qkv, freq
+    )
+    context, raw_context, log_sums = repair(lengths, flag, near, far, context, raw_context, log_sums)
+    output, grad_x2, grad_context, mid, point_two, bn_grads, two = middle(
         lengths, context, x1, cotangent[0], ln3_gain, ln4_gain, ln5_gain, w_out, w_point1, depthwise,
         bn_gain, bn_bias, w_point2, ffn2_in, ffn2_out, dp,
     )
-    grad_heads = attend_back(heads, lengths, raw_context, log_sums, grad_context)
     input_grad, full = back(
-        grad_heads, trig, tokens[0], x1, n2, grad_x2, ln1_gain, ln2_gain, ffn1_in, ffn1_out, w_qkv, mid, point_two
+        lengths, near, far, raw_context, log_sums, grad_context, trig, ln1_gain, ln2_gain, two, mid, point_two,
+        tokens[0], x1, n2, grad_x2, act, slope, ffn1_in, ffn1_out, w_qkv,
     )
-    results = unpack(full_two, full, bn_grads, output, input_grad, depthwise.shape[0])
+    results = unpack(full, bn_grads, output, input_grad, depthwise.shape[0])
     return (results[0][None], results[1][None]) + tuple(results[2:])
 
 

time: 220 us -> 206 us (0.936)
  Pallas kernels: 219 us -> 205 us
    pallas_call x1, Pallas kernels: 68 us -> 50.5 us  [middle(): pl.pallas_call(functools.partial(middle_kernel, sp, dp, lengths.shape[1],...]
    pallas_call x4 -> x3, Pallas kernels: 145 us -> 149 us  [the longest x1 113 us: back(): pl.pallas_call(functools.partial(back_kernel, sp, lengths.shape[1], chunk...]
where the time goes in v5:
time: 206 us
  Pallas kernels  205 us (100%)
    pallas_call x1, Pallas kernels, back(): pl.pallas_call(functools.partial(back_kernel, sp, lengths.shape[1], chunk...  113 us
    pallas_call x1, Pallas kernels, middle(): pl.pallas_call(functools.partial(middle_kernel, sp, dp, lengths.shape[1],...  50.5 us
    pallas_call x1, Pallas kernels, front(): pl.pallas_call(functools.partial(front_kernel, lengths.shape[1], chunk, m...  35.1 us
    pallas_call x1, Pallas kernels, unpack(): pl.pallas_call(functools.partial(unpack_kernel, taps), out_shape=[jax.Sha...  5.76 us

profile of v5, /device:TPU:0, one launch (start us, length us, event | category | flops | bytes accessed | tf_op | source)
XLA Modules:
  0.0 206.1 jit_solution(4393092101080061984)
XLA Ops:
  0.7 35.1 %front.1 = (f32[1024,256]{1,0:T(8,128)}, bf16[1024,256]{1,0:T(8,128)(2,1)}, f32[64,1024]{1,0:T(8,128)}, bf16[1024,1024]{1,0:T(8,128)(2,1)}, bf16[1024,1024]{1,0:...) custom-call(s32[1,4]{1,0:T(1,128)} %len_ref.7, ...), custom_call_target="tpu_custom_call" | custom-call | tf_op jit(solution)/shard_map/front/pallas_call | solution.py:313
  35.7 0.9 repair.1
  36.6 50.5 %middle.1 = (bf16[1024,256]{1,0:T(8,128)(2,1)}, f32[1024,256]{1,0:T(8,128)}, bf16[2,64,2048]{2,1,0:T(8,128)(2,1)}, f32[1024,256]{1,0:T(8,128)}, f32[256,256]{1,0...) custom-call(s32[1,4]{1,0:T(1,128)} %len_ref.7, bf16[2,64,2048]{2,1,0:T(8,128)(2,1)} %get-tuple-element.67.parts, ...), custom_call_target="tpu_custom_call" | custom-call | tf_op jit(solution)/shard_map/middle/pallas_call | solution.py:1015
  87.1 113.0 %back.1 = (bf16[1024,256]{1,0:T(8,128)(2,1)}, bf16[6160,256]{1,0:T(8,128)(2,1)}) custom-call(s32[1,4]{1,0:T(1,128)} %len_ref.7, bf16[2,384,1024]{2,1,0:T(8,128)(2,1)} %get-tuple-element.59.near_hbm.near, bf16[2,256,1024]{2,1,0:T(8,128)(2,1)} %get-tuple-element.60.far_hbm.far, f32[2,64,2048]{2,1,0:T(8,128)} %get-tuple-element.65.o_ref, ...), custom_call_target="tpu_custom_call" | custom-call | tf_op jit(solution)/shard_map/back/pallas_call | solution.py:1339
  200.2 5.8 %unpack.1 = (bf16[1024,256]{1,0:T(8,128)(2,1)}, bf16[1024,256]{1,0:T(8,128)(2,1)}, f32[256]{0:T(256)}, f32[256,1024]{1,0:T(8,128)}, f32[1024,256]{1,0:T(8,128)},...) custom-call(bf16[6160,256]{1,0:T(8,128)(2,1)} %get-tuple-element.78., ...), custom_call_target="tpu_custom_call" | custom-call | tf_op jit(solution)/shard_map/unpack/pallas_call | solution.py:1458

commit v6 on v5

--- a/solution.py
+++ b/solution.py
@@ -20,6 +20,7 @@
 SMEM = pl.BlockSpec(memory_space=pltpu.SMEM)
 DMA = pltpu.SemaphoreType.DMA
 VMEM_LIMIT = 56 * 2**20
+EARLY_TIMES = (0, 1, 3, 5, 9, 11, 13)
 
 
 def dg(left, right, left_dim, right_dim):
@@ -30,6 +31,18 @@
 
 def rows_at(index, count):
     return pl.ds(pl.multiple_of(index * count, count), count)
+
+
+def start_copies(pairs, sems):
+    copies = [pltpu.make_async_copy(source, target, sems.at[i]) for i, (source, target) in enumerate(pairs)]
+    for copy in copies:
+        copy.start()
+    return copies
+
+
+def wait_all(copies):
+    for copy in copies:
+        copy.wait()
 
 
 def greet(devices):
@@ -170,8 +183,9 @@
 
 def front_kernel(
     items, chunk, block, len_ref, tok, gain1, w_in, w_out, gain2, w_qkv, freq,
-    x1_ref, n2_ref, trig, act, slope, near, far, ctx, o_ref, lse, flag,
-    parts, turned, qa, ka, va, acc, send, recv,
+    x1_hbm, n2_hbm, trig_hbm, act_hbm, slope_hbm, near_hbm, far_hbm, ctx_hbm, o_hbm, lse, flag,
+    x1_ref, n2_ref, trig, act, slope, near, far, ctx, o_ref,
+    parts, turned, qa, ka, va, acc, send, recv, out_sems, last_sems,
 ):
     me = lax.axis_index("sp")
     core, pair = lax.rem(me, 2), me // 2
@@ -199,6 +213,13 @@
             )
             for i, (source, target) in enumerate(ways)
         ]
+
+    def results(c):
+        rows = rows_at(c, chunk)
+        pairs = [(ref.at[rows, :], hbm.at[rows, :]) for ref, hbm in (
+            (x1_ref, x1_hbm), (n2_ref, n2_hbm), (act, act_hbm), (slope, slope_hbm)
+        )]
+        return [pltpu.make_async_copy(source, target, out_sems.at[i, c]) for i, (source, target) in enumerate(pairs)]
 
     def step(c, carry):
         rows = rows_at(c, chunk)
@@ -241,6 +262,8 @@
         for copy in copies(c):
             copy.start()
         near[core, :, rows] = parts[core, :, rows]
+        for copy in results(c):
+            copy.start()
         return carry
 
     lax.fori_loop(0, count, step, 0)
@@ -250,6 +273,7 @@
         return carry
 
     lax.fori_loop(0, count, near_arrives, 0)
+    leaving = start_copies([(near, near_hbm), (trig, trig_hbm)], last_sems)
     reach = 2 * frames
     for slot in range(2):
         first = (2 * pair + slot) * frames
@@ -292,15 +316,20 @@
         return lax.fori_loop(0, 2 * reach // wide, inner, carry)
 
     lax.fori_loop(0, count, far_step, 0)
+    leaving += start_copies([(far, far_hbm)], last_sems.at[pl.ds(2, 1)])
     bad = jnp.zeros((1, reach), F32)
     for h in range(2):
         total = acc[h, dim : dim + 1, :]
         value = acc[h, 0:dim, :] / total
         ctx[h] = value.astype(BF16)
         o_ref[h] = value
+        leaving += start_copies([(ctx.at[h], ctx_hbm.at[h]), (o_ref.at[h], o_hbm.at[h])], last_sems.at[pl.ds(3 + 2 * h, 2)])
         lse[h : h + 1, :] = lse[h : h + 1, :] + jnp.log2(total)
         bad = jnp.maximum(bad, jnp.where(total < 2.0**60, 0.0, 1.0))
     flag[...] = jnp.broadcast_to(jnp.max(bad, axis=1, keepdims=True), flag.shape)
+    for c in range(count):
+        wait_all(results(c))
+    wait_all(leaving)
 
 
 def front(lengths, tok, gain1, w_in, w_out, gain2, w_qkv, freq):
@@ -326,8 +355,17 @@
             jax.ShapeDtypeStruct((8, 128), F32),
         ],
         in_specs=[SMEM] + [VMEM] * 7,
-        out_specs=[VMEM] * 11,
+        out_specs=[pl.BlockSpec(memory_space=pl.ANY)] * 9 + [VMEM] * 2,
         scratch_shapes=[
+            pltpu.VMEM((frames, width), F32),
+            pltpu.VMEM((frames, width), BF16),
+            pltpu.VMEM((dim, frames), F32),
+            pltpu.VMEM((frames, wide), BF16),
+            pltpu.VMEM((frames, wide), BF16),
+            pltpu.VMEM((2, 6 * dim, frames), BF16),
+            pltpu.VMEM((2, 4 * dim, frames), BF16),
+            pltpu.VMEM((2, dim, reach), BF16),
+            pltpu.VMEM((2, dim, reach), F32),
             pltpu.VMEM((2, 6 * dim, frames), BF16),
             pltpu.VMEM((3 * width, width), BF16),
             pltpu.VMEM((2, 2 * dim, reach), BF16),
@@ -336,6 +374,8 @@
             pltpu.VMEM((2, dim + 16, reach), F32),
             DMA((3, count)),
             DMA((3, count)),
+            DMA((4, count)),
+            DMA((7,)),
         ],
         compiler_params=pltpu.CompilerParams(
             collective_id=0, has_side_effects=True, vmem_limit_bytes=VMEM_LIMIT
@@ -452,8 +492,12 @@
     def groups(steps):
         return [steps[i : i + 2] for i in range(0, len(steps), 2)]
 
-    plans = [sp_steps[:1]] + groups(plane) + groups(rest), [sp_steps[:1]] + groups(rest) + groups(plane)
-    return tuple([stage for stage in plan if stage] for plan in plans)
+    plans = (
+        groups(plane) + groups(rest),
+        groups(rest) + groups(plane),
+        [dp_steps[:1]] + groups(rest) + groups(sp_steps[1:]),
+    )
+    return tuple([sp_steps[:1]] + [stage for stage in plan if stage] for plan in plans)
 
 
 def stage_masks(stage):
@@ -583,9 +627,8 @@
 
 
 def reduction_scratch(rows_list):
-    plan, _ = stage_plans()
     staged = sum(max(exchange_plan(rows, stages)[1] for stages in stage_plans()) for rows in rows_list)
-    sems = sum((1 << len(stage)) - 1 for stage in plan)
+    sems = max(sum((1 << len(stage)) - 1 for stage in plan) for plan in stage_plans())
     return staged, (len(rows_list), 2, sems)
 
 
@@ -629,9 +672,10 @@
 
 
 def middle_kernel(
-    sp, dp, items, taps, chunk, block, len_ref, parts, x1_ref, cot, gain3, gain4, gain5, w_out, w_point1,
-    depthwise, bn_gain, bn_bias, w_point2, w_in, w_down,
-    out_ref, grad_x2, heads, mid, point_two, bn_grads, two,
+    sp, dp, items, taps, chunk, block, len_ref, parts, x1_hbm, cot_hbm, gain3, gain4, gain5, w_out_hbm,
+    w_point1_hbm, depthwise, bn_gain, bn_bias, w_point2_hbm, w_in_hbm, w_down_hbm,
+    out_hbm, x2_hbm, heads, mid_hbm, point_two_hbm, bn_grads, two_hbm,
+    x1_ref, cot, w_out, w_point1, w_point2, w_in, w_down, out_ref, grad_x2, mid, point_two, two, load_sems, out_sems,
     ctx, x2_ref, n3_keep, point, glu, conv, low_lim, high_lim, act, hidden, n4_keep, branch, swish, branch2,
     grad_x3, grad_y, grad_conv, grad_glu, grad_point, branch3, back_parts, tap_sums, edge_out, edge_in,
     send_box, near_box, far_box, sums,
@@ -670,6 +714,13 @@
     edge_in[...] = jnp.zeros_like(edge_in)
     send_box[...] = jnp.zeros_like(send_box)
     greet(greeted)
+    loads = start_copies(
+        [
+            (w_out_hbm, w_out), (x1_hbm, x1_ref), (w_point1_hbm, w_point1), (w_point2_hbm, w_point2),
+            (w_in_hbm, w_in), (w_down_hbm, w_down), (cot_hbm, cot),
+        ],
+        load_sems,
+    )
     lax.fori_loop(0, count, limits, 0)
     tap_sums[...] = jnp.zeros_like(tap_sums)
     sums[...] = jnp.zeros_like(sums)
@@ -700,6 +751,7 @@
         return carry
 
     lax.fori_loop(0, count, begin, 0)
+    wait_all(loads[:3])
 
     def open_step(c, carry):
         rows = rows_at(c, chunk)
@@ -878,7 +930,9 @@
         return carry
 
     mid[3 * width :, :] = jnp.zeros((width, width), F32)
+    wait_all(loads[3:])
     lax.fori_loop(0, count, heart_step, 0)
+    leaving = start_copies([(out_ref, out_hbm)], out_sems)
 
     pair = (sums[2:3, :], sums[3:4, :], jnp.zeros((1, width), F32))
     box_begin(1, 0, pair)
@@ -894,12 +948,13 @@
     swap_rims(1, *grad_rims)
     wide = w_in.shape[1]
     for j in range(0, wide, width):
-        two[j : j + width, :] = dg(act[:, j : j + width], branch[...], 0, 0).astype(BF16)
+        two[j : j + width, :] = dg(act[:, j : j + width], branch[...], 0, 0)
     pair = box_end(1, 0, pair, total)
     box_begin(1, 1, pair)
     for j in range(0, wide, width):
-        two[wide + j : wide + j + width, :] = dg(n4_keep[...], hidden[:, j : j + width], 0, 0).astype(BF16)
+        two[wide + j : wide + j + width, :] = dg(n4_keep[...], hidden[:, j : j + width], 0, 0)
     point_two[...] = dg(swish[...], branch2[...], 0, 0)
+    leaving += start_copies([(two, two_hbm), (point_two, point_two_hbm)], out_sems.at[pl.ds(1, 2)])
     await_rims(1, *grad_rims)
     bias_sum, gain_sum, _ = box_end(1, 1, pair, total)
     bn_grads[0:1, :] = gain_sum
@@ -977,6 +1032,7 @@
         return carry
 
     lax.fori_loop(0, count, close_step, 0)
+    leaving += start_copies([(grad_x2, x2_hbm)], out_sems.at[pl.ds(3, 1)])
     for j in range(2):
         mid[j * width : (j + 1) * width, :] = dg(n3_keep[...], grad_point[:, j * width : (j + 1) * width], 0, 0)
     mid[2 * width : 3 * width, :] = dg(ctx[...].reshape(width, frames), branch3[...], 1, 0)
@@ -985,12 +1041,15 @@
         for h in range(2):
             mid[row : row + 1, h * lanes : (h + 1) * lanes] = jnp.sum(tap_sums[tap, h], axis=0, keepdims=True)
 
+    leaving += start_copies([(mid, mid_hbm)], out_sems.at[pl.ds(4, 1)])
+
     def finish(c, carry):
         for copy in back_moves(c):
             copy.wait()
         return carry
 
     lax.fori_loop(0, count, finish, 0)
+    wait_all(leaving)
 
 
 def middle(
@@ -1000,6 +1059,7 @@
     frames, width = x1.shape
     sp = lax.axis_size("sp")
     assert sp == HEADS == 4
+    anywhere = pl.BlockSpec(memory_space=pl.ANY)
     paired = pltpu.VMEM((2, 2, width // 4, frames), BF16)
     wide = w_in.shape[1]
     taps = depthwise.shape[0]
@@ -1021,11 +1081,28 @@
             jax.ShapeDtypeStruct((4 * width, width), F32),
             jax.ShapeDtypeStruct((width, width), F32),
             jax.ShapeDtypeStruct((8, width), F32),
-            jax.ShapeDtypeStruct((2 * wide, width), BF16),
+            jax.ShapeDtypeStruct((2 * wide, width), F32),
         ],
-        in_specs=[SMEM, pl.BlockSpec(memory_space=pl.ANY)] + [VMEM] * 13,
-        out_specs=[VMEM] * 7,
+        in_specs=[
+            SMEM, anywhere, anywhere, anywhere, VMEM, VMEM, VMEM, anywhere, anywhere, VMEM, VMEM, VMEM, anywhere,
+            anywhere, anywhere,
+        ],
+        out_specs=[anywhere, anywhere, VMEM, anywhere, anywhere, VMEM, anywhere],
         scratch_shapes=[
+            keep,
+            low_keep,
+            pltpu.VMEM(w_out.shape, BF16),
+            pltpu.VMEM(w_point1.shape, BF16),
+            pltpu.VMEM(w_point2.shape, BF16),
+            pltpu.VMEM(w_in.shape, BF16),
+            pltpu.VMEM(w_down.shape, BF16),
+            low_keep,
+            keep,
+            pltpu.VMEM((4 * width, width), F32),
+            pltpu.VMEM((width, width), F32),
+            pltpu.VMEM((2 * wide, width), F32),
+            DMA((7,)),
+            DMA((5,)),
             paired,
             keep,
             low_keep,
@@ -1069,10 +1146,10 @@
 
 
 def back_kernel(
-    sp, items, chunk, block, sub, len_ref, near, far, o_ref, lse_ref, do_ref, trig, gain1, gain2, two, mid, point_two,
-    tok_hbm, x1_hbm, n2_hbm, x2_hbm, act_hbm, slope_hbm, w_in_hbm, w_out_hbm, w_qkv_hbm,
+    sp, items, chunk, block, sub, len_ref, lse_ref, gain1, gain2,
+    near_hbm, far_hbm, o_hbm, do_hbm, trig_hbm, two_hbm, mid_hbm, point_two_hbm, tok_hbm, x1_hbm, n2_hbm, x2_hbm, act_hbm, slope_hbm, w_in_hbm, w_out_hbm, w_qkv_hbm,
     grad_ref, full,
-    tok, x1_ref, n2_ref, grad_x2, act, slope, w_in, w_out, w_qkv,
+    near, far, o_ref, do_ref, trig, tok, x1_ref, n2_ref, grad_x2, act, slope, w_in, w_out, w_qkv,
     qa, qt, ka, da, va, dq, far_out, near_out, dq_out, far_kv, near_kv, near_dq,
     joined, branch, hidden, grad_x1, gains, acc, stage, land,
     load_sems, far_send, far_recv, near_send, near_recv, sum_send, sum_recv,
@@ -1088,32 +1165,32 @@
     reach = 2 * frames
     greeted = [peer_at(*mask) for mask in all_masks(sp)]
     greet(greeted)
-    loads = [
-        pltpu.make_async_copy(source, target, load_sems.at[i])
-        for i, (source, target) in enumerate(
-            (
-                (x1_hbm, x1_ref), (x2_hbm, grad_x2), (w_qkv_hbm, w_qkv), (n2_hbm, n2_ref), (act_hbm, act),
-                (w_out_hbm, w_out), (slope_hbm, slope), (w_in_hbm, w_in), (tok_hbm, tok),
-            )
-        )
-    ]
-    for copy in loads:
-        copy.start()
     unit = 4 * width
     last = 6 * unit
+    loads = start_copies(
+        [
+            (near_hbm, near), (do_hbm, do_ref), (o_hbm, o_ref), (far_hbm, far),
+            (two_hbm, acc.at[0 : 2 * unit, :]), (mid_hbm, acc.at[2 * unit : 3 * unit, :]),
+            (point_two_hbm, acc.at[3 * unit + 3 * width : 4 * unit, :]), (trig_hbm, trig),
+            (x1_hbm, x1_ref), (x2_hbm, grad_x2), (w_qkv_hbm, w_qkv), (n2_hbm, n2_ref), (act_hbm, act),
+            (w_out_hbm, w_out), (slope_hbm, slope), (w_in_hbm, w_in), (tok_hbm, tok),
+        ],
+        load_sems,
+    )
     streams = make_streams(
         [
-            (0, unit, 1), (unit, unit, 1), (2 * unit, unit, 1),
+            (0, unit, 2), (unit, unit, 2), (2 * unit, unit, 2),
             (3 * unit, unit, 1), (4 * unit, unit, 0), (5 * unit, unit, 0), (last, 16, 0),
         ],
         acc, stage, land, full, sum_send, sum_recv,
     )
     early, (qkv, down, up, rest) = streams[:3], ([stream] for stream in streams[3:])
     steps = len(stage_plans()[0])
-    acc[0 : 2 * unit, :] = two[...].astype(F32)
-    acc[2 * unit : 3 * unit, :] = mid[...]
     acc[last : last + 16, :] = jnp.zeros((16, width), F32)
     gains[...] = jnp.zeros_like(gains)
+    for h in range(2):
+        dq[h] = jnp.zeros((dim, reach), F32)
+    wait_all(loads[:4])
     ends = ends_of(len_ref, items)
     wide_pad = jnp.zeros((dim - 16, frames), BF16)
     for slot in range(2):
@@ -1137,9 +1214,8 @@
                 va[h, 0:dim, where] = value
                 va[h, dim : dim + 16, where] = first_rows(3, frames)
                 va[h, dim + 16 :, where] = wide_pad
-    for h in range(2):
-        dq[h] = jnp.zeros((dim, reach), F32)
     await_greetings(greeted)
+    wait_all(loads[4:6])
 
     def attend_block(h, at):
         dk, dv, grads = [], [], []
@@ -1175,6 +1251,16 @@
             device_id=(dp, 2 * (1 - pair) + b // per), device_id_type=MESH,
         )
 
+    times = EARLY_TIMES[: 2 * len(early[0].stages) + 1]
+    remaining = list(range(len(times), 2 * len(early[0].stages) + 1))
+
+    def early_steps(t):
+        for position, time in enumerate(times):
+            for i, stream in enumerate(early):
+                @pl.when(t == min(time + i, 8 * per - 1))
+                def _():
+                    advance([stream], position)
+
     def far_step(t, carry):
         b, h = t // 2, lax.rem(t, 2)
         cols = rows_at(lax.rem(b, per), block)
@@ -1184,11 +1270,7 @@
         def _():
             far_copy(b).start()
 
-        for position in range(steps + 1):
-            @pl.when(t == 1 + position * 2)
-            def _():
-                advance(early, position)
-
+        early_steps(t)
         return carry
 
     lax.fori_loop(0, 4 * per, far_step, 0)
@@ -1210,11 +1292,7 @@
         def _():
             near_copy(b).start()
 
-        for position in range(steps + 1, 2 * steps):
-            @pl.when(t == 2 * (position - steps - 1))
-            def _():
-                advance(early, position)
-
+        early_steps(t + 4 * per)
         return carry
 
     lax.fori_loop(0, 2 * per, sibling_step, 0)
@@ -1223,10 +1301,7 @@
         b, h = t // 2, lax.rem(t, 2)
         keep(near_kv, core, h, rows_at(b, block), attend_block(h, core * frames + b * block))
 
-        @pl.when(t == 0)
-        def _():
-            advance(early, 2 * steps)
-
+        early_steps(t + 6 * per)
         return carry
 
     lax.fori_loop(0, 2 * per, own_step, 0)
@@ -1239,8 +1314,7 @@
     dq_copy.start()
     for h in range(2):
         near_dq[core, h] = (dq[h, :, pl.ds(pl.multiple_of(core * frames, frames), frames)] * dim**-0.5).astype(BF16)
-    for copy in loads:
-        copy.wait()
+    wait_all(loads[6:])
     for b in range(2 * per):
         far_copy(b).wait_send()
     for source in range(2):
@@ -1295,30 +1369,45 @@
         acc[4 * unit + j : 4 * unit + j + width, :] = dg(act[:, j : j + width], branch[...], 0, 0)
     advance(down, 0)
     acc[3 * unit : 3 * unit + 3 * width, :] = dg(joined[...], n2_ref[...], 1, 0)
-    acc[3 * unit + 3 * width : 4 * unit, :] = point_two[...]
     advance(qkv, 0)
 
     def through(c, carry):
         rows = rows_at(c, chunk)
         grad = dg(branch[rows, :], w_out[...], 1, 1)
-        low_hidden = (grad * slope[rows, :].astype(F32)).astype(BF16)
-        hidden[rows, :] = low_hidden
-        grad = dg(low_hidden, w_in[...], 1, 1)
-        hat, inv = norm_parts(tok[rows, :].astype(F32))
-        gains[0:1, :] += jnp.sum(grad * hat, axis=0, keepdims=True)
-        gain = row_of(gain1)
-        grad_ref[rows, :] = (grad_x1[rows, :] + norm_back(grad, hat, inv, gain)).astype(BF16)
-        n2_ref[rows, :] = (hat * gain).astype(BF16)
+        hidden[rows, :] = (grad * slope[rows, :].astype(F32)).astype(BF16)
+        hat, _ = norm_parts(tok[rows, :].astype(F32))
+        n2_ref[rows, :] = (hat * row_of(gain1)).astype(BF16)
         return carry
 
     lax.fori_loop(0, count, through, 0)
     for j in range(0, wide, width):
         acc[5 * unit + j : 5 * unit + j + width, :] = dg(n2_ref[...], hidden[:, j : j + width], 0, 0)
     advance(up, 0)
+    advance(down + qkv, 1)
+
+    def last_step(c, carry):
+        rows = rows_at(c, chunk)
+        grad = dg(hidden[rows, :], w_in[...], 1, 1)
+        hat, inv = norm_parts(tok[rows, :].astype(F32))
+        gains[0:1, :] += jnp.sum(grad * hat, axis=0, keepdims=True)
+        grad_ref[rows, :] = (grad_x1[rows, :] + norm_back(grad, hat, inv, row_of(gain1))).astype(BF16)
+        return carry
+
+    lax.fori_loop(0, count // 2, last_step, 0)
+    advance(up, 1)
+    lax.fori_loop(count // 2, count, last_step, 0)
     acc[last : last + 8, :] = gains[...]
     advance(rest, 0)
-    for position in range(1, 2 * steps + 1):
-        advance(down + qkv + up + rest, position)
+    advance(down + qkv, 2)
+    advance(rest, 1)
+    for position in range(2, 2 * steps + 1):
+        if position < 2 * steps:
+            advance(down + qkv, position + 1)
+        advance(up + rest, position)
+        if remaining:
+            advance(early, remaining.pop(0))
+    while remaining:
+        advance(early, remaining.pop(0))
 
 
 def back(
@@ -1342,9 +1431,14 @@
             jax.ShapeDtypeStruct((frames, width), BF16),
             jax.ShapeDtypeStruct((rows, width), BF16),
         ],
-        in_specs=[SMEM] + [VMEM] * 11 + [pl.BlockSpec(memory_space=pl.ANY)] * 9,
+        in_specs=[SMEM] + [VMEM] * 3 + [pl.BlockSpec(memory_space=pl.ANY)] * 17,
         out_specs=[VMEM] * 2,
         scratch_shapes=[
+            pltpu.VMEM(near.shape, BF16),
+            pltpu.VMEM(far.shape, BF16),
+            pltpu.VMEM(o.shape, F32),
+            pltpu.VMEM(do.shape, BF16),
+            pltpu.VMEM(trig.shape, F32),
             low_keep,
             keep,
             low_keep,
@@ -1374,7 +1468,7 @@
             pltpu.VMEM((rows, width), F32),
             pltpu.VMEM((staged, width), BF16),
             pltpu.VMEM((staged, width), BF16),
-            DMA((9,)),
+            DMA((17,)),
             DMA((2 * per,)),
             DMA((2, per)),
             DMA((per + 1,)),
@@ -1387,7 +1481,7 @@
         ),
         name="back",
     )(
-        lengths, near, far, o, lse, do, trig, gain1, gain2, two, mid, point_two,
+        lengths, lse, gain1, gain2, near, far, o, do, trig, two, mid, point_two,
         tok, x1, n2, grad_x2, act, slope, w_in, w_out, w_qkv,
     )
 

time: 206 us -> 177 us (0.86)
  Pallas kernels: 205 us -> 176 us
    pallas_call x1, Pallas kernels: 113 us -> 86.7 us  [back(): pl.pallas_call(functools.partial(back_kernel, sp, lengths.shape[1], chunk...]
where the time goes in v6:
time: 177 us
  Pallas kernels  176 us (99%)
    pallas_call x1, Pallas kernels, back(): pl.pallas_call(functools.partial(back_kernel, sp, lengths.shape[1], chunk...  86.7 us
    pallas_call x1, Pallas kernels, middle(): pl.pallas_call(functools.partial(middle_kernel, sp, dp, lengths.shape[1],...  48.9 us
    pallas_call x1, Pallas kernels, front(): pl.pallas_call(functools.partial(front_kernel, lengths.shape[1], chunk, m...  33.6 us
    pallas_call x1, Pallas kernels, unpack(): pl.pallas_call(functools.partial(unpack_kernel, taps), out_shape=[jax.Sha...  5.76 us

profile of v6, /device:TPU:0, one launch (start us, length us, event | category | flops | bytes accessed | tf_op | source)
XLA Modules:
  0.0 176.8 jit_solution(6894793958477650338)
XLA Ops:
  0.7 33.6 %front.1 = (f32[1024,256]{1,0:T(8,128)}, bf16[1024,256]{1,0:T(8,128)(2,1)}, f32[64,1024]{1,0:T(8,128)}, bf16[1024,1024]{1,0:T(8,128)(2,1)}, bf16[1024,1024]{1,0:...) custom-call(s32[1,4]{1,0:T(1,128)} %len_ref.7, ...), custom_call_target="tpu_custom_call" | custom-call | tf_op jit(solution)/shard_map/front/pallas_call | solution.py:342
  34.2 1.0 repair.1
  35.3 48.9 %middle.1 = (bf16[1024,256]{1,0:T(8,128)(2,1)}, f32[1024,256]{1,0:T(8,128)}, bf16[2,64,2048]{2,1,0:T(8,128)(2,1)}, f32[1024,256]{1,0:T(8,128)}, f32[256,256]{1,0...) custom-call(s32[1,4]{1,0:T(1,128)} %len_ref.7, bf16[2,64,2048]{2,1,0:T(8,128)(2,1)} %get-tuple-element.67.parts, ...), custom_call_target="tpu_custom_call" | custom-call | tf_op jit(solution)/shard_map/middle/pallas_call | solution.py:1075
  84.2 86.7 %back.1 = (bf16[1024,256]{1,0:T(8,128)(2,1)}, bf16[6160,256]{1,0:T(8,128)(2,1)}) custom-call(s32[1,4]{1,0:T(1,128)} %len_ref.7, f32[2,2048]{1,0:T(2,128)} %get-tuple-element.65.lse_ref, bf16[256]{0:T(256)(128)(2,1)} %gain1.3, bf16[256]{0:T(256)(128)(2,1)} %gain2.3, bf16[2,384,1024]{2,1,0:T(8,128)(2,1)} %get-tuple-element.60.near_hbm, ...), custom_call_target="tpu_custom_call" | custom-call | tf_op jit(solution)/shard_map/back/pallas_call | solution.py:1428
  170.9 5.8 %unpack.1 = (bf16[1024,256]{1,0:T(8,128)(2,1)}, bf16[1024,256]{1,0:T(8,128)(2,1)}, f32[256]{0:T(256)}, f32[256,1024]{1,0:T(8,128)}, f32[1024,256]{1,0:T(8,128)},...) custom-call(bf16[6160,256]{1,0:T(8,128)(2,1)} %get-tuple-element.78., ...), custom_call_target="tpu_custom_call" | custom-call | tf_op jit(solution)/shard_map/unpack/pallas_call | solution.py:1552

commit v7 on v6

--- a/solution.py
+++ b/solution.py
@@ -20,7 +20,8 @@
 SMEM = pl.BlockSpec(memory_space=pltpu.SMEM)
 DMA = pltpu.SemaphoreType.DMA
 VMEM_LIMIT = 56 * 2**20
-EARLY_TIMES = (0, 1, 3, 5, 9, 11, 13)
+PARTIAL_TIMES = (0, 3, 5, 10, 14)
+FRESH_TIMES = (0, 1, 4, 7, 11, 13)
 
 
 def dg(left, right, left_dim, right_dim):
@@ -674,8 +675,9 @@
 def middle_kernel(
     sp, dp, items, taps, chunk, block, len_ref, parts, x1_hbm, cot_hbm, gain3, gain4, gain5, w_out_hbm,
     w_point1_hbm, depthwise, bn_gain, bn_bias, w_point2_hbm, w_in_hbm, w_down_hbm,
-    out_hbm, x2_hbm, heads, mid_hbm, point_two_hbm, bn_grads, two_hbm,
+    out_hbm, x2_hbm, heads, mid_hbm, point_two_hbm, bn_grads, partial,
     x1_ref, cot, w_out, w_point1, w_point2, w_in, w_down, out_ref, grad_x2, mid, point_two, two, load_sems, out_sems,
+    stage, land, sum_send, sum_recv,
     ctx, x2_ref, n3_keep, point, glu, conv, low_lim, high_lim, act, hidden, n4_keep, branch, swish, branch2,
     grad_x3, grad_y, grad_conv, grad_glu, grad_point, branch3, back_parts, tap_sums, edge_out, edge_in,
     send_box, near_box, far_box, sums,
@@ -688,7 +690,9 @@
     count = frames // chunk
     peers = sp_peers(sp)
     far_peers = [peer_at(0, mask) for mask in range(1, dp)]
-    greeted = peers + far_peers
+    masks = all_masks(sp)
+    masks += [(0, mask) for mask in range(1, dp) if (0, mask) not in masks]
+    greeted = [peer_at(*mask) for mask in masks]
     core = lax.rem(me, 2)
     sibling = peer_at(1, 0)
     length = sp * frames
@@ -947,14 +951,20 @@
     )
     swap_rims(1, *grad_rims)
     wide = w_in.shape[1]
+    streams = make_streams([(0, wide, 2), (wide, wide, 2)], two, stage, land, None, sum_send, sum_recv)
+    early_stages = len(stage_plans()[2]) - 1
     for j in range(0, wide, width):
         two[j : j + width, :] = dg(act[:, j : j + width], branch[...], 0, 0)
+    advance(streams[:1], 0)
     pair = box_end(1, 0, pair, total)
     box_begin(1, 1, pair)
     for j in range(0, wide, width):
         two[wide + j : wide + j + width, :] = dg(n4_keep[...], hidden[:, j : j + width], 0, 0)
+    advance(streams[1:], 0)
+    advance(streams[:1], 1)
     point_two[...] = dg(swish[...], branch2[...], 0, 0)
-    leaving += start_copies([(two, two_hbm), (point_two, point_two_hbm)], out_sems.at[pl.ds(1, 2)])
+    leaving += start_copies([(point_two, point_two_hbm)], out_sems.at[pl.ds(1, 1)])
+    advance(streams[1:], 1)
     await_rims(1, *grad_rims)
     bias_sum, gain_sum, _ = box_end(1, 1, pair, total)
     bn_grads[0:1, :] = gain_sum
@@ -1008,7 +1018,9 @@
             grad_glu[h, rows_at(b, block), :] = result[h]
         return carry
 
-    lax.fori_loop(0, blocks, conv_back_step, 0)
+    lax.fori_loop(0, blocks // 2, conv_back_step, 0)
+    advance(streams, 2)
+    lax.fori_loop(blocks // 2, blocks, conv_back_step, 0)
 
     def back_moves(c):
         return moves(c, by_head(back_parts), by_frames(heads), back_send, back_recv, back_local)
@@ -1049,6 +1061,12 @@
         return carry
 
     lax.fori_loop(0, count, finish, 0)
+    for position in range(3, early_stages):
+        advance(streams, position)
+    size = streams[0].sizes[early_stages - 1][1]
+    for i, stream in enumerate(streams):
+        stream.sum_recv(early_stages - 1)
+        partial[i * size : (i + 1) * size, :] = two[stream.at(stream.low(early_stages), size), :]
     wait_all(leaving)
 
 
@@ -1062,6 +1080,9 @@
     anywhere = pl.BlockSpec(memory_space=pl.ANY)
     paired = pltpu.VMEM((2, 2, width // 4, frames), BF16)
     wide = w_in.shape[1]
+    staged, sems = reduction_scratch([wide, wide])
+    stages = stage_plans()[2]
+    part = exchange_plan(wide, stages[:-1])[2]
     taps = depthwise.shape[0]
     reach = taps // 2
     chunk = min(256, frames)
@@ -1081,13 +1102,13 @@
             jax.ShapeDtypeStruct((4 * width, width), F32),
             jax.ShapeDtypeStruct((width, width), F32),
             jax.ShapeDtypeStruct((8, width), F32),
-            jax.ShapeDtypeStruct((2 * wide, width), F32),
+            jax.ShapeDtypeStruct((2 * part, width), F32),
         ],
         in_specs=[
             SMEM, anywhere, anywhere, anywhere, VMEM, VMEM, VMEM, anywhere, anywhere, VMEM, VMEM, VMEM, anywhere,
             anywhere, anywhere,
         ],
-        out_specs=[anywhere, anywhere, VMEM, anywhere, anywhere, VMEM, anywhere],
+        out_specs=[anywhere, anywhere, VMEM, anywhere, anywhere, VMEM, VMEM],
         scratch_shapes=[
             keep,
             low_keep,
@@ -1103,6 +1124,10 @@
             pltpu.VMEM((2 * wide, width), F32),
             DMA((7,)),
             DMA((5,)),
+            pltpu.VMEM((staged, width), BF16),
+            pltpu.VMEM((staged, width), BF16),
+            DMA(sems),
+            DMA(sems),
             paired,
             keep,
             low_keep,
@@ -1146,11 +1171,11 @@
 
 
 def back_kernel(
-    sp, items, chunk, block, sub, len_ref, lse_ref, gain1, gain2,
-    near_hbm, far_hbm, o_hbm, do_hbm, trig_hbm, two_hbm, mid_hbm, point_two_hbm, tok_hbm, x1_hbm, n2_hbm, x2_hbm, act_hbm, slope_hbm, w_in_hbm, w_out_hbm, w_qkv_hbm,
+    sp, items, chunk, block, sub, len_ref, lse_ref, gain1, gain2, partial,
+    near_hbm, far_hbm, o_hbm, do_hbm, trig_hbm, mid_hbm, point_two_hbm, tok_hbm, x1_hbm, n2_hbm, x2_hbm, act_hbm, slope_hbm, w_in_hbm, w_out_hbm, w_qkv_hbm,
     grad_ref, full,
     near, far, o_ref, do_ref, trig, tok, x1_ref, n2_ref, grad_x2, act, slope, w_in, w_out, w_qkv,
-    qa, qt, ka, da, va, dq, far_out, near_out, dq_out, far_kv, near_kv, near_dq,
+    qa, qt, ka, da, va, dq, turned, far_out, near_out, dq_out, far_kv, near_kv, near_dq,
     joined, branch, hidden, grad_x1, gains, acc, stage, land,
     load_sems, far_send, far_recv, near_send, near_recv, sum_send, sum_recv,
 ):
@@ -1170,7 +1195,7 @@
     loads = start_copies(
         [
             (near_hbm, near), (do_hbm, do_ref), (o_hbm, o_ref), (far_hbm, far),
-            (two_hbm, acc.at[0 : 2 * unit, :]), (mid_hbm, acc.at[2 * unit : 3 * unit, :]),
+            (mid_hbm, acc.at[2 * unit : 3 * unit, :]),
             (point_two_hbm, acc.at[3 * unit + 3 * width : 4 * unit, :]), (trig_hbm, trig),
             (x1_hbm, x1_ref), (x2_hbm, grad_x2), (w_qkv_hbm, w_qkv), (n2_hbm, n2_ref), (act_hbm, act),
             (w_out_hbm, w_out), (slope_hbm, slope), (w_in_hbm, w_in), (tok_hbm, tok),
@@ -1215,10 +1240,10 @@
                 va[h, dim : dim + 16, where] = first_rows(3, frames)
                 va[h, dim + 16 :, where] = wide_pad
     await_greetings(greeted)
-    wait_all(loads[4:6])
+    wait_all(loads[4:5])
 
     def attend_block(h, at):
-        dk, dv, grads = [], [], []
+        dk, dv = [], []
 
         def score(u):
             cols = pl.ds(pl.multiple_of(at + u * sub, sub), sub)
@@ -1233,8 +1258,8 @@
             grad = (probs * grad_probs).astype(BF16)
             dv.append(dg(do_ref[h], probs.astype(BF16), 1, 0).astype(BF16))
             dk.append((dg(qt[h], grad, 1, 0) * LN2).astype(BF16))
-            grads.append(grad)
-        dq[h] += dg(ka[h, 0:dim, pl.ds(pl.multiple_of(at, block), block)], jnp.concatenate(grads, axis=1), 1, 1)
+            turned[u * sub : (u + 1) * sub, :] = grad.T
+        dq[h] += dg(ka[h, 0:dim, pl.ds(pl.multiple_of(at, block), block)], turned[...], 1, 0)
         return jnp.concatenate(dk, axis=1), jnp.concatenate(dv, axis=1)
 
     per = frames // block
@@ -1251,15 +1276,32 @@
             device_id=(dp, 2 * (1 - pair) + b // per), device_id_type=MESH,
         )
 
-    times = EARLY_TIMES[: 2 * len(early[0].stages) + 1]
-    remaining = list(range(len(times), 2 * len(early[0].stages) + 1))
+    done = len(early[0].stages) - 1
+    size = early[0].sizes[done - 1][1]
+    for i, stream in enumerate(early[:2]):
+        acc[stream.at(stream.low(done), size), :] = partial[i * size : (i + 1) * size, :]
+    schedule, remaining = {}, []
+    for stream, times, first in zip(early, (PARTIAL_TIMES, PARTIAL_TIMES, FRESH_TIMES), (done, done, 0)):
+        positions = range(first, 2 * len(stream.stages) + 1)
+        for position, time in zip(positions, times):
+            schedule.setdefault(time, []).append((stream, position, position == first))
+        remaining.append([(stream, position) for position in positions[len(times) :]])
 
     def early_steps(t):
-        for position, time in enumerate(times):
-            for i, stream in enumerate(early):
-                @pl.when(t == min(time + i, 8 * per - 1))
-                def _():
-                    advance([stream], position)
+        for time, moves in schedule.items():
+            @pl.when(t == min(time, 8 * per - 1))
+            def _():
+                for stream, position, opening in moves:
+                    if opening:
+                        stream.sum_send(position)
+                    else:
+                        advance([stream], position)
+
+    def late_steps():
+        for moves in remaining:
+            if moves:
+                stream, position = moves.pop(0)
+                advance([stream], position)
 
     def far_step(t, carry):
         b, h = t // 2, lax.rem(t, 2)
@@ -1314,7 +1356,7 @@
     dq_copy.start()
     for h in range(2):
         near_dq[core, h] = (dq[h, :, pl.ds(pl.multiple_of(core * frames, frames), frames)] * dim**-0.5).astype(BF16)
-    wait_all(loads[6:])
+    wait_all(loads[5:])
     for b in range(2 * per):
         far_copy(b).wait_send()
     for source in range(2):
@@ -1380,10 +1422,10 @@
         return carry
 
     lax.fori_loop(0, count, through, 0)
+    advance(down + qkv, 1)
     for j in range(0, wide, width):
         acc[5 * unit + j : 5 * unit + j + width, :] = dg(n2_ref[...], hidden[:, j : j + width], 0, 0)
     advance(up, 0)
-    advance(down + qkv, 1)
 
     def last_step(c, carry):
         rows = rows_at(c, chunk)
@@ -1398,20 +1440,17 @@
     lax.fori_loop(count // 2, count, last_step, 0)
     acc[last : last + 8, :] = gains[...]
     advance(rest, 0)
-    advance(down + qkv, 2)
-    advance(rest, 1)
     for position in range(2, 2 * steps + 1):
-        if position < 2 * steps:
-            advance(down + qkv, position + 1)
-        advance(up + rest, position)
-        if remaining:
-            advance(early, remaining.pop(0))
-    while remaining:
-        advance(early, remaining.pop(0))
+        advance(down + qkv + up, position)
+        advance(rest, position - 1)
+        late_steps()
+    advance(rest, 2 * steps)
+    while any(remaining):
+        late_steps()
 
 
 def back(
-    lengths, near, far, o, lse, do, trig, gain1, gain2, two, mid, point_two,
+    lengths, near, far, o, lse, do, trig, gain1, gain2, partial, mid, point_two,
     tok, x1, n2, grad_x2, act, slope, w_in, w_out, w_qkv,
 ):
     frames, width = tok.shape
@@ -1426,12 +1465,12 @@
     staged, sems = reduction_scratch([4 * width] * 6 + [16])
     low_keep, keep = pltpu.VMEM((frames, width), BF16), pltpu.VMEM((frames, width), F32)
     return pl.pallas_call(
-        functools.partial(back_kernel, sp, lengths.shape[1], chunk, block, min(256, block)),
+        functools.partial(back_kernel, sp, lengths.shape[1], chunk, block, min(128, block)),
         out_shape=[
             jax.ShapeDtypeStruct((frames, width), BF16),
             jax.ShapeDtypeStruct((rows, width), BF16),
         ],
-        in_specs=[SMEM] + [VMEM] * 3 + [pl.BlockSpec(memory_space=pl.ANY)] * 17,
+        in_specs=[SMEM] + [VMEM] * 4 + [pl.BlockSpec(memory_space=pl.ANY)] * 16,
         out_specs=[VMEM] * 2,
         scratch_shapes=[
             pltpu.VMEM(near.shape, BF16),
@@ -1454,6 +1493,7 @@
             pltpu.VMEM((2, reach, 2 * dim), BF16),
             pltpu.VMEM((2, 2 * dim, 2 * reach), BF16),
             pltpu.VMEM((2, dim, reach), F32),
+            pltpu.VMEM((block, reach), BF16),
             pltpu.VMEM((2, 4, dim, frames), BF16),
             pltpu.VMEM((4, dim, frames), BF16),
             pltpu.VMEM((2, dim, frames), BF16),
@@ -1468,7 +1508,7 @@
             pltpu.VMEM((rows, width), F32),
             pltpu.VMEM((staged, width), BF16),
             pltpu.VMEM((staged, width), BF16),
-            DMA((17,)),
+            DMA((16,)),
             DMA((2 * per,)),
             DMA((2, per)),
             DMA((per + 1,)),
@@ -1481,7 +1521,7 @@
         ),
         name="back",
     )(
-        lengths, lse, gain1, gain2, near, far, o, do, trig, two, mid, point_two,
+        lengths, lse, gain1, gain2, partial, near, far, o, do, trig, mid, point_two,
         tok, x1, n2, grad_x2, act, slope, w_in, w_out, w_qkv,
     )
 
@@ -1579,12 +1619,12 @@
         lengths, tokens[0], ln1_gain, ffn1_in, ffn1_out, ln2_gain, w_qkv, freq
     )
     context, raw_context, log_sums = repair(lengths, flag, near, far, context, raw_context, log_sums)
-    output, grad_x2, grad_context, mid, point_two, bn_grads, two = middle(
+    output, grad_x2, grad_context, mid, point_two, bn_grads, partial = middle(
         lengths, context, x1, cotangent[0], ln3_gain, ln4_gain, ln5_gain, w_out, w_point1, depthwise,
         bn_gain, bn_bias, w_point2, ffn2_in, ffn2_out, dp,
     )
     input_grad, full = back(
-        lengths, near, far, raw_context, log_sums, grad_context, trig, ln1_gain, ln2_gain, two, mid, point_two,
+        lengths, near, far, raw_context, log_sums, grad_context, trig, ln1_gain, ln2_gain, partial, mid, point_two,
         tokens[0], x1, n2, grad_x2, act, slope, ffn1_in, ffn1_out, w_qkv,
     )
     results = unpack(full, bn_grads, output, input_grad, depthwise.shape[0])

time: 177 us -> 171 us (0.966)
  Pallas kernels: 176 us -> 170 us
    pallas_call x1, Pallas kernels: 86.7 us -> 79.8 us  [back(): pl.pallas_call(functools.partial(back_kernel, sp, lengths.shape[1], chunk...]
where the time goes in v7:
time: 171 us
  Pallas kernels  170 us (99%)
    pallas_call x1, Pallas kernels, back(): pl.pallas_call(functools.partial(back_kernel, sp, lengths.shape[1], chunk...  79.8 us
    pallas_call x1, Pallas kernels, middle(): pl.pallas_call(functools.partial(middle_kernel, sp, dp, lengths.shape[1],...  49.6 us
    pallas_call x1, Pallas kernels, front(): pl.pallas_call(functools.partial(front_kernel, lengths.shape[1], chunk, m...  33.5 us
    pallas_call x1, Pallas kernels, unpack(): pl.pallas_call(functools.partial(unpack_kernel, taps), out_shape=[jax.Sha...  5.76 us

profile of v7, /device:TPU:0, one launch (start us, length us, event | category | flops | bytes accessed | tf_op | source)
XLA Modules:
  0.0 170.6 jit_solution(2647577684620826925)
XLA Ops:
  0.7 33.5 %front.1 = (f32[1024,256]{1,0:T(8,128)}, bf16[1024,256]{1,0:T(8,128)(2,1)}, f32[64,1024]{1,0:T(8,128)}, bf16[1024,1024]{1,0:T(8,128)(2,1)}, bf16[1024,1024]{1,0:...) custom-call(s32[1,4]{1,0:T(1,128)} %len_ref.7, ...), custom_call_target="tpu_custom_call" | custom-call | tf_op jit(solution)/shard_map/front/pallas_call | solution.py:343
  34.2 1.0 repair.1
  35.3 49.6 %middle.1 = (bf16[1024,256]{1,0:T(8,128)(2,1)}, f32[1024,256]{1,0:T(8,128)}, bf16[2,64,2048]{2,1,0:T(8,128)(2,1)}, f32[1024,256]{1,0:T(8,128)}, f32[256,256]{1,0...) custom-call(s32[1,4]{1,0:T(1,128)} %len_ref.7, bf16[2,64,2048]{2,1,0:T(8,128)(2,1)} %get-tuple-element.66.parts, ...), custom_call_target="tpu_custom_call" | custom-call | tf_op jit(solution)/shard_map/middle/pallas_call | solution.py:1096
  84.9 79.8 %back.1 = (bf16[1024,256]{1,0:T(8,128)(2,1)}, bf16[6160,256]{1,0:T(8,128)(2,1)}) custom-call(s32[1,4]{1,0:T(1,128)} %len_ref.7, f32[2,2048]{1,0:T(2,128)} %get-tuple-element.65.lse_ref, bf16[256]{0:T(256)(128)(2,1)} %gain1.3, bf16[256]{0:T(256)(128)(2,1)} %gain2.3, f32[128,256]{1,0:T(8,128)} %get-tuple-element.68.partial, ...), custom_call_target="tpu_custom_call" | custom-call | tf_op jit(solution)/shard_map/back/pallas_call | solution.py:1467
  164.7 5.8 %unpack.1 = (bf16[1024,256]{1,0:T(8,128)(2,1)}, bf16[1024,256]{1,0:T(8,128)(2,1)}, f32[256]{0:T(256)}, f32[256,1024]{1,0:T(8,128)}, f32[1024,256]{1,0:T(8,128)},...) custom-call(bf16[6160,256]{1,0:T(8,128)(2,1)} %get-tuple-element.78., ...), custom_call_target="tpu_custom_call" | custom-call | tf_op jit(solution)/shard_map/unpack/pallas_call | solution.py:1592

commit v8 on v7

--- a/solution.py
+++ b/solution.py
@@ -20,8 +20,8 @@
 SMEM = pl.BlockSpec(memory_space=pltpu.SMEM)
 DMA = pltpu.SemaphoreType.DMA
 VMEM_LIMIT = 56 * 2**20
-PARTIAL_TIMES = (0, 3, 5, 10, 14)
-FRESH_TIMES = (0, 1, 4, 7, 11, 13)
+PARTIAL_TIMES = (0, 4, 8, 13)
+FRESH_TIMES = (0, 2, 5, 9, 13)
 
 
 def dg(left, right, left_dim, right_dim):
@@ -124,7 +124,7 @@
 
 
 def sigmoid(x):
-    return 1.0 / (1.0 + jnp.exp(-x))
+    return 0.5 * jnp.tanh(0.5 * x) + 0.5
 
 
 def sine_cosine(position, freq_hi, freq_lo):
@@ -1094,7 +1094,7 @@
     rims = pltpu.VMEM((2, 3 * reach, width), F32)
     moves = [DMA((count,)), DMA((count,)), DMA((count,))]
     return pl.pallas_call(
-        functools.partial(middle_kernel, sp, dp, lengths.shape[1], taps, chunk, 32),
+        functools.partial(middle_kernel, sp, dp, lengths.shape[1], taps, chunk, 64),
         out_shape=[
             jax.ShapeDtypeStruct((frames, width), BF16),
             jax.ShapeDtypeStruct((frames, width), F32),
@@ -1239,7 +1239,6 @@
                 va[h, 0:dim, where] = value
                 va[h, dim : dim + 16, where] = first_rows(3, frames)
                 va[h, dim + 16 :, where] = wide_pad
-    await_greetings(greeted)
     wait_all(loads[4:5])
 
     def attend_block(h, at):
@@ -1307,6 +1306,10 @@
         b, h = t // 2, lax.rem(t, 2)
         cols = rows_at(lax.rem(b, per), block)
         keep(far_out, b // per, h, cols, attend_block(h, reach + b * block))
+
+        @pl.when(t == 0)
+        def _():
+            await_greetings(greeted)
 
         @pl.when(h == 1)
         def _():
@@ -1527,57 +1530,70 @@
 
 
 def unpack_kernel(
-    taps, full, bn_grads, output, input_grad,
+    taps, full_hbm, bn_grads, output_hbm, input_hbm,
     output_to, input_to, gain1_to, in_one_to, out_one_to, gain2_to, qkv_to, out_weight_to, gain3_to, point_one_to,
     depthwise_to, bn_gain_to, bn_bias_to, point_two_to, gain4_to, in_two_to, out_two_to, gain5_to,
-    in_one, out_one, qkv, point_one, point_two, out_weight, in_two, out_two, depthwise, sems,
+    full, output, input_grad, in_one, out_one, qkv, point_one, point_two, out_weight, in_two, out_two, depthwise,
+    load_sems, sems,
 ):
     width = full.shape[1]
     unit = 4 * width
     copies = []
+    pieces = [pl.ds(i * unit, unit) for i in range(6)] + [pl.ds(6 * unit, 16)]
+    loads = start_copies(
+        [(full_hbm.at[piece, :], full.at[piece, :]) for piece in pieces]
+        + [(output_hbm, output), (input_hbm, input_grad)],
+        load_sems,
+    )
 
     def send(source, target):
         copies.append(pltpu.make_async_copy(source, target, sems.at[len(copies)]))
         copies[-1].start()
 
-    def block(ref, base):
-        return ref[base : base + width, :].astype(F32)
-
-    send(output, output_to)
-    send(input_grad, input_to)
+    def block(base):
+        return full[base : base + width, :].astype(F32)
+
+    loads[0].wait()
     for j in range(0, unit, width):
-        out_two[j : j + width, :] = block(full, j)
+        out_two[j : j + width, :] = block(j)
     send(out_two, out_two_to)
+    loads[1].wait()
     for j in range(0, unit, width):
-        in_two[:, j : j + width] = block(full, unit + j)
+        in_two[:, j : j + width] = block(unit + j)
     send(in_two, in_two_to)
-    for j in range(0, unit, width):
-        out_one[j : j + width, :] = block(full, 4 * unit + j)
-    send(out_one, out_one_to)
-    for j in range(0, unit, width):
-        in_one[:, j : j + width] = block(full, 5 * unit + j)
-    send(in_one, in_one_to)
+    loads[2].wait()
     for j in range(0, 2 * width, width):
-        point_one[:, j : j + width] = block(full, 2 * unit + j)
+        point_one[:, j : j + width] = block(2 * unit + j)
     send(point_one, point_one_to)
-    out_weight[...] = block(full, 2 * unit + 2 * width)
+    out_weight[...] = block(2 * unit + 2 * width)
     send(out_weight, out_weight_to)
-    point_two[...] = block(full, 3 * unit + 3 * width)
-    send(point_two, point_two_to)
-    for j in range(0, 3 * width, width):
-        qkv[:, j : j + width] = block(full, 3 * unit + j).T
-    send(qkv, qkv_to)
     small = full[2 * unit + 3 * width : 2 * unit + 3 * width + 64, :].astype(F32)
     depthwise[...] = small[8 : 8 + taps]
     send(depthwise, depthwise_to)
+    loads[3].wait()
+    point_two[...] = block(3 * unit + 3 * width)
+    send(point_two, point_two_to)
+    for j in range(0, 3 * width, width):
+        qkv[:, j : j + width] = block(3 * unit + j).T
+    send(qkv, qkv_to)
+    loads[4].wait()
+    for j in range(0, unit, width):
+        out_one[j : j + width, :] = block(4 * unit + j)
+    send(out_one, out_one_to)
+    loads[5].wait()
+    for j in range(0, unit, width):
+        in_one[:, j : j + width] = block(5 * unit + j)
+    send(in_one, in_one_to)
+    wait_all(loads[6:])
+    send(output, output_to)
+    send(input_grad, input_to)
     rest = full[6 * unit : 6 * unit + 16, :].astype(F32)
     for ref, row in (
         (gain1_to, rest[0]), (gain2_to, rest[1]), (gain3_to, small[2]), (gain4_to, small[3]), (gain5_to, small[4]),
         (bn_gain_to, bn_grads[0, :]), (bn_bias_to, bn_grads[1, :]),
     ):
         ref[...] = row
-    for copy in copies:
-        copy.wait()
+    wait_all(copies)
 
 
 def unpack(full, bn_grads, output, input_grad, taps):
@@ -1592,13 +1608,18 @@
     return pl.pallas_call(
         functools.partial(unpack_kernel, taps),
         out_shape=[jax.ShapeDtypeStruct(shape, F32 if i > 1 else BF16) for i, shape in enumerate(shapes)],
-        in_specs=[VMEM] * 4,
+        in_specs=[anywhere, VMEM, anywhere, anywhere],
         out_specs=[VMEM if shape == row else anywhere for shape in shapes],
         scratch_shapes=[
+            pltpu.VMEM(full.shape, BF16),
+            pltpu.VMEM(output.shape, BF16),
+            pltpu.VMEM(input_grad.shape, BF16),
+        ]
+        + [
             pltpu.VMEM(shape, F32)
             for shape in (flat, tall, thrice, twice, square, square, flat, tall, (taps, width))
         ]
-        + [DMA((11,))],
+        + [DMA((9,)), DMA((11,))],
         compiler_params=pltpu.CompilerParams(vmem_limit_bytes=VMEM_LIMIT),
         name="unpack",
     )(full, bn_grads, output, input_grad)

time: 171 us -> 167 us (0.977)
  Pallas kernels: 170 us -> 165 us
    pallas_call x1, Pallas kernels: 79.8 us -> 76.5 us  [back(): pl.pallas_call(functools.partial(back_kernel, sp, lengths.shape[1], chunk...]
where the time goes in v8:
time: 167 us; the launch traced here: 166 us
  Pallas kernels  165 us (99%)
    pallas_call x1, Pallas kernels, back(): pl.pallas_call(functools.partial(back_kernel, sp, lengths.shape[1], chunk...  76.5 us
    pallas_call x1, Pallas kernels, middle(): pl.pallas_call(functools.partial(middle_kernel, sp, dp, lengths.shape[1],...  48.9 us
    pallas_call x1, Pallas kernels, front(): pl.pallas_call(functools.partial(front_kernel, lengths.shape[1], chunk, m...  33.5 us
    pallas_call x1, Pallas kernels, unpack(): pl.pallas_call(functools.partial(unpack_kernel, taps), out_shape=[jax.Sha...  5.49 us

profile of v8, /device:TPU:0, one launch (start us, length us, event | category | flops | bytes accessed | tf_op | source)
XLA Modules:
  0.0 166.3 jit_solution(8244723090760140710)
XLA Ops:
  0.7 33.5 %front.1 = (f32[1024,256]{1,0:T(8,128)}, bf16[1024,256]{1,0:T(8,128)(2,1)}, f32[64,1024]{1,0:T(8,128)}, bf16[1024,1024]{1,0:T(8,128)(2,1)}, bf16[1024,1024]{1,0:...) custom-call(s32[1,4]{1,0:T(1,128)} %len_ref.7, ...), custom_call_target="tpu_custom_call" | custom-call | tf_op jit(solution)/shard_map/front/pallas_call | solution.py:343
  34.2 1.0 repair.1
  35.2 48.9 %middle.1 = (bf16[1024,256]{1,0:T(8,128)(2,1)}, f32[1024,256]{1,0:T(8,128)}, bf16[2,64,2048]{2,1,0:T(8,128)(2,1)}, f32[1024,256]{1,0:T(8,128)}, f32[256,256]{1,0...) custom-call(s32[1,4]{1,0:T(1,128)} %len_ref.7, bf16[2,64,2048]{2,1,0:T(8,128)(2,1)} %get-tuple-element.66.parts, ...), custom_call_target="tpu_custom_call" | custom-call | tf_op jit(solution)/shard_map/middle/pallas_call | solution.py:1096
  84.2 76.5 %back.1 = (bf16[1024,256]{1,0:T(8,128)(2,1)}, bf16[6160,256]{1,0:T(8,128)(2,1)}) custom-call(s32[1,4]{1,0:T(1,128)} %len_ref.7, f32[2,2048]{1,0:T(2,128)} %get-tuple-element.65.lse_ref, bf16[256]{0:T(256)(128)(2,1)} %gain1.3, bf16[256]{0:T(256)(128)(2,1)} %gain2.3, f32[128,256]{1,0:T(8,128)} %get-tuple-element.68.partial, ...), custom_call_target="tpu_custom_call" | custom-call | tf_op jit(solution)/shard_map/back/pallas_call | solution.py:1470
  160.6 5.5 %unpack.1 = (bf16[1024,256]{1,0:T(8,128)(2,1)}, bf16[1024,256]{1,0:T(8,128)(2,1)}, f32[256]{0:T(256)}, f32[256,1024]{1,0:T(8,128)}, f32[1024,256]{1,0:T(8,128)},...) custom-call(bf16[6160,256]{1,0:T(8,128)(2,1)} %get-tuple-element.78., ...), custom_call_target="tpu_custom_call" | custom-call | tf_op jit(solution)/shard_map/unpack/pallas_call | solution.py:1608

commit v9 on v8

--- a/solution.py
+++ b/solution.py
@@ -11,7 +11,6 @@
 HEADS = 4
 EPS = 1e-05
 NEG = -1e30
-LN2 = float(np.log(2.0))
 F32 = jnp.float32
 BF16 = jnp.bfloat16
 I32 = jnp.int32
@@ -198,7 +197,7 @@
     greet(peers)
     turned[...] = w_qkv[...].T
     ends = ends_of(len_ref, items)
-    scale = float(np.log2(np.e)) * dim**-0.5
+    scale = dim**-0.5
 
     def copies(c):
         cols = rows_at(c, chunk)
@@ -287,7 +286,7 @@
 
     def near_step(i, carry):
         h, cols = i // (reach // block), rows_at(lax.rem(i, reach // block), block)
-        powers = jnp.exp2(dg(ka[h, 0:reach, :], qa[h, :, cols], 1, 0)).astype(BF16)
+        powers = jnp.exp(dg(ka[h, 0:reach, :], qa[h, :, cols], 1, 0)).astype(BF16)
         acc[h, :, cols] = dg(va[h, :, 0:reach], powers, 1, 0)
         return carry
 
@@ -310,7 +309,7 @@
 
         def inner(i, carry):
             h, cols = i // (reach // wide), rows_at(lax.rem(i, reach // wide), wide)
-            powers = jnp.exp2(dg(ka[h, rows, :], qa[h, :, cols], 1, 0)).astype(BF16)
+            powers = jnp.exp(dg(ka[h, rows, :], qa[h, :, cols], 1, 0)).astype(BF16)
             acc[h, :, cols] += dg(va[h, :, rows], powers, 1, 0)
             return carry
 
@@ -325,7 +324,7 @@
         ctx[h] = value.astype(BF16)
         o_ref[h] = value
         leaving += start_copies([(ctx.at[h], ctx_hbm.at[h]), (o_ref.at[h], o_hbm.at[h])], last_sems.at[pl.ds(3 + 2 * h, 2)])
-        lse[h : h + 1, :] = lse[h : h + 1, :] + jnp.log2(total)
+        lse[h : h + 1, :] = lse[h : h + 1, :] + jnp.log(total)
         bad = jnp.maximum(bad, jnp.where(total < 2.0**60, 0.0, 1.0))
     flag[...] = jnp.broadcast_to(jnp.max(bad, axis=1, keepdims=True), flag.shape)
     for c in range(count):
@@ -428,14 +427,14 @@
 
             def add(j, total):
                 rows = rows_at(j, block)
-                powers = jnp.exp2(dg(ka[h, rows, :], query, 1, 0) - top).astype(BF16)
+                powers = jnp.exp(dg(ka[h, rows, :], query, 1, 0) - top).astype(BF16)
                 return total + dg(va[h, :, rows], powers, 1, 0)
 
             total = lax.fori_loop(0, 2 * reach // block, add, jnp.zeros((dim + 16, block), F32))
             value = total[0:dim, :] / total[dim : dim + 1, :]
             ctx[h, :, cols] = value.astype(BF16)
             o_ref[h, :, cols] = value
-            change = top + jnp.log2(total[dim : dim + 1, :])
+            change = top + jnp.log(total[dim : dim + 1, :])
             row = lax.broadcasted_iota(I32, (2, block), 0)
             lse[:, cols] = lse[:, cols] + jnp.where(row == h, change, 0.0)
             return carry
@@ -778,7 +777,7 @@
     lax.fori_loop(0, count, open_step, 0)
 
     def rim_copies(call, side, source, target):
-        peer = (me_dp, me - 1 if side == 0 else me + 1)
+        peer = (me_dp, lax.rem(me + (sp - 1 if side == 0 else 1), sp))
         return pltpu.make_async_remote_copy(
             src_ref=source, dst_ref=target, send_sem=rim_send.at[call, side], recv_sem=rim_recv.at[call, side],
             device_id=peer, device_id_type=MESH,
@@ -1253,10 +1252,10 @@
             scores, grad_probs = ready
             if u + 1 < block // sub:
                 ready = score(u + 1)
-            probs = jnp.exp2(scores)
+            probs = jnp.exp(scores)
             grad = (probs * grad_probs).astype(BF16)
             dv.append(dg(do_ref[h], probs.astype(BF16), 1, 0).astype(BF16))
-            dk.append((dg(qt[h], grad, 1, 0) * LN2).astype(BF16))
+            dk.append(dg(qt[h], grad, 1, 0).astype(BF16))
             turned[u * sub : (u + 1) * sub, :] = grad.T
         dq[h] += dg(ka[h, 0:dim, pl.ds(pl.multiple_of(at, block), block)], turned[...], 1, 0)
         return jnp.concatenate(dk, axis=1), jnp.concatenate(dv, axis=1)

time: 167 us -> 167 us (level)
  no operation moved by 1% of the time
where the time goes in v9:
time: 167 us; the launch traced here: 166 us
  Pallas kernels  166 us (99%)
    pallas_call x1, Pallas kernels, back(): pl.pallas_call(functools.partial(back_kernel, sp, lengths.shape[1], chunk...  76.5 us
    pallas_call x1, Pallas kernels, middle(): pl.pallas_call(functools.partial(middle_kernel, sp, dp, lengths.shape[1],...  48.9 us
    pallas_call x1, Pallas kernels, front(): pl.pallas_call(functools.partial(front_kernel, lengths.shape[1], chunk, m...  33.5 us
    pallas_call x1, Pallas kernels, unpack(): pl.pallas_call(functools.partial(unpack_kernel, taps), out_shape=[jax.Sha...  5.49 us

profile of v9, /device:TPU:0, one launch (start us, length us, event | category | flops | bytes accessed | tf_op | source)
XLA Modules:
  0.0 166.4 jit_solution(13413258933197124866)
XLA Ops:
  0.7 33.5 %front.1 = (f32[1024,256]{1,0:T(8,128)}, bf16[1024,256]{1,0:T(8,128)(2,1)}, f32[64,1024]{1,0:T(8,128)}, bf16[1024,1024]{1,0:T(8,128)(2,1)}, bf16[1024,1024]{1,0:...) custom-call(s32[1,4]{1,0:T(1,128)} %len_ref.7, ...), custom_call_target="tpu_custom_call" | custom-call | tf_op jit(solution)/shard_map/front/pallas_call | solution.py:342
  34.2 1.0 repair.1
  35.2 48.9 %middle.1 = (bf16[1024,256]{1,0:T(8,128)(2,1)}, f32[1024,256]{1,0:T(8,128)}, bf16[2,64,2048]{2,1,0:T(8,128)(2,1)}, f32[1024,256]{1,0:T(8,128)}, f32[256,256]{1,0...) custom-call(s32[1,4]{1,0:T(1,128)} %len_ref.7, bf16[2,64,2048]{2,1,0:T(8,128)(2,1)} %get-tuple-element.66.parts, ...), custom_call_target="tpu_custom_call" | custom-call | tf_op jit(solution)/shard_map/middle/pallas_call | solution.py:1095
  84.2 76.5 %back.1 = (bf16[1024,256]{1,0:T(8,128)(2,1)}, bf16[6160,256]{1,0:T(8,128)(2,1)}) custom-call(s32[1,4]{1,0:T(1,128)} %len_ref.7, f32[2,2048]{1,0:T(2,128)} %get-tuple-element.65.lse_ref, bf16[256]{0:T(256)(128)(2,1)} %gain1.3, bf16[256]{0:T(256)(128)(2,1)} %gain2.3, f32[128,256]{1,0:T(8,128)} %get-tuple-element.68.partial, ...), custom_call_target="tpu_custom_call" | custom-call | tf_op jit(solution)/shard_map/back/pallas_call | solution.py:1469
  160.7 5.5 %unpack.1 = (bf16[1024,256]{1,0:T(8,128)(2,1)}, bf16[1024,256]{1,0:T(8,128)(2,1)}, f32[256]{0:T(256)}, f32[256,1024]{1,0:T(8,128)}, f32[1024,256]{1,0:T(8,128)},...) custom-call(bf16[6160,256]{1,0:T(8,128)(2,1)} %get-tuple-element.78., ...), custom_call_target="tpu_custom_call" | custom-call | tf_op jit(solution)/shard_map/unpack/pallas_call | solution.py:1607
